TPU v7x, 128 devices: a whole 4x4x4 slice. The times are simulated.
128 devices in a mesh: seq: 8 (over x, core), head: 16 (over z, y).
Axes of the slice: x: 4, y: 4, z: 4, core: 2. Of those that a mesh axis runs over, the one named last changes fastest.
Arguments:
- hidden: bfloat16 [4096, 3584], P('seq', 'head'), may hold values from -6 to 6
- embedding: bfloat16 [4096, 3584], P('seq', 'head'), may hold values from -6 to 6
- input_gain: float32 [3584], replicated, may hold values from 0.1 to 1.9
- w_input: bfloat16 [3584, 8192], P(None, 'head'), may hold values from -0.09375 to 0.09375
- w_groups: bfloat16 [3584, 256], replicated, may hold values from -0.09375 to 0.09375
- w_step: bfloat16 [3584, 64], P(None, 'head'), may hold values from -0.09375 to 0.09375
- step_bias: float32 [64], P('head'), may hold values from -1 to 1
- decay_rate: float32 [64], P('head'), may hold values from 0.000390625 to 0.0390625
- skip_gain: float32 [64], P('head'), may hold values from -16 to 16
- conv_weight: float32 [4, 4096], P(None, 'head'), may hold values from -3 to 3
- mix_gain: float32 [4096], P('head'), may hold values from 0.1 to 1.9
- w_output: bfloat16 [4096, 3584], P('head'), may hold values from -0.09375 to 0.09375
- state_store: float32 [16, 64, 4096], P('seq', 'head'), may hold values from -6 to 6
- conv_store: bfloat16 [16, 3, 4096], P('seq', None, 'head'), may hold values from -6 to 6
- state_slot: int32 [8], replicated, may hold values from 0 to 15, as said below
- prefix_len: int32 [8], replicated, may hold values from 1 to 8192, as said below
- block_table: int32 [8, 64], replicated, may hold values from 0 to 159, as said below
- shared_gain: float32 [7168], replicated, may hold values from 0.1 to 1.9
- w_attend: bfloat16 [7168, 10752], P(None, 'head'), may hold values from -0.06496264 to 0.06496264
- cache_pool: bfloat16 [160, 2, 128, 3584], P('seq', None, None, 'head'), may hold values from -8 to 8
- w_merge: bfloat16 [3584, 3584], P('head'), may hold values from -0.09375 to 0.09375
Outputs:
- layer_output: float32 [4096, 3584], P('seq', 'head')
- final_state: float32 [8, 64, 4096], P('seq', 'head')
Inputs may be any that keep to these rules, and one draw needn't show every extreme that they name: `prefix_len`: one request has a prefix of exactly 8192 tokens; every other has at most 1664. block_table[r, j] is the first index of cache_pool holding prefix positions j * 128 to (j + 1) * 128 - 1 of request r; it is read only where j * 128 < prefix_len[r], and such entries are distinct over all requests. `state_slot`: different requests have different rows.
All inputs are finite; a program needn't handle non-finite values.
Results may differ from a plain program's by a relative error of at most 0.014.
Values may be sent and summed in bfloat16 or wider, within the bound.
A program may use at most 192 MiB of HBM per device.

v0:
```python
import jax
import jax.numpy as jnp
from jax import lax
from jax.sharding import PartitionSpec as P

MH = 64
P_SIZE = 64
NS = 64
G = 2
CONV = 4
HD = 224
STRETCH = 512
BLOCK = 128
MAXB = 64


epsilon = 1e-05
masked = -1e30
highest = lax.Precision.HIGHEST


def norm_rows(matrix, norm_gain):
    matrix = matrix.astype(jnp.float32)
    return (
        matrix * lax.rsqrt(jnp.mean(matrix * matrix, axis=-1, keepdims=True) + epsilon) * norm_gain
    )


def state_block(activated, step_sizes, cumulative, b_proj, c_proj, init_state, skip_gain):
    length = activated.shape[0]
    positions = jnp.arange(length)
    causal = (positions[:, None] >= positions[None, :])[None]
    cums_heads = cumulative.T
    gaps = cums_heads[:, :, None] - cums_heads[:, None, :]
    decays = jnp.where(causal, jnp.exp(jnp.where(causal, gaps, 0.0)), 0.0)
    product = jnp.einsum("tn,sn->ts", c_proj, b_proj, precision=highest)
    weighted = decays * product[None] * step_sizes.T[:, None, :]
    within = jnp.einsum("hts,shp->thp", weighted, activated, precision=highest)
    carried = (
        jnp.einsum("tn,hpn->thp", c_proj, init_state, precision=highest)
        * jnp.exp(cumulative)[:, :, None]
    )
    output = within + carried + skip_gain[None, :, None] * activated
    to_end = jnp.exp(cumulative[-1][None, :] - cumulative) * step_sizes
    final_state = jnp.exp(cumulative[-1])[:, None, None] * init_state + jnp.einsum(
        "shp,sn->hpn", activated * to_end[:, :, None], b_proj, precision=highest
    )
    return (output, final_state)


def body(
    hidden,
    embedding,
    input_gain,
    w_input,
    w_groups,
    w_step,
    step_bias,
    decay_rate,
    skip_gain,
    conv_weight,
    mix_gain,
    w_output,
    state_store,
    conv_store,
    state_slot,
    prefix_len,
    block_table,
    shared_gain,
    w_attend,
    cache_pool,
    w_merge,
):
    heads_local = w_step.shape[1]
    attend_local = w_merge.shape[0] // HD
    my_head = lax.axis_index("head")
    my_seq = lax.axis_index("seq")
    group_heads = MH // G
    group_id = my_head * heads_local // group_heads
    scale_factor = HD ** (-0.5)
    whole_rows = lax.all_gather(hidden, "head", axis=1, tiled=True)
    normed = norm_rows(whole_rows, input_gain).astype(jnp.bfloat16)
    paired = jnp.dot(normed, w_input, preferred_element_type=jnp.float32).reshape(
        STRETCH, heads_local, 2, P_SIZE
    )
    gate_part = paired[:, :, 0]
    signal = paired[:, :, 1].reshape(STRETCH, heads_local * P_SIZE)
    b_columns = lax.dynamic_slice_in_dim(w_groups, group_id * NS, NS, 1)
    c_columns = lax.dynamic_slice_in_dim(w_groups, (G + group_id) * NS, NS, 1)
    grouped = jnp.dot(
        normed, jnp.concatenate([b_columns, c_columns], axis=1), preferred_element_type=jnp.float32
    )
    raw_steps = jnp.dot(normed, w_step, preferred_element_type=jnp.float32)
    stores, conv_tails = (
        lax.all_gather(state_store, "seq", axis=0, tiled=True),
        lax.all_gather(conv_store.astype(jnp.float32), "seq", axis=0, tiled=True).astype(
            conv_store.dtype
        ),
    )
    slot_row = state_slot[my_seq]
    init_state = lax.dynamic_index_in_dim(stores, slot_row, 0, keepdims=False).reshape(
        heads_local, P_SIZE, NS
    )
    conv_tail = lax.dynamic_index_in_dim(conv_tails, slot_row, 0, keepdims=False).astype(
        jnp.float32
    )
    padded = jnp.concatenate([conv_tail, signal], axis=0)
    convolved = sum(
        (conv_weight[offset] * padded[offset : offset + STRETCH] for offset in range(CONV))
    )
    activated = jax.nn.silu(convolved).reshape(STRETCH, heads_local, P_SIZE)
    step_sizes = jax.nn.softplus(raw_steps + step_bias)
    cumulative = jnp.cumsum(-decay_rate * step_sizes, axis=0)
    scanned, final_state = state_block(
        activated, step_sizes, cumulative, grouped[:, :NS], grouped[:, NS:], init_state, skip_gain
    )
    gated = scanned * jax.nn.silu(gate_part)
    local_squares = jnp.sum(gated * gated, axis=(1, 2))
    pick_group = (jnp.arange(G) == group_id).astype(jnp.float32)
    totals = lax.psum(local_squares[:, None] * pick_group[None, :], "head")
    mean_squares = jnp.sum(totals * pick_group[None, :], axis=1) / (group_heads * P_SIZE)
    mixed_rows = (
        gated.reshape(STRETCH, heads_local * P_SIZE)
        * lax.rsqrt(mean_squares + epsilon)[:, None]
        * mix_gain
    ).astype(jnp.bfloat16)
    partial_value = jnp.dot(mixed_rows, w_output, preferred_element_type=jnp.float32)
    shard_sum = lax.psum_scatter(partial_value, "head", scatter_dimension=1, tiled=True)
    hidden_next = hidden.astype(jnp.float32) + shard_sum
    first_half, second_half = (
        lax.all_gather(hidden_next.astype(jnp.bfloat16), "head", axis=1, tiled=True),
        lax.all_gather(embedding, "head", axis=1, tiled=True),
    )
    joined = jnp.concatenate([first_half, second_half], axis=1)
    shared_normed = norm_rows(joined, shared_gain).astype(jnp.bfloat16)
    projected = jnp.dot(shared_normed, w_attend, preferred_element_type=jnp.float32).astype(
        jnp.bfloat16
    )
    projected = projected.reshape(STRETCH, attend_local, 3, HD)
    queries = projected[:, :, 0]
    keys_new = projected[:, :, 1]
    values_new = projected[:, :, 2]
    positions = jnp.arange(STRETCH)
    causal = (positions[:, None] >= positions[None, :])[None]
    self_scores = (
        jnp.einsum("qad,kad->aqk", queries, keys_new, preferred_element_type=jnp.float32)
        * scale_factor
    )
    self_scores = jnp.where(causal, self_scores, masked)
    self_max = jnp.max(self_scores, axis=2)
    self_weights = jnp.where(causal, jnp.exp(self_scores - self_max[:, :, None]), 0.0)
    self_total = jnp.sum(self_weights, axis=2)
    self_acc = jnp.einsum(
        "aqk,kad->aqd",
        self_weights.astype(jnp.bfloat16),
        values_new,
        preferred_element_type=jnp.float32,
    )
    block_index = jnp.arange(MAXB)
    table_row = block_table[my_seq]
    my_length = prefix_len[my_seq]
    live_row = block_index * BLOCK < my_length
    blocks_in = lax.all_gather(cache_pool, "seq", axis=0, tiled=True)
    block_count = blocks_in.shape[0]
    block_ids = jnp.arange(block_count)
    matches = (table_row[None, :] == block_ids[:, None]) & live_row[None, :]
    is_owned = jnp.any(matches, axis=1)
    block_pos = jnp.sum(jnp.where(matches, block_index[None, :], 0), axis=1)
    key_pos = block_pos[:, None] * BLOCK + jnp.arange(BLOCK)[None, :]
    usable = (is_owned[:, None] & (key_pos < my_length)).reshape(block_count * BLOCK)[None, None, :]
    keys_piece = blocks_in[:, 0].reshape(block_count * BLOCK, attend_local, HD)
    values_piece = blocks_in[:, 1].reshape(block_count * BLOCK, attend_local, HD)
    scores = (
        jnp.einsum("qad,kad->aqk", queries, keys_piece, preferred_element_type=jnp.float32)
        * scale_factor
    )
    scores = jnp.where(usable, scores, masked)
    new_max = jnp.maximum(self_max, jnp.max(scores, axis=2))
    weights = jnp.where(usable, jnp.exp(scores - new_max[:, :, None]), 0.0)
    factor = jnp.exp(self_max - new_max)
    added = jnp.einsum(
        "aqk,kad->aqd",
        weights.astype(jnp.bfloat16),
        values_piece,
        preferred_element_type=jnp.float32,
    )
    total_sum = self_total * factor + jnp.sum(weights, axis=2)
    total_acc = self_acc * factor[:, :, None] + added
    attended = (total_acc / total_sum[:, :, None]).astype(jnp.bfloat16)
    attended = jnp.transpose(attended, (1, 0, 2)).reshape(STRETCH, attend_local * HD)
    attn_partial = jnp.dot(attended, w_merge, preferred_element_type=jnp.float32)
    attn_shard = lax.psum_scatter(attn_partial, "head", scatter_dimension=1, tiled=True)
    layer_output = hidden_next + attn_shard
    return (layer_output, final_state.reshape(1, heads_local, P_SIZE * NS))


def solution(mesh):
    return jax.shard_map(
        body,
        mesh=mesh,
        in_specs=(
            P("seq", "head"),
            P("seq", "head"),
            P(),
            P(None, "head"),
            P(),
            P(None, "head"),
            P("head"),
            P("head"),
            P("head"),
            P(None, "head"),
            P("head"),
            P("head", None),
            P("seq", "head", None),
            P("seq", None, "head"),
            P(),
            P(),
            P(),
            P(),
            P(None, "head"),
            P("seq", None, None, "head"),
            P("head", None),
        ),
        out_specs=(P("seq", "head"), P("seq", "head", None)),
        check_vma=False,
    )
```

profile of v0, /device:TPU:0, one launch (start us, length us, event | category | flops | bytes accessed | tf_op | source)
XLA Modules:
  0.0 635.8 jit_solution(1690037415051048695)
XLA Ops:
  8.7 1.2 dynamic_slice.23
  12.6 13.3 %all_gather.18 = bf16[16,3,256]{2,1,0:T(4,128)(2,1)S(1)} all-gather(bf16[2,3,256]{2,1,0:T(4,128)(2,1)S(1)} %copy.69), channel_id=1, replica_groups=mesh['seq'=8,'head'=16] {'seq'}, dimensions={0}, use_global_device_ids=true | all-gather | bytes 27648 | tf_op jit(solution)/shard_map/all_gather | solution.py:96
  28.7 3.0 constant_dynamic-slice_fusion.3
  31.6 3.9 all-gather.8.cloned.1.call-done
  36.5 51.0 %all-gather.6.cloned.1.call-done = bf16[512,3584]{0,1:T(8,128)(2,1)} async-done(((bf16[512,224]{0,1:T(8,128)(2,1)}), bf16[512,3584]{0,1:T(8,128)(2,1)}) %all-gather.6.cloned.1.call-update) | async-done | bytes 3670032 | tf_op jit(solution)/shard_map/all_gather | solution.py:81
  87.5 3.0 fusion.14
  90.5 4.2 fusion.59
  94.7 2.0 fusion.85
  96.8 2.5 fusion.111
  100.4 1.4 reduce-window.6
  103.2 6.4 %fusion.43 = f32[512,4,64]{0,2,1:T(8,128)S(1)} fusion(f32[512,4,64]{0,2,1:T(8,128)S(1)} %bitcast.125, f32[4,512]{1,0:T(4,128)S(1)} %get-tuple-element.13, f32[512,512]{1,0:T(8,128)} %fusion.85, f32[4,512]{1,0:T(4,128)S(1)} %bitcast.135, pred[512,512]{1,0:T(8,128)(4,1)} %copy.39), kind=kOutput, calls=%fused_computation.43 | convolution fusion | flops 810549248 | bytes 2375680 | tf_op jit(solution)/shard_map/hts,shp->thp/dot_general | solution.py:38
  110.4 38.1 %psum.7 = f32[512,2]{0,1:T(2,128)S(1)} all-reduce(f32[512,2]{0,1:T(2,128)S(1)} %broadcast_multiply_fusion.1), channel_id=1, replica_groups=mesh['seq'=8,'head'=16] {'head'}, use_global_device_ids=true, to_apply=%region_4.5 | all-reduce | flops 1024 | bytes 8192 | tf_op jit(solution)/shard_map/psum | solution.py:120
  148.7 4.1 fusion.116
  153.6 78.7 %reduce-scatter.3.cloned.1.call-done = f32[512,224]{0,1:T(8,128)} async-done(((f32[512,3584]{0,1:T(8,128)}), f32[512,224]{0,1:T(8,128)}) %reduce-scatter.3.cloned.1.call-update) | async-done | bytes 458768 | tf_op jit(solution)/shard_map/reduce_scatter | solution.py:128
  232.3 1.8 fusion.80
  237.6 45.9 %all-gather.12.cloned.1.call-done = bf16[512,3584]{0,1:T(8,128)(2,1)} async-done(((bf16[512,224]{0,1:T(8,128)(2,1)}), bf16[512,3584]{0,1:T(8,128)(2,1)}) %all-gather.12.cloned.1.call-update) | async-done | bytes 3670032 | tf_op jit(solution)/shard_map/all_gather | solution.py:132
  283.6 51.7 %all-gather.10.cloned.1.call-done = bf16[512,3584]{0,1:T(8,128)(2,1)} async-done(((bf16[512,224]{0,1:T(8,128)(2,1)}), bf16[512,3584]{0,1:T(8,128)(2,1)}) %all-gather.10.cloned.1.call-update) | async-done | bytes 3670032 | tf_op jit(solution)/shard_map/all_gather | solution.py:131
  335.3 4.9 fusion.6
  340.6 9.0 %fusion.35 = bf16[512,672]{0,1:T(8,128)(2,1)S(1)} fusion(bf16[7168,672]{0,1:T(8,128)(2,1)} %param.39, f32[7168]{0:T(1024)S(1)} %copy-done.13, f32[512]{0:T(512)S(1)} %add_rsqrt_fusion, bf16[512,3584]{0,1:T(8,128)(2,1)S(1)} %copy-done.3, bf16[512,3584]{0,1:T(8,128)(2,1)S(1)} %copy-done.4), kind=kOutput, calls=%fused_computation.41 | convolution fusion | flops 4958535680 | bytes 17692672 | tf_op jit(solution)/shard_map/dot_general | solution.py:136
  350.1 77.4 %all-gather.14.cloned.1.call-done = bf16[160,2,128,224]{2,3,1,0:T(8,128)(2,1)} async-done(((bf16[20,2,128,224]{2,3,1,0:T(8,128)(2,1)}), bf16[160,2,128,224]{2,3,1,0:T(8,128)(2,1)}) %all-gather.14.cloned.1.call-update) | async-done | bytes 18350096 | tf_op jit(solution)/shard_map/all_gather | solution.py:163
  427.5 14.7 %fusion.113 = (bf16[160,1,128,224]{2,3,1,0:T(8,128)(2,1)}, bf16[160,1,128,224]{2,3,1,0:T(8,128)(2,1)}) fusion(bf16[160,2,128,224]{2,3,1,0:T(8,128)(2,1)} %all-gather.14.cloned.1.call-done), kind=kLoop, calls=%fused_computation.147 | loop fusion | bytes 36700160 | tf_op jit(solution)/shard_map/slice | solution.py:172
  442.2 10.7 %copy.41 = bf16[160,1,128,224]{2,0,3,1:T(8,128)(2,1)} copy(bf16[160,1,128,224]{2,3,1,0:T(8,128)(2,1)} %get-tuple-element.5) | data formatting | bytes 18350080 | tf_op jit(solution)/shard_map/slice | solution.py:171
  452.9 24.7 %fusion = (f32[512]{0:T(512)S(1)}, f32[512,20480]{1,0:T(8,128)}) fusion(pred[20480]{0:T(1024)(128)(4,1)S(1)} %fusion.90, bf16[28,8,160,128]{3,2,1,0:T(8,128)(2,1)} %bitcast.123, bf16[512,1,3,224]{0,3,2,1:T(8,128)(2,1)S(1)} %bitcast.132), kind=kOutput, calls=%fused_computation.2 | convolution fusion | flops 4729077248 | bytes 51369984 | tf_op jit(solution)/shard_map/qad,kad->aqk/dot_general | solution.py:174
  477.6 19.5 %fusion.1 = f32[512]{0:T(512)S(1)} fusion(f32[512,20480]{1,0:T(8,128)} %get-tuple-element.24, f32[512]{0:T(512)S(1)} %max.33, pred[20480]{0:T(1024)(128)(4,1)S(1)} %fusion.90), kind=kLoop, calls=%fused_computation.3 | loop fusion | flops 52428288 | bytes 41967616 | tf_op jit(solution)/shard_map/reduce_sum | solution.py:187
  497.1 1.1 convolution_multiply_fusion.2
  498.2 10.7 %copy.42 = bf16[160,1,128,224]{2,0,3,1:T(8,128)(2,1)} copy(bf16[160,1,128,224]{2,3,1,0:T(8,128)(2,1)} %get-tuple-element.4) | data formatting | bytes 18350080 | tf_op jit(solution)/shard_map/slice | solution.py:172
  508.9 29.9 %fusion.54 = bf16[512,224]{0,1:T(8,128)(2,1)S(1)} fusion(f32[512,224]{0,1:T(8,128)} %convolution_multiply_fusion.2, bf16[28,8,160,128]{3,2,1,0:T(8,128)(2,1)} %bitcast.124, f32[512,20480]{1,0:T(8,128)} %get-tuple-element.24, f32[512]{0:T(512)S(1)} %max.33, pred[20480]{0:T(1024)(128)(4,1)S(1)} %fusion.90, f32[512]{0:T(512)S(1)} %get-tuple-element.2), kind=kOutput, calls=%fused_computation.52 | convolution fusion | flops 4750393344 | bytes 51830784 | tf_op jit(solution)/shard_map/aqk,kad->aqd/dot_general | solution.py:181
  538.8 4.2 fusion.117
  543.1 1.2 convolution_add_fusion
  544.3 1.6 reshape.259
  545.9 81.0 %reduce-scatter.5.cloned.1.call-done = f32[512,224]{0,1:T(8,128)} async-done(((f32[512,3584]{0,1:T(8,128)}), f32[512,224]{0,1:T(8,128)}) %reduce-scatter.5.cloned.1.call-update) | async-done | bytes 458768 | tf_op jit(solution)/shard_map/reduce_scatter | solution.py:192
  626.9 1.9 fusion.79
  (89 shorter events, 14.6 us)
Async XLA Ops:
  7.2 141.6 %copy-start = (bf16[256,3584]{1,0:T(8,128)(2,1)S(1)}, bf16[256,3584]{1,0:T(8,128)(2,1)}, u32[]{:S(2)}) copy-start(bf16[256,3584]{1,0:T(8,128)(2,1)} %param.32) | copy-start | bytes 5505028
  7.2 83.4 %copy-start.14 = (f32[3584]{0:T(1024)S(1)}, f32[3584]{0:T(1024)}, u32[]{:S(2)}) copy-start(f32[3584]{0:T(1024)} %param.23) | copy-start | bytes 43012
  7.2 28.4 %all-gather.8.cloned.1.call-start = ((), (), s32[]{:S(2)}) async-start(), calls=%async_computation.3 | async-start | bytes 1179648 | tf_op jit(solution)/shard_map/all_gather | solution.py:95
  7.9 79.6 %all-gather.6.cloned.1.call-start = ((), (), s32[]{:S(2)}) async-start(), calls=%async_computation.2 | async-start | bytes 3899392 | tf_op jit(solution)/shard_map/all_gather | solution.py:81
  8.7 223.6 %reduce-scatter.3.cloned.1.call-start = ((), (), s32[]{:S(2)}) async-start(), calls=%async_computation.4 | async-start | bytes 7798784 | tf_op jit(solution)/shard_map/reduce_scatter | solution.py:128
  87.5 9.2 %copy-start.2 = (bf16[512,3584]{0,1:T(8,128)(2,1)S(1)}, bf16[512,3584]{0,1:T(8,128)(2,1)}, u32[]{:S(2)}) copy-start(bf16[512,3584]{0,1:T(8,128)(2,1)} %all-gather.6.cloned.1.call-done) | copy-start | bytes 11010052
  87.5 9.2 %copy-start.11 = (bf16[3584,512]{1,0:T(8,128)(2,1)S(1)}, bf16[3584,512]{1,0:T(8,128)(2,1)}, u32[]{:S(2)}) copy-start(bf16[3584,512]{1,0:T(8,128)(2,1)} %param.24) | copy-start | bytes 11010052
  96.7 2.6 copy-start.12
  96.7 2.6 copy-start.15
  99.2 1.1 copy-start.8
  99.3 10.2 %copy-start.16 = (f32[4]{0:T(128)S(1)}, f32[4]{0:T(128)}, u32[]{:S(2)}) copy-start(f32[4]{0:T(128)} %param.29) | copy-start | bytes 52
  100.3 48.3 %copy-start.10 = (f32[256]{0:T(256)S(1)}, f32[256]{0:T(256)}, u32[]{:S(2)}) copy-start(f32[256]{0:T(256)} %param.31) | copy-start | bytes 3076
  102.1 7.4 %copy-start.9 = (f32[512,512]{0,1:T(8,128)S(1)}, f32[512,512]{0,1:T(8,128)}, u32[]{:S(2)}) copy-start(f32[512,512]{0,1:T(8,128)} %copy-done.8) | copy-start | bytes 3145732
  148.7 83.6 %copy-start.5 = (bf16[512,224]{0,1:T(8,128)(2,1)S(1)}, bf16[512,224]{0,1:T(8,128)(2,1)}, u32[]{:S(2)}) copy-start(bf16[512,224]{0,1:T(8,128)(2,1)} %param.21) | copy-start | bytes 688132
  152.9 81.8 %copy-start.17 = (s32[8]{0:T(128)S(1)}, s32[8]{0:T(128)}, u32[]{:S(2)}) copy-start(s32[8]{0:T(128)} %param.36) | copy-start | bytes 100
  152.9 187.3 %copy-start.13 = (f32[7168]{0:T(1024)S(1)}, f32[7168]{0:T(1024)}, u32[]{:S(2)}) copy-start(f32[7168]{0:T(1024)} %param.38) | copy-start | bytes 86020
  152.9 130.7 %all-gather.12.cloned.1.call-start = ((), (), s32[]{:S(2)}) async-start(), calls=%async_computation.6 | async-start | bytes 3899392 | tf_op jit(solution)/shard_map/all_gather | solution.py:132
  153.5 181.8 %all-gather.10.cloned.1.call-start = ((), (), s32[]{:S(2)}) async-start(), calls=%async_computation.5 | async-start | bytes 3899392 | tf_op jit(solution)/shard_map/all_gather | solution.py:131
  234.1 193.4 %all-gather.14.cloned.1.call-start = ((), (), s32[]{:S(2)}) async-start(), calls=%async_computation.7 | async-start | bytes 20643840 | tf_op jit(solution)/shard_map/all_gather | solution.py:163
  234.7 392.2 %reduce-scatter.5.cloned.1.call-start = ((), (), s32[]{:S(2)}) async-start(), calls=%async_computation.8 | async-start | bytes 7798784 | tf_op jit(solution)/shard_map/reduce_scatter | solution.py:192
  335.3 4.9 copy-start.3
  335.3 5.3 copy-start.4
  508.9 29.9 %copy-start.7 = (bf16[224,3584]{1,0:T(8,128)(2,1)S(1)}, bf16[224,3584]{1,0:T(8,128)(2,1)}, u32[]{:S(2)}) copy-start(bf16[224,3584]{1,0:T(8,128)(2,1)} %param.41) | copy-start | bytes 4816900
  508.9 119.9 %copy-start.1 = (bf16[256,3584]{1,0:T(8,128)(2,1)S(1)}, bf16[256,3584]{1,0:T(8,128)(2,1)}, u32[]{:S(2)}) copy-start(bf16[256,3584]{1,0:T(8,128)(2,1)} %param.32) | copy-start | bytes 5505028
  538.8 88.1 %copy-start.6 = (f32[512,224]{0,1:T(8,128)S(1)}, f32[512,224]{0,1:T(8,128)}, u32[]{:S(2)}) copy-start(f32[512,224]{0,1:T(8,128)} %reduce-scatter.3.cloned.1.call-done) | copy-start | bytes 1376260
Sparse Core Ops, SparseCore 0:
  9.7 25.7 all-gather.7
  37.7 49.7 all-gather.5
  153.0 79.2 reduce-scatter.2
  234.5 49.0 all-gather.11
  286.4 48.8 all-gather.9
  336.9 90.5 all-gather.13
  543.2 83.6 reduce-scatter.4
where the time goes:
time: 643 us; the launch traced here: 636 us
  waiting for transfers between devices  392 us (61%)
  matrix products  91.4 us (14%)
  blocking collectives  51.4 us (8%)
  local copies, waits for them, and re-layouts  47.7 us (7%)
  other arithmetic  36.4 us (6%)
  between operations  16.6 us (3%)
    reduce_scatter x1, waiting for transfers between devices, body(): lax.psum_scatter(attn_partial, 'head', scatter_dimension=1, tiled=True)  81 us
    reduce_scatter x1, waiting for transfers between devices, body(): lax.psum_scatter(partial_value, 'head', scatter_dimension=1, tiled=True)  78.7 us
    all_gather x1, waiting for transfers between devices, body(): blocks_in = lax.all_gather(cache_pool, 'seq', axis=0, tiled=True)  77.4 us
    all_gather x1, waiting for transfers between devices, body(): lax.all_gather(hidden_next.astype(jnp.bfloat16), 'head', axis=1, tiled=True)  51.7 us
    all_gather x1, waiting for transfers between devices, body(): whole_rows = lax.all_gather(hidden, 'head', axis=1, tiled=True)  51 us
    all_gather x1, waiting for transfers between devices, body(): lax.all_gather(embedding, 'head', axis=1, tiled=True)  45.9 us
    psum x1, blocking collectives, body(): totals = lax.psum(local_squares[:, None] * pick_group[None, :], 'head')  38.1 us
    dot_general x1, matrix products, body(): jnp.einsum('aqk,kad->aqd', weights.astype(jnp.bfloat16), values_piece, pr...  29.9 us
  transfers between devices with their start and end apart: 7, of which 7 were waited for; matrix products, arithmetic and copies ran while one was open for 5% of the time, Pallas kernels for 0%

commit v1 on v0

v1 whole, which is shorter than its diff:
```python
import functools

import jax
import jax.numpy as jnp
from jax import lax
from jax.experimental import pallas as pl
from jax.experimental.pallas import tpu as pltpu
from jax.sharding import PartitionSpec as P

D = 3584
MH = 64
P_SIZE = 64
NS = 64
G = 2
CONV = 4
HD = 224
STRETCH = 512
BLOCK = 128
MAXB = 64
SEQ = 8
SIDE = 4
HEADS = SIDE * SIDE
SHARD = D // HEADS
HALF = SHARD // 2
LANES = STRETCH // 2
PACK = 136
STEPB = 8

MESH = pl.DeviceIdType.MESH
epsilon = 1e-05
masked = -1e30
highest = lax.Precision.HIGHEST
f32 = jnp.float32
bf16 = jnp.bfloat16


def place():
    me = lax.axis_index("head")
    return lax.div(me, SIDE), lax.rem(me, SIDE)


def around(c, by):
    return lax.rem(c + by + SIDE, SIDE)


def coords(half):
    z, y = place()
    return (y, z) if half == 0 else (z, y)


def device(half, c1, c2):
    return c2 * SIDE + c1 if half == 0 else c1 * SIDE + c2


def piece(half, c1, c2):
    return pl.ds(pl.multiple_of(device(half, c1, c2) * SHARD + half * HALF, 16), HALF)


OFFSETS = (0, -1, 1, 2)
LEFT = pl.ds(0, LANES)
RIGHT = pl.ds(LANES, LANES)
FULL = pl.ds(0, STRETCH)


def remote(src, dst, send_sem, recv_sem, dev):
    return pltpu.make_async_remote_copy(
        src_ref=src, dst_ref=dst, send_sem=send_sem, recv_sem=recv_sem,
        device_id={"head": dev}, device_id_type=MESH,
    )


class Gather:
    def __init__(self, own, out, send_sems, recv_sems):
        self.own, self.out, self.ss, self.rs = own, out, send_sems, recv_sems
        self.sent = []

    def go(self, half, idx, src, c1, c2, lanes, to1, to2):
        dst = self.out.at[piece(half, c1, c2), lanes]
        copy = remote(src, dst, self.ss.at[half, idx], self.rs.at[half, idx], device(half, to1, to2))
        copy.start()
        self.sent.append(copy)

    def arrive(self, half, idx, c1, c2, lanes):
        where = self.out.at[piece(half, c1, c2), lanes]
        me1, me2 = coords(half)
        remote(where, where, self.ss.at[half, idx], self.rs.at[half, idx], device(half, around(me1, 1), me2)).wait_recv()

    def start(self):
        for axis in (1, 2):
            for half in (0, 1):
                c1, c2 = coords(half)
                src = self.own.at[pl.ds(half * HALF, HALF), FULL]
                if axis == 1:
                    self.go(half, 0, src, c1, c2, FULL, around(c1, 1), c2)
                    self.go(half, 1, src, c1, c2, FULL, around(c1, -1), c2)
                else:
                    self.go(half, 4, src, c1, c2, FULL, c1, around(c2, 1))
                    self.go(half, 5, src, c1, c2, FULL, c1, around(c2, -1))

    def second(self, half, k):
        c1, c2 = coords(half)
        o1 = around(c1, OFFSETS[k])
        src = self.out.at[piece(half, o1, c2), FULL]
        self.go(half, 4 + 4 * k, src, o1, c2, FULL, c1, around(c2, 1))
        self.go(half, 5 + 4 * k, src, o1, c2, FULL, c1, around(c2, -1))

    def first_near(self):
        for half in (0, 1):
            c1, c2 = coords(half)
            left = around(c1, -1)
            self.arrive(half, 0, left, c2, FULL)
            self.go(half, 2, self.out.at[piece(half, left, c2), LEFT], left, c2, LEFT, around(c1, 1), c2)
            self.second(half, 1)
        for half in (0, 1):
            c1, c2 = coords(half)
            right = around(c1, 1)
            self.arrive(half, 1, right, c2, FULL)
            self.go(half, 3, self.out.at[piece(half, right, c2), RIGHT], right, c2, RIGHT, around(c1, -1), c2)
            self.second(half, 2)

    def first_far(self):
        for half in (0, 1):
            c1, c2 = coords(half)
            far = around(c1, 2)
            self.arrive(half, 2, far, c2, LEFT)
            self.arrive(half, 3, far, c2, RIGHT)
            self.second(half, 3)

    def second_near(self, k):
        for half in (0, 1):
            c1, c2 = coords(half)
            o1 = around(c1, OFFSETS[k])
            for way in (0, 1):
                nb = around(c2, -1 if way == 0 else 1)
                to = around(c2, 1 if way == 0 else -1)
                lanes = LEFT if way == 0 else RIGHT
                self.arrive(half, 4 + 4 * k + way, o1, nb, FULL)
                self.go(half, 6 + 4 * k + way, self.out.at[piece(half, o1, nb), lanes], o1, nb, lanes, c1, to)

    def second_far(self, k):
        for half in (0, 1):
            c1, c2 = coords(half)
            o1 = around(c1, OFFSETS[k])
            far = around(c2, 2)
            self.arrive(half, 6 + 4 * k, o1, far, LEFT)
            self.arrive(half, 7 + 4 * k, o1, far, RIGHT)

    def run(self):
        self.start()
        self.first_near()
        self.second_near(0)
        self.first_far()
        for k in (1, 2, 3):
            self.second_near(k)
        for k in range(SIDE):
            self.second_far(k)

    def finish(self):
        for copy in self.sent:
            copy.wait_send()


GATHER_SEMS = [pltpu.SemaphoreType.DMA((2, 20)), pltpu.SemaphoreType.DMA((2, 20))]

SCATTER_SCRATCH = [
    pltpu.VMEM((D, STRETCH), bf16),
    pltpu.VMEM((2, SIDE, 2, HALF, LANES), bf16),
    pltpu.VMEM((2, SIDE, 2, HALF, STRETCH), bf16),
    pltpu.VMEM((2, SIDE, HALF, STRETCH), bf16),
    pltpu.VMEM((2, 2, HALF, LANES), bf16),
    pltpu.VMEM((2, 2, HALF, STRETCH), bf16),
    pltpu.SemaphoreType.DMA((2, 20)),
    pltpu.SemaphoreType.DMA((2, 20)),
]


class Scatter:
    def __init__(self, part, near1, full1, mid, near2, full2, send_sems, recv_sems):
        self.part, self.near1, self.full1, self.mid = part, near1, full1, mid
        self.near2, self.full2, self.ss, self.rs = near2, full2, send_sems, recv_sems
        self.sent = []

    def go(self, half, idx, src, dst, to1, to2):
        copy = remote(src, dst, self.ss.at[half, idx], self.rs.at[half, idx], device(half, to1, to2))
        copy.start()
        self.sent.append(copy)

    def arrive(self, half, idx, where):
        me1, me2 = coords(half)
        remote(where, where, self.ss.at[half, idx], self.rs.at[half, idx], device(half, around(me1, 1), me2)).wait_recv()

    def one(self, k):
        for half in (0, 1):
            c1, c2 = coords(half)
            o1 = around(c1, OFFSETS[k])
            rows = piece(half, o1, around(c2, 2))
            self.go(half, 4 * k, self.part.at[rows, LEFT], self.near1.at[half, k, 0], c1, around(c2, 1))
            self.go(half, 4 * k + 1, self.part.at[rows, RIGHT], self.near1.at[half, k, 1], c1, around(c2, -1))

    def two(self, k):
        for half in (0, 1):
            c1, c2 = coords(half)
            o1 = around(c1, OFFSETS[k])
            for way in (0, 1):
                to = around(c2, 1 if way == 0 else -1)
                lanes = LEFT if way == 0 else RIGHT
                rows = piece(half, o1, to)
                self.arrive(half, 4 * k + way, self.near1.at[half, k, way])
                mine = self.part[rows, lanes].astype(f32)
                self.part[rows, lanes] = (mine + self.near1[half, k, way].astype(f32)).astype(bf16)
                self.go(half, 4 * k + 2 + way, self.part.at[rows, FULL], self.full1.at[half, k, way], c1, to)

    def three(self, k):
        for half in (0, 1):
            c1, c2 = coords(half)
            o1 = around(c1, OFFSETS[k])
            self.arrive(half, 4 * k + 2, self.full1.at[half, k, 0])
            self.arrive(half, 4 * k + 3, self.full1.at[half, k, 1])
            if k:
                self.mid[half, k] = self.total(half, k).astype(bf16)
                if k == 3:
                    self.go(half, 16, self.mid.at[half, 3, :, LEFT], self.near2.at[half, 0], around(c1, 1), c2)
                    self.go(half, 17, self.mid.at[half, 3, :, RIGHT], self.near2.at[half, 1], around(c1, -1), c2)

    def total(self, half, k):
        c1, c2 = coords(half)
        rows = piece(half, around(c1, OFFSETS[k]), c2)
        return (
            self.part[rows, :].astype(f32)
            + self.full1[half, k, 0].astype(f32)
            + self.full1[half, k, 1].astype(f32)
        )

    def four(self, k):
        way = 0 if k == 2 else 1
        lanes = LEFT if way == 0 else RIGHT
        for half in (0, 1):
            c1, c2 = coords(half)
            self.arrive(half, 16 + way, self.near2.at[half, way])
            mine = self.mid[half, k, :, lanes].astype(f32)
            self.mid[half, k, :, lanes] = (mine + self.near2[half, way].astype(f32)).astype(bf16)
            self.go(half, 18 + way, self.mid.at[half, k], self.full2.at[half, way], around(c1, OFFSETS[k]), c2)

    def run(self):
        for k in (3, 2, 1, 0):
            self.one(k)
        for k in (3, 2, 1, 0):
            self.two(k)
        self.three(3)
        self.three(2)
        self.four(2)
        self.three(1)
        self.four(1)
        self.three(0)

    def result(self, half):
        self.arrive(half, 18, self.full2.at[half, 0])
        self.arrive(half, 19, self.full2.at[half, 1])
        return (
            self.total(half, 0)
            + self.full2[half, 0].astype(f32)
            + self.full2[half, 1].astype(f32)
        )

    def finish(self):
        for copy in self.sent:
            copy.wait_send()


def greet_heads():
    barrier = pltpu.get_barrier_semaphore()
    me = lax.axis_index("head")
    for by in range(1, HEADS):
        pl.semaphore_signal(
            barrier, inc=1, device_id={"head": lax.rem(me + by, HEADS)}, device_id_type=MESH
        )
    return barrier


def gather_kernel(hidden, embed, packed, hidden_all, embed_all, packed_all,
                  h_send, h_recv, e_send, e_recv, p_send, p_recv, local):
    barrier = greet_heads()
    seq = lax.axis_index("seq")
    for by in range(1, SEQ):
        pl.semaphore_signal(
            barrier, inc=1, device_id={"seq": lax.rem(seq + by, SEQ)}, device_id_type=MESH
        )
    me = lax.axis_index("head")
    mine = pl.ds(pl.multiple_of(me * SHARD, 16), SHARD)
    kept = [
        pltpu.make_async_copy(hidden, hidden_all.at[mine, FULL], local.at[0]),
        pltpu.make_async_copy(embed, embed_all.at[mine, FULL], local.at[1]),
        pltpu.make_async_copy(packed, packed_all.at[seq], local.at[2]),
    ]
    for copy in kept:
        copy.start()
    pl.semaphore_wait(barrier, HEADS - 1 + SEQ - 1)
    first = Gather(hidden, hidden_all, h_send, h_recv)
    second = Gather(embed, embed_all, e_send, e_recv)
    first.start()
    states = []
    for by in range(1, SEQ):
        copy = pltpu.make_async_remote_copy(
            src_ref=packed, dst_ref=packed_all.at[seq], send_sem=p_send.at[by - 1], recv_sem=p_recv.at[by - 1],
            device_id={"seq": lax.rem(seq + by, SEQ)}, device_id_type=MESH,
        )
        copy.start()
        states.append(copy)
    first.first_near()
    first.second_near(0)
    first.first_far()
    for k in (1, 2, 3):
        first.second_near(k)
    second.start()
    for k in range(SIDE):
        first.second_far(k)
    second.first_near()
    second.second_near(0)
    second.first_far()
    for k in (1, 2, 3):
        second.second_near(k)
    for k in range(SIDE):
        second.second_far(k)
    for by in range(1, SEQ):
        where = packed_all.at[lax.rem(seq - by + SEQ, SEQ)]
        pltpu.make_async_remote_copy(
            src_ref=where, dst_ref=where, send_sem=p_send.at[by - 1], recv_sem=p_recv.at[by - 1],
            device_id={"seq": lax.rem(seq + by, SEQ)}, device_id_type=MESH,
        ).wait_recv()
    first.finish()
    second.finish()
    for copy in states:
        copy.wait_send()
    for copy in kept:
        copy.wait()


def gather_call(hidden, embed, packed):
    anywhere = pl.BlockSpec(memory_space=pl.ANY)
    return pl.pallas_call(
        gather_kernel,
        out_shape=(
            jax.ShapeDtypeStruct((D, STRETCH), bf16),
            jax.ShapeDtypeStruct((D, STRETCH), bf16),
            jax.ShapeDtypeStruct((SEQ,) + packed.shape, f32),
        ),
        in_specs=[anywhere] * 3,
        out_specs=(anywhere,) * 3,
        scratch_shapes=GATHER_SEMS + GATHER_SEMS + [
            pltpu.SemaphoreType.DMA((SEQ - 1,)),
            pltpu.SemaphoreType.DMA((SEQ - 1,)),
            pltpu.SemaphoreType.DMA((3,)),
        ],
        compiler_params=pltpu.CompilerParams(collective_id=0, has_side_effects=True),
        name="gather_rows",
    )(hidden, embed, packed)


def products(weight, rows, part):
    width = 512

    def chunk(i, _):
        span = pl.ds(pl.multiple_of(i * width, width), width)
        part[span, :] = lax.dot_general(
            weight[:, span], rows, (((0,), (0,)), ((), ())), preferred_element_type=f32
        ).astype(bf16)
        return 0

    lax.fori_loop(0, D // width, chunk, 0)


def mix_kernel(gated, squares, weight, hidden, next_out, all_out,
               part, near1, full1, mid, near2, full2, s_send, s_recv,
               g_send, g_recv, peers, q_send, q_recv, rounded, local):
    barrier = greet_heads()
    pl.semaphore_wait(barrier, HEADS - 1)
    me = lax.axis_index("head")
    group = lax.div(me, 8)
    spot = lax.rem(me, 8)
    out = []
    for by in range(1, 8):
        copy = remote(
            squares, peers.at[by - 1], q_send.at[by - 1], q_recv.at[by - 1],
            group * 8 + lax.rem(spot + by, 8),
        )
        copy.start()
        out.append(copy)
    total = squares[0:1, :]
    for by in range(1, 8):
        out[by - 1].wait_recv()
        total = total + peers[by - 1, 0:1, :]
    scale = lax.rsqrt(total * (1.0 / (MH // G * P_SIZE)) + epsilon)
    products(weight, (gated[...] * scale).astype(bf16), part)
    scatter = Scatter(part, near1, full1, mid, near2, full2, s_send, s_recv)
    scatter.run()
    for half in (0, 1):
        rows = pl.ds(half * HALF, HALF)
        value = hidden[rows, :].astype(f32) + scatter.result(half)
        next_out[rows, :] = value
        rounded[rows, :] = value.astype(bf16)
    mine = pl.ds(pl.multiple_of(me * SHARD, 16), SHARD)
    keep = pltpu.make_async_copy(rounded, all_out.at[mine, FULL], local)
    keep.start()
    gather = Gather(rounded, all_out, g_send, g_recv)
    gather.run()
    gather.finish()
    scatter.finish()
    for copy in out:
        copy.wait_send()
    keep.wait()


def mix_call(gated, squares, weight, hidden):
    vmem = pl.BlockSpec(memory_space=pltpu.VMEM)
    return pl.pallas_call(
        mix_kernel,
        out_shape=(
            jax.ShapeDtypeStruct((SHARD, STRETCH), f32),
            jax.ShapeDtypeStruct((D, STRETCH), bf16),
        ),
        in_specs=[vmem] * 4,
        out_specs=(vmem, pl.BlockSpec(memory_space=pl.ANY)),
        scratch_shapes=SCATTER_SCRATCH + GATHER_SEMS + [
            pltpu.VMEM((7, 8, STRETCH), f32),
            pltpu.SemaphoreType.DMA((7,)),
            pltpu.SemaphoreType.DMA((7,)),
            pltpu.VMEM((SHARD, STRETCH), bf16),
            pltpu.SemaphoreType.DMA,
        ],
        compiler_params=pltpu.CompilerParams(
            collective_id=1, has_side_effects=True, vmem_limit_bytes=40 * 2**20
        ),
        name="mix_rows",
    )(gated, squares, weight, hidden)


def merge_kernel(attended, weight, before, out,
                 part, near1, full1, mid, near2, full2, s_send, s_recv):
    barrier = greet_heads()
    products(weight, attended[...], part)
    pl.semaphore_wait(barrier, HEADS - 1)
    scatter = Scatter(part, near1, full1, mid, near2, full2, s_send, s_recv)
    scatter.run()
    for half in (0, 1):
        rows = pl.ds(half * HALF, HALF)
        out[rows, :] = before[rows, :] + scatter.result(half)
    scatter.finish()


def merge_call(attended, weight, before):
    vmem = pl.BlockSpec(memory_space=pltpu.VMEM)
    return pl.pallas_call(
        merge_kernel,
        out_shape=jax.ShapeDtypeStruct((SHARD, STRETCH), f32),
        in_specs=[vmem] * 3,
        out_specs=vmem,
        scratch_shapes=SCATTER_SCRATCH,
        compiler_params=pltpu.CompilerParams(
            collective_id=2, has_side_effects=True, vmem_limit_bytes=40 * 2**20
        ),
        name="merge_rows",
    )(attended, weight, before)


def attend_kernel(table, length, queries, keys_new, values_new, pool, out, held, sems, acc, top, total):
    scale = HD ** -0.5
    span = STEPB * BLOCK
    limit = length[0]
    blocks = lax.div(limit + BLOCK - 1, BLOCK)
    steps = lax.div(blocks + STEPB - 1, STEPB)

    def fetch(step, slot):
        return [
            pltpu.make_async_copy(
                pool.at[table[step * STEPB + i]], held.at[slot, i], sems.at[slot, i]
            )
            for i in range(STEPB)
        ]

    for copy in fetch(0, 0):
        copy.start()
    q = queries[...]
    scores = lax.dot_general(q, keys_new[...], (((1,), (0,)), ((), ())), preferred_element_type=f32)
    row = lax.broadcasted_iota(jnp.int32, scores.shape, 0)
    col = lax.broadcasted_iota(jnp.int32, scores.shape, 1)
    scores = jnp.where(row >= col, scores, masked)
    high = jnp.max(scores, axis=1, keepdims=True)
    weights = jnp.exp((scores - high) * scale)
    top[...] = high
    total[...] = jnp.sum(weights, axis=1, keepdims=True)
    acc[...] = jnp.dot(weights.astype(bf16), values_new[...], preferred_element_type=f32)

    def step_body(step, _):
        slot = lax.rem(step, 2)

        @pl.when(step + 1 < steps)
        def _():
            for copy in fetch(step + 1, 1 - slot):
                copy.start()

        for copy in fetch(step, slot):
            copy.wait()
        keys = held[slot, :, 0].reshape(span, HD)
        values = held[slot, :, 1].reshape(span, HD)
        scores = lax.dot_general(q, keys, (((1,), (1,)), ((), ())), preferred_element_type=f32)

        def rest(scores):
            old = top[...]
            high = jnp.maximum(old, jnp.max(scores, axis=1, keepdims=True))
            weights = jnp.exp((scores - high) * scale)
            factor = jnp.exp((old - high) * scale)
            top[...] = high
            total[...] = total[...] * factor + jnp.sum(weights, axis=1, keepdims=True)
            acc[...] = acc[...] * factor + jnp.dot(
                weights.astype(bf16), values, preferred_element_type=f32
            )

        @pl.when((step + 1) * span <= limit)
        def _():
            rest(scores)

        @pl.when((step + 1) * span > limit)
        def _():
            where = step * span + lax.broadcasted_iota(jnp.int32, scores.shape, 1)
            rest(jnp.where(where < limit, scores, masked))

        return 0

    lax.fori_loop(0, steps, step_body, 0)
    out[...] = (acc[...] / total[...]).astype(bf16)


def attend_call(table, length, queries, keys_new, values_new, pool):
    vmem = pl.BlockSpec(memory_space=pltpu.VMEM)
    smem = pl.BlockSpec(memory_space=pltpu.SMEM)
    return pl.pallas_call(
        attend_kernel,
        out_shape=jax.ShapeDtypeStruct((STRETCH, HD), bf16),
        in_specs=[smem, smem, vmem, vmem, vmem, pl.BlockSpec(memory_space=pl.ANY)],
        out_specs=vmem,
        scratch_shapes=[
            pltpu.VMEM((2, STEPB, 2, BLOCK, HD), bf16),
            pltpu.SemaphoreType.DMA((2, STEPB)),
            pltpu.VMEM((STRETCH, HD), f32),
            pltpu.VMEM((STRETCH, 1), f32),
            pltpu.VMEM((STRETCH, 1), f32),
        ],
        compiler_params=pltpu.CompilerParams(vmem_limit_bytes=48 * 2**20),
        name="attend_rows",
    )(table, length, queries, keys_new, values_new, pool)


def shift_rows(matrix, by):
    if by == 0:
        return matrix
    return jnp.concatenate([jnp.zeros((by, matrix.shape[1]), f32), matrix[:-by]], axis=0)


def state_block(activated, step_sizes, cumulative, b_proj, c_proj, init_state, skip_gain):
    length = activated.shape[0]
    positions = jnp.arange(length)
    causal = (positions[:, None] >= positions[None, :])[None]
    cums_heads = cumulative.T
    gaps = cums_heads[:, :, None] - cums_heads[:, None, :]
    decays = jnp.where(causal, jnp.exp(jnp.where(causal, gaps, 0.0)), 0.0)
    product = jnp.einsum("tn,sn->ts", c_proj, b_proj, precision=highest)
    weighted = decays * product[None] * step_sizes.T[:, None, :]
    within = jnp.einsum("hts,shp->thp", weighted, activated, precision=highest)
    carried = (
        jnp.einsum("tn,hpn->thp", c_proj, init_state, precision=highest)
        * jnp.exp(cumulative)[:, :, None]
    )
    output = within + carried + skip_gain[None, :, None] * activated
    to_end = jnp.exp(cumulative[-1][None, :] - cumulative) * step_sizes
    final_state = jnp.exp(cumulative[-1])[:, None, None] * init_state + jnp.einsum(
        "shp,sn->hpn", activated * to_end[:, :, None], b_proj, precision=highest
    )
    return (output, final_state)


def body(hidden, embedding, input_gain, w_input, w_groups, w_step, step_bias, decay_rate, skip_gain,
         conv_weight, mix_gain, w_output, state_store, conv_store, state_slot, prefix_len, block_table,
         shared_gain, w_attend, cache_pool, w_merge):
    heads_local = w_step.shape[1]
    my_head = lax.axis_index("head")
    my_seq = lax.axis_index("seq")
    group_id = my_head * heads_local // (MH // G)
    pool = lax.all_gather(cache_pool, "seq", axis=0, tiled=True)

    rows = state_store.shape[0]
    tails = conv_store.astype(f32).reshape(rows, 6, 128)
    packed = jnp.concatenate(
        [state_store.reshape(rows, 128, 128), tails, jnp.zeros((rows, PACK - 134, 128), f32)], axis=1
    )
    hidden_t = hidden.T
    hidden_all, embed_all, packed_all = gather_call(hidden_t, embedding.T, packed)
    held = lax.dynamic_index_in_dim(
        packed_all.reshape(SEQ * rows, PACK, 128), state_slot[my_seq], 0, keepdims=False
    )
    init_state = held[:128].reshape(heads_local, P_SIZE, NS)
    conv_tail = held[128:134].reshape(CONV - 1, heads_local * P_SIZE)

    wide = hidden_all.astype(f32)
    mean = jnp.mean(wide * wide, axis=0, keepdims=True)
    normed = (wide * lax.rsqrt(mean + epsilon) * input_gain[:, None]).astype(bf16)
    over = (((0,), (0,)), ((), ()))
    paired = lax.dot_general(normed, w_input, over, preferred_element_type=f32).reshape(
        STRETCH, heads_local, 2, P_SIZE
    )
    gate_part = paired[:, :, 0]
    signal = paired[:, :, 1].reshape(STRETCH, heads_local * P_SIZE)
    grouped = lax.dot_general(normed, w_groups, over, preferred_element_type=f32)
    b_proj = lax.dynamic_slice_in_dim(grouped, group_id * NS, NS, 1)
    c_proj = lax.dynamic_slice_in_dim(grouped, (G + group_id) * NS, NS, 1)
    raw_steps = lax.dot_general(normed, w_step, over, preferred_element_type=f32)
    padded = jnp.concatenate([conv_tail, signal], axis=0)
    convolved = sum(conv_weight[k] * padded[k : k + STRETCH] for k in range(CONV))
    activated = jax.nn.silu(convolved).reshape(STRETCH, heads_local, P_SIZE)
    step_sizes = jax.nn.softplus(raw_steps + step_bias)
    cumulative = jnp.cumsum(-decay_rate * step_sizes, axis=0)
    scanned, final_state = state_block(
        activated, step_sizes, cumulative, b_proj, c_proj, init_state, skip_gain
    )
    gated = scanned * jax.nn.silu(gate_part)
    squares = jnp.sum(gated * gated, axis=(1, 2))
    gained = (gated.reshape(STRETCH, heads_local * P_SIZE) * mix_gain).T
    hidden_next, residual_all = mix_call(
        gained, jnp.broadcast_to(squares[None, :], (8, STRETCH)), w_output, hidden_t
    )

    res = residual_all.astype(f32)
    emb = embed_all.astype(f32)
    mean = (jnp.sum(res * res, axis=0) + jnp.sum(emb * emb, axis=0)) / (2 * D)
    scale = lax.rsqrt(mean + epsilon)[None, :]
    res = (res * scale * shared_gain[:D, None]).astype(bf16)
    emb = (emb * scale * shared_gain[D:, None]).astype(bf16)
    projected = (
        lax.dot_general(w_attend[:D], res, over, preferred_element_type=f32)
        + lax.dot_general(w_attend[D:], emb, over, preferred_element_type=f32)
    ).astype(bf16)
    attended = attend_call(
        block_table[my_seq], prefix_len[my_seq][None],
        projected[:HD].T, projected[HD : 2 * HD], projected[2 * HD :].T, pool,
    )
    layer_output = merge_call(attended.T, w_merge, hidden_next)
    return (layer_output.T, final_state.reshape(1, heads_local, P_SIZE * NS))


def solution(mesh):
    return jax.shard_map(
        body,
        mesh=mesh,
        in_specs=(
            P("seq", "head"),
            P("seq", "head"),
            P(),
            P(None, "head"),
            P(),
            P(None, "head"),
            P("head"),
            P("head"),
            P("head"),
            P(None, "head"),
            P("head"),
            P("head", None),
            P("seq", "head", None),
            P("seq", None, "head"),
            P(),
            P(),
            P(),
            P(),
            P(None, "head"),
            P("seq", None, None, "head"),
            P("head", None),
        ),
        out_specs=(P("seq", "head"), P("seq", "head", None)),
        check_vma=False,
    )
```

time: 643 us -> 238 us (0.37)
  the two profiles are of different devices: /device:TPU:0 before, /device:TPU:2 now
where the time goes in v1:
time: 238 us; the launch traced here: 236 us
  Pallas kernels  139 us (58%)
  local copies, waits for them, and re-layouts  44.4 us (19%)
  matrix products  25.9 us (11%)
  between operations  16.5 us (7%)
  other arithmetic  9.91 us (4%)
    pallas_call x1, Pallas kernels, mix_call(): pl.pallas_call(mix_kernel, out_shape=(jax.ShapeDtypeStruct((SHARD, STRETC...  53 us
    pallas_call x1, Pallas kernels, gather_call(): pl.pallas_call(gather_kernel, out_shape=(jax.ShapeDtypeStruct((D, STRETCH...  51 us
    all_gather x1, local copies, waits for them, and re-layouts, body(): pool = lax.all_gather(cache_pool, 'seq', axis=0, tiled=True)  24.7 us
    pallas_call x1, Pallas kernels, merge_call(): pl.pallas_call(merge_kernel, out_shape=jax.ShapeDtypeStruct((SHARD, STRET...  20.7 us
    pallas_call x1, Pallas kernels, attend_call(): pl.pallas_call(attend_kernel, out_shape=jax.ShapeDtypeStruct((STRETCH, HD...  14.2 us
    unnamed x54, local copies, waits for them, and re-layouts  7.97 us
    dot_general x1, matrix products, body(): lax.dot_general(w_attend[D:], emb, over, preferred_element_type=f32)  5.64 us
    dot_general x1, matrix products, body(): lax.dot_general(normed, w_input, over, preferred_element_type=f32)  5.55 us
  transfers between devices with their start and end apart: 1, of which 0 were waited for; matrix products, arithmetic and copies ran while one was open for 19% of the time, Pallas kernels for 44%

profile of v1, /device:TPU:2, one launch (start us, length us, event | category | flops | bytes accessed | tf_op | source)
XLA Modules:
  0.0 236.3 jit_solution(17254316997240197195)
XLA Ops:
  7.9 1.3 dynamic_slice.20.length
  9.2 1.2 dynamic_slice.21
  13.1 1.0 reshape.114
  14.9 0.7 maximum_maximum_fusion.packed
  15.6 51.0 %gather_rows.1 = (bf16[3584,512]{1,0:T(8,128)(2,1)}, bf16[3584,512]{1,0:T(8,128)(2,1)}, f32[8,2,136,128]{3,2,1,0:T(8,128)}) custom-call(bf16[224,512]{1,0:T(8,128)(2,1)} %bitcast.83, bf16[224,512]{1,0:T(8,128)(2,1)} %bitcast.93, f32[2,136,128]{2,1,0:T(8,128)} %maximum_maximum_fusion.packed), custom_call_target="tpu_custom_call" | custom-call | tf_op jit(solution)/shard_map/gather_rows/pallas_call | solution.py:340
  67.4 5.0 %fusion = (f32[512]{0:T(512)S(1)}, f32[512]{0:T(512)S(1)}) fusion(bf16[3584,512]{1,0:T(8,128)(2,1)} %get-tuple-element.8, bf16[3584,512]{1,0:T(8,128)(2,1)} %get-tuple-element.10), kind=kLoop, calls=%fused_computation.6 | loop fusion | flops 11009024 | bytes 7344128 | tf_op jit(solution)/shard_map/reduce_sum | solution.py:604
  72.4 1.0 broadcast_multiply_fusion
  73.4 1.4 reduce-window.6
  75.5 0.9 constant_dynamic-slice_fusion.1
  76.6 5.6 %fusion.74 = f32[512,512]{0,1:T(8,128)S(1)} fusion(bf16[3584,512]{1,0:T(8,128)(2,1)} %param.24, bf16[3584,512]{1,0:T(8,128)(2,1)} %get-tuple-element.8, f32[3584]{0:T(1024)S(1)} %copy-done.20, f32[512]{0:T(512)S(1)} %add_rsqrt_fusion.1), kind=kOutput, calls=%fused_computation.102 | convolution fusion | flops 1886388224 | bytes 8404992 | tf_op jit(solution)/shard_map/dot_general | solution.py:607
  82.1 1.0 copy-done.14
  84.0 3.5 %fusion.71 = f32[512,256]{0,1:T(8,128)S(1)} fusion(bf16[3584,256]{1,0:T(8,128)(2,1)S(1)} %copy-done, bf16[3584,512]{1,0:T(8,128)(2,1)} %get-tuple-element.8, f32[3584]{0:T(1024)S(1)} %copy-done.20, f32[512]{0:T(512)S(1)} %add_rsqrt_fusion.1), kind=kOutput, calls=%fused_computation.101 | convolution fusion | flops 946864128 | bytes 6045696 | tf_op jit(solution)/shard_map/dot_general | solution.py:612
  88.1 0.7 reshape.125
  89.0 1.0 fusion.56
  90.0 5.1 %fusion.37 = f32[512,4,64]{0,2,1:T(8,128)S(1)} fusion(f32[512,4,64]{0,2,1:T(8,128)S(1)} %bitcast.88, f32[4,512]{1,0:T(4,128)S(1)} %get-tuple-element.22, f32[512,512]{1,0:T(8,128)S(1)} %fusion.56, f32[4,512]{1,0:T(4,128)S(1)} %bitcast.95, pred[512,512]{1,0:T(8,128)(4,1)S(1)} %iota_compare_fusion), kind=kOutput, calls=%fused_computation.37 | convolution fusion | flops 810549248 | bytes 2375680 | tf_op jit(solution)/shard_map/hts,shp->thp/dot_general | solution.py:568
  95.2 0.7 multiply_reduce_fusion
  96.6 53.0 %mix_rows.1 = (f32[224,512]{1,0:T(8,128)S(1)}, bf16[3584,512]{1,0:T(8,128)(2,1)S(1)}) custom-call(f32[256,512]{1,0:T(8,128)S(1)} %bitcast.81, f32[8,512]{1,0:T(8,128)S(1)} %broadcast_in_dim.25.squares, bf16[256,3584]{1,0:T(8,128)(2,1)S(1)} %copy-done.2, bf16[224,512]{1,0:T(8,128)(2,1)S(1)} %bitcast.84), custom_call_target="tpu_custom_call" | custom-call | tf_op jit(solution)/shard_map/mix_rows/pallas_call | solution.py:415
  149.7 0.8 fusion.3
  150.6 5.6 %fusion.9 = f32[512,672]{0,1:T(8,128)S(1)} fusion(bf16[7168,672]{0,1:T(8,128)(2,1)} %param.39, bf16[3584,512]{1,0:T(8,128)(2,1)S(1)} %copy-done.12, f32[3584]{0:T(1024)S(1)} %get-tuple-element.16, f32[512]{0:T(512)S(1)} %add_rsqrt_fusion), kind=kOutput, calls=%fused_computation.15 | convolution fusion | flops 2473590784 | bytes 9879552 | tf_op jit(solution)/shard_map/dot_general | solution.py:639
  156.3 2.7 %fusion.32 = bf16[512,672]{0,1:T(8,128)(2,1)S(1)} fusion(f32[512,672]{0,1:T(8,128)S(1)} %fusion.9, bf16[3584,512]{1,0:T(8,128)(2,1)S(1)} %get-tuple-element.9, f32[3584]{0:T(1024)S(1)} %get-tuple-element.15, f32[512]{0:T(512)S(1)} %add_rsqrt_fusion, bf16[7168,672]{0,1:T(8,128)(2,1)S(1)} %bitcast.104), kind=kOutput, calls=%fused_computation.36 | convolution fusion | flops 2474278912 | bytes 10569728 | tf_op jit(solution)/shard_map/dot_general | solution.py:638
  159.3 0.9 slice_bitcast_fusion.1
  160.3 0.8 copy.51.keys_new
  161.8 24.7 %copy.52.pool = bf16[160,2,128,224]{3,2,1,0:T(8,128)(2,1)} copy(bf16[160,2,128,224]{2,3,1,0:T(8,128)(2,1)} %all-gather.2.cloned.1.call-done) | data formatting | bytes 36700160 | tf_op jit(solution)/shard_map/all_gather | solution.py:588
  186.5 0.9 copy-done.5
  187.5 0.9 copy-done.6
  188.4 0.9 copy-done.7
  189.3 14.2 %attend_rows.1 = bf16[512,224]{1,0:T(8,128)(2,1)S(1)} custom-call(s32[64]{0:T(128)S(1)} %fusion.68.table, s32[1]{0:T(128)} %dynamic_slice.20.length, bf16[512,224]{1,0:T(8,128)(2,1)S(1)} %copy-done.6, bf16[224,512]{1,0:T(8,128)(2,1)S(1)} %copy-done.7, bf16[512,224]{1,0:T(8,128)(2,1)S(1)} %copy-done.5, bf16[160,2,128,224]{3,2,1,0:T(8,128)(2,1)} %copy.52.pool), custom_call_target="tpu_custom_call" | custom-call | tf_op jit(solution)/shard_map/attend_rows/pallas_call | solution.py:536
  204.3 1.8 copy.53
  206.1 0.9 copy-done.9
  207.0 1.0 copy-done.11
  208.0 20.7 %merge_rows.1 = f32[224,512]{1,0:T(8,128)S(1)} custom-call(bf16[224,512]{1,0:T(8,128)(2,1)S(1)} %bitcast.85, bf16[224,3584]{1,0:T(8,128)(2,1)S(1)} %copy-done.3, f32[224,512]{1,0:T(8,128)S(1)} %copy-done.11), custom_call_target="tpu_custom_call" | custom-call | tf_op jit(solution)/shard_map/merge_rows/pallas_call | solution.py:452
  228.7 0.8 copy.65
  (79 shorter events, 7.6 us)
Async XLA Ops:
  7.2 76.9 %copy-start = (bf16[3584,256]{1,0:T(8,128)(2,1)S(1)}, bf16[3584,256]{1,0:T(8,128)(2,1)}, u32[]{:S(2)}) copy-start(bf16[3584,256]{1,0:T(8,128)(2,1)} %param.25) | copy-start | bytes 5505028
  7.2 154.6 %all-gather.2.cloned.1.call-start = ((), (), s32[]{:S(2)}) async-start(), calls=%async_computation | async-start | bytes 20643840 | tf_op jit(solution)/shard_map/all_gather | solution.py:588
  14.1 58.3 %copy-start.19 = (bf16[3584,4]{0,1:T(4,128)(2,1)S(1)}, bf16[3584,4]{0,1:T(4,128)(2,1)}, u32[]{:S(2)}) copy-start(bf16[3584,4]{0,1:T(4,128)(2,1)} %param.26) | copy-start | bytes 86020
  14.1 58.3 %copy-start.20 = (f32[3584]{0:T(1024)S(1)}, f32[3584]{0:T(1024)}, u32[]{:S(2)}) copy-start(f32[3584]{0:T(1024)} %param.23) | copy-start | bytes 43012
  14.1 58.3 %copy-start.21 = (f32[4]{0:T(128)S(1)}, f32[4]{0:T(128)}, u32[]{:S(2)}) copy-start(f32[4]{0:T(128)} %param.27) | copy-start | bytes 52
  67.4 5.1 %copy-start.13 = (bf16[3584,512]{1,0:T(8,128)(2,1)S(1)}, bf16[3584,512]{1,0:T(8,128)(2,1)}, u32[]{:S(2)}) copy-start(bf16[3584,512]{1,0:T(8,128)(2,1)} %get-tuple-element.8) | copy-start | bytes 11010052
  76.5 6.7 %copy-start.17 = (f32[4,256]{1,0:T(4,128)S(1)}, f32[4,256]{1,0:T(4,128)}, u32[]{:S(2)}) copy-start(f32[4,256]{1,0:T(4,128)} %param.30) | copy-start | bytes 12292
  82.1 1.0 copy-start.14
  90.0 5.2 %copy-start.15 = (f32[512,512]{0,1:T(8,128)S(1)}, f32[512,512]{0,1:T(8,128)}, u32[]{:S(2)}) copy-start(f32[512,512]{0,1:T(8,128)} %copy-done.14) | copy-start | bytes 3145732
  90.0 5.2 %copy-start.22 = (f32[4]{0:T(128)S(1)}, f32[4]{0:T(128)}, u32[]{:S(2)}) copy-start(f32[4]{0:T(128)} %param.29) | copy-start | bytes 52
  90.0 5.9 %copy-start.18 = (f32[256]{0:T(256)S(1)}, f32[256]{0:T(256)}, u32[]{:S(2)}) copy-start(f32[256]{0:T(256)} %param.31) | copy-start | bytes 3076
  95.1 1.5 copy-start.2
  95.1 1.5 copy-start.8
  95.9 54.7 %copy-start.16 = (f32[7168]{0:T(1024)S(1)}, f32[7168]{0:T(1024)}, u32[]{:S(2)}) copy-start(f32[7168]{0:T(1024)} %param.38) | copy-start | bytes 86020
  95.9 54.7 %copy-start.12 = (bf16[3584,512]{1,0:T(8,128)(2,1)S(1)}, bf16[3584,512]{1,0:T(8,128)(2,1)}, u32[]{:S(2)}) copy-start(bf16[3584,512]{1,0:T(8,128)(2,1)} %get-tuple-element.10) | copy-start | bytes 11010052
  149.7 6.6 %copy-start.10 = (f32[224,512]{1,0:T(8,128)}, f32[224,512]{1,0:T(8,128)S(1)}, u32[]{:S(2)}) copy-start(f32[224,512]{1,0:T(8,128)S(1)} %get-tuple-element.11.before) | copy-start | bytes 1376260
  149.7 6.6 %slice-start = ((s8[9633792]{0:T(1024)(128)(4,1)}), s8[4194304]{0:T(1024)(128)(4,1)S(1)}, s32[]{:S(2)}) async-start(s8[9633792]{0:T(1024)(128)(4,1)} %bitcast.103), calls=%async_computation.1 | async-start | bytes 8388608
  150.6 5.7 %slice-start.1 = ((s8[9633792]{0:T(1024)(128)(4,1)}), s8[4194304]{0:T(1024)(128)(4,1)S(1)}, s32[]{:S(2)}) async-start(s8[9633792]{0:T(1024)(128)(4,1)} %bitcast.103), calls=%async_computation.2 | async-start | bytes 8388608
  150.6 5.7 %slice-start.2 = ((s8[9633792]{0:T(1024)(128)(4,1)}), s8[1245184]{0:T(1024)(128)(4,1)S(1)}, s32[]{:S(2)}) async-start(s8[9633792]{0:T(1024)(128)(4,1)} %bitcast.103), calls=%async_computation.3 | async-start | bytes 2490368
  186.5 0.9 copy-start.5
  187.4 0.9 copy-start.6
  188.4 0.9 copy-start.7
  189.3 16.7 %copy-start.3 = (bf16[224,3584]{1,0:T(8,128)(2,1)S(1)}, bf16[224,3584]{1,0:T(8,128)(2,1)}, u32[]{:S(2)}) copy-start(bf16[224,3584]{1,0:T(8,128)(2,1)} %weight.3) | copy-start | bytes 4816900
  189.3 40.1 %copy-start.1 = (bf16[3584,256]{1,0:T(8,128)(2,1)S(1)}, bf16[3584,256]{1,0:T(8,128)(2,1)}, u32[]{:S(2)}) copy-start(bf16[3584,256]{1,0:T(8,128)(2,1)} %param.25) | copy-start | bytes 5505028
  203.6 0.7 copy-start.4
  206.1 0.9 copy-start.9
  207.0 1.0 copy-start.11
Sparse Core Ops, SparseCore 0:
  9.7 102.3 all-gather.1

commit v2 on v1

--- a/solution.py
+++ b/solution.py
@@ -23,7 +23,6 @@
 SHARD = D // HEADS
 HALF = SHARD // 2
 LANES = STRETCH // 2
-PACK = 136
 STEPB = 8
 
 MESH = pl.DeviceIdType.MESH
@@ -277,35 +276,98 @@
     return barrier
 
 
-def gather_kernel(hidden, embed, packed, hidden_all, embed_all, packed_all,
-                  h_send, h_recv, e_send, e_recv, p_send, p_recv, local):
+def flat(row, count):
+    turned = jnp.broadcast_to(row, (128, count)).T
+    return jnp.concatenate([turned] * (STRETCH // 128), axis=1)
+
+
+def column(table, start, count):
+    rows = table.shape[0]
+    entry = start + lax.broadcasted_iota(jnp.int32, (count, rows), 0)
+    pick = (lax.shift_right_logical(entry, 7) == lax.broadcasted_iota(jnp.int32, (count, rows), 1))
+    lines = jnp.dot(pick.astype(f32), table[...], precision=highest, preferred_element_type=f32)
+    entry = start + lax.broadcasted_iota(jnp.int32, (count, 128), 0)
+    keep = jnp.bitwise_and(entry, 127) == lax.broadcasted_iota(jnp.int32, (count, 128), 1)
+    return jnp.sum(jnp.where(keep, lines, 0.0), axis=1, keepdims=True)
+
+
+def send_sums(mine, peers, send_sems, recv_sems):
+    me = lax.axis_index("head")
+    out = []
+    for by in range(1, HEADS):
+        copy = remote(
+            mine, peers.at[by - 1], send_sems.at[by - 1], recv_sems.at[by - 1],
+            lax.rem(me + by, HEADS),
+        )
+        copy.start()
+        out.append(copy)
+    return out
+
+
+def add_sums(mine, peers, out):
+    total = mine[...]
+    for by in range(1, HEADS):
+        out[by - 1].wait_recv()
+        total = total + peers[by - 1]
+    return total
+
+
+def silu(value):
+    return value / (1.0 + jnp.exp(-value))
+
+
+TN = (((0,), (0,)), ((), ()))
+NT = (((1,), (1,)), ((), ()))
+HL = 4
+
+
+def scan_kernel(hidden, embed, gain_in, gain_sh, states, tails, slots, w_in, w_gr, w_st, bias, decay, skip,
+                conv_w, mix_g, gained_out, squares_out, final_out, embed_all, embed_sq,
+                wide, own_h, own_e, win, wgr, paired, grouped, sums, peers, stores, tail_all, lines,
+                h_send, h_recv, e_send, e_recv, q_send, q_recv, s_send, s_recv, t_send, t_recv, local):
+    seq = lax.axis_index("seq")
+    me = lax.axis_index("head")
+    loads = [
+        pltpu.make_async_copy(w_in, win, local.at[0]),
+        pltpu.make_async_copy(w_gr, wgr, local.at[1]),
+        pltpu.make_async_copy(states, stores.at[pl.ds(seq * 2, 2)], local.at[2]),
+        pltpu.make_async_copy(tails, tail_all.at[pl.ds(seq * 2, 2)], local.at[3]),
+    ]
+    for copy in loads:
+        copy.start()
     barrier = greet_heads()
-    seq = lax.axis_index("seq")
     for by in range(1, SEQ):
         pl.semaphore_signal(
             barrier, inc=1, device_id={"seq": lax.rem(seq + by, SEQ)}, device_id_type=MESH
         )
-    me = lax.axis_index("head")
     mine = pl.ds(pl.multiple_of(me * SHARD, 16), SHARD)
-    kept = [
-        pltpu.make_async_copy(hidden, hidden_all.at[mine, FULL], local.at[0]),
-        pltpu.make_async_copy(embed, embed_all.at[mine, FULL], local.at[1]),
-        pltpu.make_async_copy(packed, packed_all.at[seq], local.at[2]),
-    ]
-    for copy in kept:
-        copy.start()
+    value = hidden[...].astype(f32)
+    sq_h = jnp.sum(value * value, axis=0, keepdims=True)
+    ready = (value * column(gain_in, me * SHARD, SHARD)).astype(bf16)
+    own_h[...] = ready
+    wide[mine, :] = ready
     pl.semaphore_wait(barrier, HEADS - 1 + SEQ - 1)
-    first = Gather(hidden, hidden_all, h_send, h_recv)
-    second = Gather(embed, embed_all, e_send, e_recv)
+    first = Gather(own_h, wide, h_send, h_recv)
+    second = Gather(own_e, embed_all, e_send, e_recv)
     first.start()
-    states = []
+    value = embed[...].astype(f32)
+    sq_e = jnp.sum(value * value, axis=0, keepdims=True)
+    own_e[...] = (value * column(gain_sh, D + me * SHARD, SHARD)).astype(bf16)
+    line = lax.broadcasted_iota(jnp.int32, (8, STRETCH), 0)
+    sums[...] = jnp.where(line == 0, sq_h, jnp.where(line == 1, sq_e, 0.0))
+    out = send_sums(sums, peers, q_send, q_recv)
+    kept = pltpu.make_async_copy(own_e, embed_all.at[mine, FULL], local.at[4])
+    kept.start()
+    moved = []
     for by in range(1, SEQ):
-        copy = pltpu.make_async_remote_copy(
-            src_ref=packed, dst_ref=packed_all.at[seq], send_sem=p_send.at[by - 1], recv_sem=p_recv.at[by - 1],
-            device_id={"seq": lax.rem(seq + by, SEQ)}, device_id_type=MESH,
-        )
-        copy.start()
-        states.append(copy)
+        to = {"seq": lax.rem(seq + by, SEQ)}
+        for src, dst, ss, rs in ((states, stores, s_send, s_recv), (tails, tail_all, t_send, t_recv)):
+            copy = pltpu.make_async_remote_copy(
+                src_ref=src, dst_ref=dst.at[pl.ds(seq * 2, 2)], send_sem=ss.at[by - 1], recv_sem=rs.at[by - 1],
+                device_id=to, device_id_type=MESH,
+            )
+            copy.start()
+            moved.append(copy)
     first.first_near()
     first.second_near(0)
     first.first_far()
@@ -314,46 +376,147 @@
     second.start()
     for k in range(SIDE):
         first.second_far(k)
+    total = add_sums(sums, peers, out)
+    embed_sq[...] = total
+    scale = lax.rsqrt(total[0:1, :] * (1.0 / D) + epsilon)
+    for copy in loads:
+        copy.wait()
+
+    def project(i, _):
+        span = pl.ds(pl.multiple_of(i * 256, 256), 256)
+        paired[span, :] = scale * lax.dot_general(win[:, span], wide[...], TN, preferred_element_type=f32)
+        return 0
+
+    lax.fori_loop(0, 2, project, 0)
     second.first_near()
+    grouped[...] = scale * lax.dot_general(wgr[...], wide[...], TN, preferred_element_type=f32)
+    raw = scale * jnp.dot(w_st[...], wide[...], preferred_element_type=f32)
     second.second_near(0)
     second.first_far()
-    for k in (1, 2, 3):
-        second.second_near(k)
+    head = lax.broadcasted_iota(jnp.int32, (HL, STRETCH), 0)
+
+    def by_head(ref):
+        line = jnp.zeros((HL, STRETCH), f32)
+        for i in range(HL):
+            line = jnp.where(head == i, ref[i], line)
+        return line
+
+    raw = raw + by_head(bias)
+    steps = jnp.maximum(raw, 0.0) + jnp.log1p(jnp.exp(-jnp.abs(raw)))
+    cums = -by_head(decay) * steps
+    lane = lax.broadcasted_iota(jnp.int32, (HL, STRETCH), 1)
+    by = 1
+    while by < STRETCH:
+        cums = cums + jnp.where(lane >= by, pltpu.roll(cums, by, 1), 0.0)
+        by *= 2
+    turned = jnp.concatenate([cums, steps, jnp.zeros((128 - 2 * HL, STRETCH), f32)], axis=0).T
+    group = lax.div(me, 8)
+    b_proj = grouped[pl.ds(pl.multiple_of(group * NS, NS), NS), :]
+    c_proj = grouped[pl.ds(pl.multiple_of(G * NS + group * NS, NS), NS), :]
+    pairs = lax.dot_general(b_proj.astype(bf16), c_proj.astype(bf16), TN, preferred_element_type=f32)
+    src = lax.broadcasted_iota(jnp.int32, pairs.shape, 0)
+    dst = lax.broadcasted_iota(jnp.int32, pairs.shape, 1)
+    pairs = jnp.where(src <= dst, pairs, 0.0)
+
+    for copy in moved:
+        copy.wait_recv()
+    slot = slots[seq]
+    for h in range(HL):
+        for i in range(32):
+            lines[pl.ds(h * 32 + i, 1), :] = stores[slot, h : h + 1, i * 128 : (i + 1) * 128]
+    p_row = lax.broadcasted_iota(jnp.int32, (P_SIZE, 32), 0)
+    p_col = lax.broadcasted_iota(jnp.int32, (P_SIZE, 32), 1)
+    even = (p_row == 2 * p_col).astype(f32)
+    odd = (p_row == 2 * p_col + 1).astype(f32)
+    tail = tail_all[slot]
+    t_row = lax.broadcasted_iota(jnp.int32, (8, 128), 0)
+    t_col = lax.broadcasted_iota(jnp.int32, (8, 128), 1)
+    before = []
+    for j in range(2):
+        pick = jnp.zeros((8, 128), f32)
+        for k in range(CONV - 1):
+            pick = jnp.where((t_row == 2 * k + j) & (t_col == 125 + k), 1.0, pick)
+        before.append(lax.dot_general(tail, pick, TN, precision=highest, preferred_element_type=f32))
+    taps = [flat(conv_w[k : k + 1, :], HL * P_SIZE) for k in range(CONV)]
+    mixing = flat(mix_g[...], HL * P_SIZE)
+    squares = jnp.zeros((1, STRETCH), f32)
+    for h in range(HL):
+        chan = slice(h * P_SIZE, (h + 1) * P_SIZE)
+        gate = paired[h * 128 : h * 128 + 64, :]
+        signal = paired[h * 128 + 64 : h * 128 + 128, :]
+        half = (h % 2) * P_SIZE
+        padded = jnp.concatenate([before[h // 2][half : half + P_SIZE], signal], axis=1)
+        conv = taps[CONV - 1][chan] * signal
+        for back in range(1, CONV):
+            conv = conv + taps[CONV - 1 - back][chan] * pltpu.roll(padded, back, 1)[:, 128:]
+        active = silu(conv)
+        cum = cums[h : h + 1, :]
+        step = steps[h : h + 1, :]
+        mix = jnp.exp(jnp.minimum(cum - turned[:, h : h + 1], 0.0)) * pairs * turned[:, HL + h : HL + h + 1]
+        within = jnp.dot(active.astype(bf16), mix.astype(bf16), preferred_element_type=f32)
+        rows = lines[h * 32 : (h + 1) * 32, :]
+        init = jnp.dot(even, rows[:, :NS], precision=highest, preferred_element_type=f32)
+        init = init + jnp.dot(odd, rows[:, NS:], precision=highest, preferred_element_type=f32)
+        carried = jnp.dot(init, c_proj, precision=highest, preferred_element_type=f32) * jnp.exp(cum)
+        gated = (within + carried + skip[h] * active) * silu(gate)
+        squares = squares + jnp.sum(gated * gated, axis=0, keepdims=True)
+        gained_out[chan, :] = gated * mixing[chan]
+        last = cum[:, STRETCH - 1 :]
+        to_end = jnp.exp(last - cum) * step
+        final_out[chan, :] = jnp.exp(last) * init + lax.dot_general(
+            active * to_end, b_proj, NT, precision=highest, preferred_element_type=f32
+        )
+        if h:
+            second.second_near(h)
+    squares_out[...] = jnp.broadcast_to(squares, (8, STRETCH))
     for k in range(SIDE):
         second.second_far(k)
-    for by in range(1, SEQ):
-        where = packed_all.at[lax.rem(seq - by + SEQ, SEQ)]
-        pltpu.make_async_remote_copy(
-            src_ref=where, dst_ref=where, send_sem=p_send.at[by - 1], recv_sem=p_recv.at[by - 1],
-            device_id={"seq": lax.rem(seq + by, SEQ)}, device_id_type=MESH,
-        ).wait_recv()
     first.finish()
     second.finish()
-    for copy in states:
+    for copy in out + moved:
         copy.wait_send()
-    for copy in kept:
-        copy.wait()
-
-
-def gather_call(hidden, embed, packed):
+    kept.wait()
+
+
+def scan_call(hidden, embed, gain_in, gain_sh, states, tails, slots, w_in, w_gr, w_st, bias, decay, skip,
+              conv_w, mix_g):
     anywhere = pl.BlockSpec(memory_space=pl.ANY)
+    vmem = pl.BlockSpec(memory_space=pltpu.VMEM)
+    smem = pl.BlockSpec(memory_space=pltpu.SMEM)
+    dma = pltpu.SemaphoreType.DMA
     return pl.pallas_call(
-        gather_kernel,
+        scan_kernel,
         out_shape=(
+            jax.ShapeDtypeStruct((HL * P_SIZE, STRETCH), f32),
+            jax.ShapeDtypeStruct((8, STRETCH), f32),
+            jax.ShapeDtypeStruct((HL * P_SIZE, NS), f32),
             jax.ShapeDtypeStruct((D, STRETCH), bf16),
-            jax.ShapeDtypeStruct((D, STRETCH), bf16),
-            jax.ShapeDtypeStruct((SEQ,) + packed.shape, f32),
+            jax.ShapeDtypeStruct((8, STRETCH), f32),
         ),
-        in_specs=[anywhere] * 3,
-        out_specs=(anywhere,) * 3,
-        scratch_shapes=GATHER_SEMS + GATHER_SEMS + [
-            pltpu.SemaphoreType.DMA((SEQ - 1,)),
-            pltpu.SemaphoreType.DMA((SEQ - 1,)),
-            pltpu.SemaphoreType.DMA((3,)),
+        in_specs=[vmem] * 4 + [anywhere] * 2 + [smem] + [anywhere] * 2 + [vmem] + [smem] * 3 + [vmem] * 2,
+        out_specs=(vmem, vmem, vmem, anywhere, vmem),
+        scratch_shapes=[
+            pltpu.VMEM((D, STRETCH), bf16),
+            pltpu.VMEM((SHARD, STRETCH), bf16),
+            pltpu.VMEM((SHARD, STRETCH), bf16),
+            pltpu.VMEM((D, HL * 128), bf16),
+            pltpu.VMEM((D, 2 * G * NS), bf16),
+            pltpu.VMEM((HL * 128, STRETCH), f32),
+            pltpu.VMEM((2 * G * NS, STRETCH), f32),
+            pltpu.VMEM((8, STRETCH), f32),
+            pltpu.VMEM((HEADS - 1, 8, STRETCH), f32),
+            pltpu.VMEM((2 * SEQ, HL, P_SIZE * NS), f32),
+            pltpu.VMEM((2 * SEQ, 8, 128), f32),
+            pltpu.VMEM((128, 128), f32),
+        ] + GATHER_SEMS + GATHER_SEMS + [
+            dma((HEADS - 1,)), dma((HEADS - 1,)), dma((SEQ - 1,)), dma((SEQ - 1,)),
+            dma((SEQ - 1,)), dma((SEQ - 1,)), dma((5,)),
         ],
-        compiler_params=pltpu.CompilerParams(collective_id=0, has_side_effects=True),
-        name="gather_rows",
-    )(hidden, embed, packed)
+        compiler_params=pltpu.CompilerParams(
+            collective_id=0, has_side_effects=True, vmem_limit_bytes=48 * 2**20
+        ),
+        name="scan_rows",
+    )(hidden, embed, gain_in, gain_sh, states, tails, slots, w_in, w_gr, w_st, bias, decay, skip, conv_w, mix_g)
 
 
 def products(weight, rows, part):
@@ -369,9 +532,16 @@
     lax.fori_loop(0, D // width, chunk, 0)
 
 
-def mix_kernel(gated, squares, weight, hidden, next_out, all_out,
+def mix_kernel(gated, squares, weight, hidden, gain_sh, w_att, embed_all, embed_sq, next_out, proj_out,
                part, near1, full1, mid, near2, full2, s_send, s_recv,
-               g_send, g_recv, peers, q_send, q_recv, rounded, local):
+               g_send, g_recv, peers, q_send, q_recv, sums, peers2, r_send, r_recv, rounded, watt, emb, wide,
+               acc, local):
+    loads = [
+        pltpu.make_async_copy(embed_all, emb, local.at[0]),
+        pltpu.make_async_copy(w_att, watt, local.at[1]),
+    ]
+    for copy in loads:
+        copy.start()
     barrier = greet_heads()
     pl.semaphore_wait(barrier, HEADS - 1)
     me = lax.axis_index("head")
@@ -392,46 +562,93 @@
     scale = lax.rsqrt(total * (1.0 / (MH // G * P_SIZE)) + epsilon)
     products(weight, (gated[...] * scale).astype(bf16), part)
     scatter = Scatter(part, near1, full1, mid, near2, full2, s_send, s_recv)
-    scatter.run()
+    for k in (3, 2, 1, 0):
+        scatter.one(k)
+    for copy in loads:
+        copy.wait()
+
+    def from_embed(i):
+        acc[i * SHARD : (i + 1) * SHARD, :] = jnp.dot(
+            watt[i * SHARD : (i + 1) * SHARD, D:], emb[...], preferred_element_type=f32
+        )
+
+    for k in (3, 2, 1, 0):
+        scatter.two(k)
+    from_embed(0)
+    scatter.three(3)
+    scatter.three(2)
+    from_embed(1)
+    scatter.four(2)
+    scatter.three(1)
+    scatter.four(1)
+    scatter.three(0)
+    from_embed(2)
+    gain = column(gain_sh, me * SHARD, SHARD)
+    mine = pl.ds(pl.multiple_of(me * SHARD, 16), SHARD)
+    sq = jnp.zeros((1, STRETCH), f32)
     for half in (0, 1):
         rows = pl.ds(half * HALF, HALF)
         value = hidden[rows, :].astype(f32) + scatter.result(half)
         next_out[rows, :] = value
-        rounded[rows, :] = value.astype(bf16)
-    mine = pl.ds(pl.multiple_of(me * SHARD, 16), SHARD)
-    keep = pltpu.make_async_copy(rounded, all_out.at[mine, FULL], local)
-    keep.start()
-    gather = Gather(rounded, all_out, g_send, g_recv)
-    gather.run()
+        value = value.astype(bf16).astype(f32)
+        sq = sq + jnp.sum(value * value, axis=0, keepdims=True)
+        rounded[rows, :] = (value * gain[half * HALF : (half + 1) * HALF]).astype(bf16)
+    sums[...] = jnp.broadcast_to(sq, (8, STRETCH))
+    gather = Gather(rounded, wide, g_send, g_recv)
+    gather.start()
+    sent = send_sums(sums, peers2, r_send, r_recv)
+    wide[mine, :] = rounded[...]
+    gather.first_near()
+    gather.second_near(0)
+    gather.first_far()
+    for k in (1, 2, 3):
+        gather.second_near(k)
+    for k in range(SIDE):
+        gather.second_far(k)
+    total = add_sums(sums, peers2, sent)[0:1, :] + embed_sq[1:2, :]
+    scale = lax.rsqrt(total * (0.5 / D) + epsilon)
+    for i in range(3):
+        rows = slice(i * SHARD, (i + 1) * SHARD)
+        value = acc[rows, :] + jnp.dot(watt[rows, :D], wide[...], preferred_element_type=f32)
+        proj_out[rows, :] = (value * scale).astype(bf16)
     gather.finish()
     scatter.finish()
-    for copy in out:
+    for copy in out + sent:
         copy.wait_send()
-    keep.wait()
-
-
-def mix_call(gated, squares, weight, hidden):
+
+
+def mix_call(gated, squares, weight, hidden, gain_sh, w_att, embed_all, embed_sq):
     vmem = pl.BlockSpec(memory_space=pltpu.VMEM)
+    anywhere = pl.BlockSpec(memory_space=pl.ANY)
+    dma = pltpu.SemaphoreType.DMA
     return pl.pallas_call(
         mix_kernel,
         out_shape=(
             jax.ShapeDtypeStruct((SHARD, STRETCH), f32),
-            jax.ShapeDtypeStruct((D, STRETCH), bf16),
+            jax.ShapeDtypeStruct((3 * HD, STRETCH), bf16),
         ),
-        in_specs=[vmem] * 4,
-        out_specs=(vmem, pl.BlockSpec(memory_space=pl.ANY)),
+        in_specs=[vmem] * 5 + [anywhere] * 2 + [vmem],
+        out_specs=(vmem, vmem),
         scratch_shapes=SCATTER_SCRATCH + GATHER_SEMS + [
             pltpu.VMEM((7, 8, STRETCH), f32),
-            pltpu.SemaphoreType.DMA((7,)),
-            pltpu.SemaphoreType.DMA((7,)),
+            dma((7,)),
+            dma((7,)),
+            pltpu.VMEM((8, STRETCH), f32),
+            pltpu.VMEM((HEADS - 1, 8, STRETCH), f32),
+            dma((HEADS - 1,)),
+            dma((HEADS - 1,)),
             pltpu.VMEM((SHARD, STRETCH), bf16),
-            pltpu.SemaphoreType.DMA,
+            pltpu.VMEM((3 * HD, 2 * D), bf16),
+            pltpu.VMEM((D, STRETCH), bf16),
+            pltpu.VMEM((D, STRETCH), bf16),
+            pltpu.VMEM((3 * HD, STRETCH), f32),
+            dma((2,)),
         ],
         compiler_params=pltpu.CompilerParams(
-            collective_id=1, has_side_effects=True, vmem_limit_bytes=40 * 2**20
+            collective_id=1, has_side_effects=True, vmem_limit_bytes=56 * 2**20
         ),
         name="mix_rows",
-    )(gated, squares, weight, hidden)
+    )(gated, squares, weight, hidden, gain_sh, w_att, embed_all, embed_sq)
 
 
 def merge_kernel(attended, weight, before, out,
@@ -462,33 +679,42 @@
     )(attended, weight, before)
 
 
-def attend_kernel(table, length, queries, keys_new, values_new, pool, out, held, sems, acc, top, total):
-    scale = HD ** -0.5
+def turn(value):
+    return jnp.concatenate([value, jnp.zeros((256 - HD, STRETCH), f32)], axis=0).T[:, :HD]
+
+
+def attend_kernel(table, lengths, projected, pool, out, held, sems, acc, top, total):
+    seq = lax.axis_index("seq")
+    scale = HD ** -0.5 * 1.4426950408889634
     span = STEPB * BLOCK
-    limit = length[0]
+    limit = lengths[seq]
     blocks = lax.div(limit + BLOCK - 1, BLOCK)
     steps = lax.div(blocks + STEPB - 1, STEPB)
 
     def fetch(step, slot):
         return [
             pltpu.make_async_copy(
-                pool.at[table[step * STEPB + i]], held.at[slot, i], sems.at[slot, i]
+                pool.at[table[seq, step * STEPB + i]],
+                held.at[slot, :, :, pl.ds(i * BLOCK, BLOCK)],
+                sems.at[slot, i],
             )
             for i in range(STEPB)
         ]
 
     for copy in fetch(0, 0):
         copy.start()
-    q = queries[...]
-    scores = lax.dot_general(q, keys_new[...], (((1,), (0,)), ((), ())), preferred_element_type=f32)
+    q = turn(projected[:HD, :].astype(f32)).astype(bf16)
+    scores = jnp.dot(q, projected[HD : 2 * HD, :], preferred_element_type=f32)
     row = lax.broadcasted_iota(jnp.int32, scores.shape, 0)
     col = lax.broadcasted_iota(jnp.int32, scores.shape, 1)
     scores = jnp.where(row >= col, scores, masked)
     high = jnp.max(scores, axis=1, keepdims=True)
-    weights = jnp.exp((scores - high) * scale)
+    weights = jnp.exp2((scores - high) * scale)
     top[...] = high
     total[...] = jnp.sum(weights, axis=1, keepdims=True)
-    acc[...] = jnp.dot(weights.astype(bf16), values_new[...], preferred_element_type=f32)
+    acc[...] = lax.dot_general(
+        weights.astype(bf16), projected[2 * HD :, :], NT, preferred_element_type=f32
+    )
 
     def step_body(step, _):
         slot = lax.rem(step, 2)
@@ -500,19 +726,17 @@
 
         for copy in fetch(step, slot):
             copy.wait()
-        keys = held[slot, :, 0].reshape(span, HD)
-        values = held[slot, :, 1].reshape(span, HD)
-        scores = lax.dot_general(q, keys, (((1,), (1,)), ((), ())), preferred_element_type=f32)
+        scores = jnp.dot(q, held[slot, 0], preferred_element_type=f32)
 
         def rest(scores):
             old = top[...]
             high = jnp.maximum(old, jnp.max(scores, axis=1, keepdims=True))
-            weights = jnp.exp((scores - high) * scale)
-            factor = jnp.exp((old - high) * scale)
+            weights = jnp.exp2((scores - high) * scale)
+            factor = jnp.exp2((old - high) * scale)
             top[...] = high
             total[...] = total[...] * factor + jnp.sum(weights, axis=1, keepdims=True)
-            acc[...] = acc[...] * factor + jnp.dot(
-                weights.astype(bf16), values, preferred_element_type=f32
+            acc[...] = acc[...] * factor + lax.dot_general(
+                weights.astype(bf16), held[slot, 1], NT, preferred_element_type=f32
             )
 
         @pl.when((step + 1) * span <= limit)
@@ -527,19 +751,21 @@
         return 0
 
     lax.fori_loop(0, steps, step_body, 0)
-    out[...] = (acc[...] / total[...]).astype(bf16)
-
-
-def attend_call(table, length, queries, keys_new, values_new, pool):
+    value = acc[...] / total[...]
+    value = jnp.concatenate([value, jnp.zeros((STRETCH, 256 - HD), f32)], axis=1).T
+    out[...] = value[:HD].astype(bf16)
+
+
+def attend_call(table, lengths, projected, pool):
     vmem = pl.BlockSpec(memory_space=pltpu.VMEM)
     smem = pl.BlockSpec(memory_space=pltpu.SMEM)
     return pl.pallas_call(
         attend_kernel,
-        out_shape=jax.ShapeDtypeStruct((STRETCH, HD), bf16),
-        in_specs=[smem, smem, vmem, vmem, vmem, pl.BlockSpec(memory_space=pl.ANY)],
+        out_shape=jax.ShapeDtypeStruct((HD, STRETCH), bf16),
+        in_specs=[smem, smem, vmem, pl.BlockSpec(memory_space=pl.ANY)],
         out_specs=vmem,
         scratch_shapes=[
-            pltpu.VMEM((2, STEPB, 2, BLOCK, HD), bf16),
+            pltpu.VMEM((2, 2, HD, STEPB * BLOCK), bf16),
             pltpu.SemaphoreType.DMA((2, STEPB)),
             pltpu.VMEM((STRETCH, HD), f32),
             pltpu.VMEM((STRETCH, 1), f32),
@@ -547,102 +773,27 @@
         ],
         compiler_params=pltpu.CompilerParams(vmem_limit_bytes=48 * 2**20),
         name="attend_rows",
-    )(table, length, queries, keys_new, values_new, pool)
-
-
-def shift_rows(matrix, by):
-    if by == 0:
-        return matrix
-    return jnp.concatenate([jnp.zeros((by, matrix.shape[1]), f32), matrix[:-by]], axis=0)
-
-
-def state_block(activated, step_sizes, cumulative, b_proj, c_proj, init_state, skip_gain):
-    length = activated.shape[0]
-    positions = jnp.arange(length)
-    causal = (positions[:, None] >= positions[None, :])[None]
-    cums_heads = cumulative.T
-    gaps = cums_heads[:, :, None] - cums_heads[:, None, :]
-    decays = jnp.where(causal, jnp.exp(jnp.where(causal, gaps, 0.0)), 0.0)
-    product = jnp.einsum("tn,sn->ts", c_proj, b_proj, precision=highest)
-    weighted = decays * product[None] * step_sizes.T[:, None, :]
-    within = jnp.einsum("hts,shp->thp", weighted, activated, precision=highest)
-    carried = (
-        jnp.einsum("tn,hpn->thp", c_proj, init_state, precision=highest)
-        * jnp.exp(cumulative)[:, :, None]
-    )
-    output = within + carried + skip_gain[None, :, None] * activated
-    to_end = jnp.exp(cumulative[-1][None, :] - cumulative) * step_sizes
-    final_state = jnp.exp(cumulative[-1])[:, None, None] * init_state + jnp.einsum(
-        "shp,sn->hpn", activated * to_end[:, :, None], b_proj, precision=highest
-    )
-    return (output, final_state)
+    )(table, lengths, projected, pool)
 
 
 def body(hidden, embedding, input_gain, w_input, w_groups, w_step, step_bias, decay_rate, skip_gain,
          conv_weight, mix_gain, w_output, state_store, conv_store, state_slot, prefix_len, block_table,
          shared_gain, w_attend, cache_pool, w_merge):
     heads_local = w_step.shape[1]
-    my_head = lax.axis_index("head")
-    my_seq = lax.axis_index("seq")
-    group_id = my_head * heads_local // (MH // G)
-    pool = lax.all_gather(cache_pool, "seq", axis=0, tiled=True)
-
+    pool = lax.all_gather(cache_pool.transpose(0, 1, 3, 2), "seq", axis=0, tiled=True)
     rows = state_store.shape[0]
-    tails = conv_store.astype(f32).reshape(rows, 6, 128)
-    packed = jnp.concatenate(
-        [state_store.reshape(rows, 128, 128), tails, jnp.zeros((rows, PACK - 134, 128), f32)], axis=1
+    tails = jnp.pad(conv_store.astype(f32).reshape(rows, 6, 128), ((0, 0), (0, 2), (0, 0)))
+    hidden_t = hidden.T
+    gain_sh = shared_gain.reshape(2 * D // 128, 128)
+    gained, squares, final_state, embed_all, embed_sq = scan_call(
+        hidden_t, embedding.T, input_gain.reshape(D // 128, 128), gain_sh, state_store, tails, state_slot,
+        w_input, w_groups, w_step.T, step_bias, decay_rate, skip_gain, conv_weight, mix_gain[None, :],
     )
-    hidden_t = hidden.T
-    hidden_all, embed_all, packed_all = gather_call(hidden_t, embedding.T, packed)
-    held = lax.dynamic_index_in_dim(
-        packed_all.reshape(SEQ * rows, PACK, 128), state_slot[my_seq], 0, keepdims=False
+    hidden_next, projected = mix_call(
+        gained, squares, w_output, hidden_t, gain_sh, w_attend.T, embed_all, embed_sq
     )
-    init_state = held[:128].reshape(heads_local, P_SIZE, NS)
-    conv_tail = held[128:134].reshape(CONV - 1, heads_local * P_SIZE)
-
-    wide = hidden_all.astype(f32)
-    mean = jnp.mean(wide * wide, axis=0, keepdims=True)
-    normed = (wide * lax.rsqrt(mean + epsilon) * input_gain[:, None]).astype(bf16)
-    over = (((0,), (0,)), ((), ()))
-    paired = lax.dot_general(normed, w_input, over, preferred_element_type=f32).reshape(
-        STRETCH, heads_local, 2, P_SIZE
-    )
-    gate_part = paired[:, :, 0]
-    signal = paired[:, :, 1].reshape(STRETCH, heads_local * P_SIZE)
-    grouped = lax.dot_general(normed, w_groups, over, preferred_element_type=f32)
-    b_proj = lax.dynamic_slice_in_dim(grouped, group_id * NS, NS, 1)
-    c_proj = lax.dynamic_slice_in_dim(grouped, (G + group_id) * NS, NS, 1)
-    raw_steps = lax.dot_general(normed, w_step, over, preferred_element_type=f32)
-    padded = jnp.concatenate([conv_tail, signal], axis=0)
-    convolved = sum(conv_weight[k] * padded[k : k + STRETCH] for k in range(CONV))
-    activated = jax.nn.silu(convolved).reshape(STRETCH, heads_local, P_SIZE)
-    step_sizes = jax.nn.softplus(raw_steps + step_bias)
-    cumulative = jnp.cumsum(-decay_rate * step_sizes, axis=0)
-    scanned, final_state = state_block(
-        activated, step_sizes, cumulative, b_proj, c_proj, init_state, skip_gain
-    )
-    gated = scanned * jax.nn.silu(gate_part)
-    squares = jnp.sum(gated * gated, axis=(1, 2))
-    gained = (gated.reshape(STRETCH, heads_local * P_SIZE) * mix_gain).T
-    hidden_next, residual_all = mix_call(
-        gained, jnp.broadcast_to(squares[None, :], (8, STRETCH)), w_output, hidden_t
-    )
-
-    res = residual_all.astype(f32)
-    emb = embed_all.astype(f32)
-    mean = (jnp.sum(res * res, axis=0) + jnp.sum(emb * emb, axis=0)) / (2 * D)
-    scale = lax.rsqrt(mean + epsilon)[None, :]
-    res = (res * scale * shared_gain[:D, None]).astype(bf16)
-    emb = (emb * scale * shared_gain[D:, None]).astype(bf16)
-    projected = (
-        lax.dot_general(w_attend[:D], res, over, preferred_element_type=f32)
-        + lax.dot_general(w_attend[D:], emb, over, preferred_element_type=f32)
-    ).astype(bf16)
-    attended = attend_call(
-        block_table[my_seq], prefix_len[my_seq][None],
-        projected[:HD].T, projected[HD : 2 * HD], projected[2 * HD :].T, pool,
-    )
-    layer_output = merge_call(attended.T, w_merge, hidden_next)
+    attended = attend_call(block_table, prefix_len, projected, pool)
+    layer_output = merge_call(attended, w_merge, hidden_next)
     return (layer_output.T, final_state.reshape(1, heads_local, P_SIZE * NS))
 
 

time: 238 us -> 180 us (0.76)
  the two profiles are of different devices: /device:TPU:2 before, /device:TPU:0 now
where the time goes in v2:
time: 180 us; the launch traced here: 178 us
  Pallas kernels  148 us (82%)
  local copies, waits for them, and re-layouts  15.8 us (9%)
  between operations  14.1 us (8%)
    pallas_call x1, Pallas kernels, mix_call(): pl.pallas_call(mix_kernel, out_shape=(jax.ShapeDtypeStruct((SHARD, STRETC...  60 us
    pallas_call x1, Pallas kernels, scan_call(): pl.pallas_call(scan_kernel, out_shape=(jax.ShapeDtypeStruct((HL * P_SIZE,...  55.3 us
    pallas_call x1, Pallas kernels, merge_call(): pl.pallas_call(merge_kernel, out_shape=jax.ShapeDtypeStruct((SHARD, STRET...  28.6 us
    unnamed x44, local copies, waits for them, and re-layouts  15 us
    pallas_call x1, Pallas kernels, attend_call(): pl.pallas_call(attend_kernel, out_shape=jax.ShapeDtypeStruct((HD, STRETCH...  3.8 us
  transfers between devices with their start and end apart: 1, of which 0 were waited for; matrix products, arithmetic and copies ran while one was open for 1% of the time, Pallas kernels for 65%

profile of v2, /device:TPU:0, one launch (start us, length us, event | category | flops | bytes accessed | tf_op | source)
XLA Modules:
  0.0 178.3 jit_solution(3293236554976682691)
XLA Ops:
  7.2 0.0 all-gather.2.cloned.1.call-start
  7.2 0.7 all-gather.2.cloned.1.call-update
  7.9 0.7 copy.25
  8.6 1.5 copy-done
  10.1 0.9 copy-done.2
  11.1 0.9 copy-done.6
  12.0 0.9 copy-done.7
  12.9 0.7 copy-done.8
  13.6 0.7 copy-done.9
  14.4 0.7 copy-done.10
  15.1 0.7 copy-done.14
  15.8 0.7 copy-done.15
  16.5 0.7 copy-done.17
  17.1 0.7 copy-done.18
  17.8 0.7 copy-done.19
  18.4 0.7 copy-done.20
  19.1 55.3 %scan_rows.1 = (f32[256,512]{1,0:T(8,128)S(1)}, f32[8,512]{1,0:T(8,128)S(1)}, f32[256,64]{1,0:T(8,128)S(1)}, bf16[3584,512]{1,0:T(8,128)(2,1)}, f32[8,512]{1,0:T(8,128)S(1)}) custom-call(bf16[224,512]{1,0:T(8,128)(2,1)S(1)} %bitcast.11, bf16[224,512]{1,0:T(8,128)(2,1)S(1)} %bitcast.12, f32[28,128]{1,0:T(8,128)S(1)} %bitcast.16, f32[56,128]{1,0:T(8,128)S(1)} %bitcast.14, ...), custom_call_target="tpu_custom_call" | custom-call | tf_op jit(solution)/shard_map/scan_rows/pallas_call | solution.py:487
  74.4 0.0 copy-start.4
  74.4 0.8 copy-done.4
  75.2 0.6 copy-done.11
  75.8 0.6 copy-done.12
  76.4 0.7 reshape.20
  77.1 60.0 %mix_rows.1 = (f32[224,512]{1,0:T(8,128)}, bf16[672,512]{1,0:T(8,128)(2,1)}) custom-call(f32[256,512]{1,0:T(8,128)} %copy-done.4, f32[8,512]{1,0:T(8,128)} %copy-done.11, bf16[256,3584]{1,0:T(8,128)(2,1)} %weight.2, bf16[224,512]{1,0:T(8,128)(2,1)} %bitcast.10, f32[56,128]{1,0:T(8,128)} %bitcast.13, bf16[672,7168]{1,0:T(8,128)(2,1)} %bitcast.18, ...), custom_call_target="tpu_custom_call" | custom-call | tf_op jit(solution)/shard_map/mix_rows/pallas_call | solution.py:624
  137.1 0.0 all-gather.2.cloned.1.call-done.pool
  137.2 0.0 copy-done.13
  137.2 0.0 copy-done.16
  137.2 1.1 copy-done.3
  138.3 3.8 %attend_rows.1.attended = bf16[224,512]{1,0:T(8,128)(2,1)S(1)} custom-call(s32[8,64]{1,0:T(8,128)S(1)} %copy-done.13, s32[8]{0:T(128)S(1)} %copy-done.16, bf16[672,512]{1,0:T(8,128)(2,1)S(1)} %copy-done.3, bf16[160,2,224,128]{3,2,1,0:T(8,128)(2,1)} %all-gather.2.cloned.1.call-done.pool), custom_call_target="tpu_custom_call" | custom-call | tf_op jit(solution)/shard_map/attend_rows/pallas_call | solution.py:762
  142.1 0.0 copy-done.1
  142.1 0.0 copy-done.5
  142.1 28.6 %merge_rows.1 = f32[224,512]{1,0:T(8,128)S(1)} custom-call(bf16[224,512]{1,0:T(8,128)(2,1)S(1)} %attend_rows.1.attended, bf16[224,3584]{1,0:T(8,128)(2,1)S(1)} %copy-done.1, f32[224,512]{1,0:T(8,128)S(1)} %copy-done.5), custom_call_target="tpu_custom_call" | custom-call | tf_op jit(solution)/shard_map/merge_rows/pallas_call | solution.py:669
  170.7 0.8 copy.27
  (22 shorter events, 0.1 us)
Async XLA Ops:
  7.2 130.0 %all-gather.2.cloned.1.call-start = ((), (), s32[]{:S(2)}) async-start(), calls=%async_computation | async-start | bytes 20643840 | tf_op jit(solution)/shard_map/all_gather | solution.py:783
  8.6 1.5 copy-start
  10.1 0.9 copy-start.2
  11.1 0.9 copy-start.6
  12.0 0.9 copy-start.7
  12.9 0.7 copy-start.8
  13.6 0.7 copy-start.9
  14.4 0.7 copy-start.10
  15.1 0.7 copy-start.14
  15.8 0.7 copy-start.15
  16.5 0.7 copy-start.17
  17.1 0.7 copy-start.18
  17.8 0.7 copy-start.19
  18.4 0.7 copy-start.20
  74.4 0.8 copy-start.4
  75.2 0.6 copy-start.11
  75.8 0.6 copy-start.12
  77.1 60.1 %copy-start.13 = (s32[8,64]{1,0:T(8,128)S(1)}, s32[8,64]{1,0:T(8,128)}, u32[]{:S(2)}) copy-start(s32[8,64]{1,0:T(8,128)} %table.1) | copy-start | bytes 6148
  77.1 60.1 %copy-start.16 = (s32[8]{0:T(128)S(1)}, s32[8]{0:T(128)}, u32[]{:S(2)}) copy-start(s32[8]{0:T(128)} %lengths.1) | copy-start | bytes 100
  137.2 1.1 copy-start.3
  138.3 3.8 %copy-start.1 = (bf16[224,3584]{1,0:T(8,128)(2,1)S(1)}, bf16[224,3584]{1,0:T(8,128)(2,1)}, u32[]{:S(2)}) copy-start(bf16[224,3584]{1,0:T(8,128)(2,1)} %weight.3) | copy-start | bytes 4816900
  138.3 3.8 %copy-start.5 = (f32[224,512]{1,0:T(8,128)S(1)}, f32[224,512]{1,0:T(8,128)}, u32[]{:S(2)}) copy-start(f32[224,512]{1,0:T(8,128)} %get-tuple-element.14.before) | copy-start | bytes 1376260
Sparse Core Ops, SparseCore 0:
  9.7 105.9 all-gather.1

commit v3 on v2

--- a/solution.py
+++ b/solution.py
@@ -319,204 +319,6 @@
 TN = (((0,), (0,)), ((), ()))
 NT = (((1,), (1,)), ((), ()))
 HL = 4
-
-
-def scan_kernel(hidden, embed, gain_in, gain_sh, states, tails, slots, w_in, w_gr, w_st, bias, decay, skip,
-                conv_w, mix_g, gained_out, squares_out, final_out, embed_all, embed_sq,
-                wide, own_h, own_e, win, wgr, paired, grouped, sums, peers, stores, tail_all, lines,
-                h_send, h_recv, e_send, e_recv, q_send, q_recv, s_send, s_recv, t_send, t_recv, local):
-    seq = lax.axis_index("seq")
-    me = lax.axis_index("head")
-    loads = [
-        pltpu.make_async_copy(w_in, win, local.at[0]),
-        pltpu.make_async_copy(w_gr, wgr, local.at[1]),
-        pltpu.make_async_copy(states, stores.at[pl.ds(seq * 2, 2)], local.at[2]),
-        pltpu.make_async_copy(tails, tail_all.at[pl.ds(seq * 2, 2)], local.at[3]),
-    ]
-    for copy in loads:
-        copy.start()
-    barrier = greet_heads()
-    for by in range(1, SEQ):
-        pl.semaphore_signal(
-            barrier, inc=1, device_id={"seq": lax.rem(seq + by, SEQ)}, device_id_type=MESH
-        )
-    mine = pl.ds(pl.multiple_of(me * SHARD, 16), SHARD)
-    value = hidden[...].astype(f32)
-    sq_h = jnp.sum(value * value, axis=0, keepdims=True)
-    ready = (value * column(gain_in, me * SHARD, SHARD)).astype(bf16)
-    own_h[...] = ready
-    wide[mine, :] = ready
-    pl.semaphore_wait(barrier, HEADS - 1 + SEQ - 1)
-    first = Gather(own_h, wide, h_send, h_recv)
-    second = Gather(own_e, embed_all, e_send, e_recv)
-    first.start()
-    value = embed[...].astype(f32)
-    sq_e = jnp.sum(value * value, axis=0, keepdims=True)
-    own_e[...] = (value * column(gain_sh, D + me * SHARD, SHARD)).astype(bf16)
-    line = lax.broadcasted_iota(jnp.int32, (8, STRETCH), 0)
-    sums[...] = jnp.where(line == 0, sq_h, jnp.where(line == 1, sq_e, 0.0))
-    out = send_sums(sums, peers, q_send, q_recv)
-    kept = pltpu.make_async_copy(own_e, embed_all.at[mine, FULL], local.at[4])
-    kept.start()
-    moved = []
-    for by in range(1, SEQ):
-        to = {"seq": lax.rem(seq + by, SEQ)}
-        for src, dst, ss, rs in ((states, stores, s_send, s_recv), (tails, tail_all, t_send, t_recv)):
-            copy = pltpu.make_async_remote_copy(
-                src_ref=src, dst_ref=dst.at[pl.ds(seq * 2, 2)], send_sem=ss.at[by - 1], recv_sem=rs.at[by - 1],
-                device_id=to, device_id_type=MESH,
-            )
-            copy.start()
-            moved.append(copy)
-    first.first_near()
-    first.second_near(0)
-    first.first_far()
-    for k in (1, 2, 3):
-        first.second_near(k)
-    second.start()
-    for k in range(SIDE):
-        first.second_far(k)
-    total = add_sums(sums, peers, out)
-    embed_sq[...] = total
-    scale = lax.rsqrt(total[0:1, :] * (1.0 / D) + epsilon)
-    for copy in loads:
-        copy.wait()
-
-    def project(i, _):
-        span = pl.ds(pl.multiple_of(i * 256, 256), 256)
-        paired[span, :] = scale * lax.dot_general(win[:, span], wide[...], TN, preferred_element_type=f32)
-        return 0
-
-    lax.fori_loop(0, 2, project, 0)
-    second.first_near()
-    grouped[...] = scale * lax.dot_general(wgr[...], wide[...], TN, preferred_element_type=f32)
-    raw = scale * jnp.dot(w_st[...], wide[...], preferred_element_type=f32)
-    second.second_near(0)
-    second.first_far()
-    head = lax.broadcasted_iota(jnp.int32, (HL, STRETCH), 0)
-
-    def by_head(ref):
-        line = jnp.zeros((HL, STRETCH), f32)
-        for i in range(HL):
-            line = jnp.where(head == i, ref[i], line)
-        return line
-
-    raw = raw + by_head(bias)
-    steps = jnp.maximum(raw, 0.0) + jnp.log1p(jnp.exp(-jnp.abs(raw)))
-    cums = -by_head(decay) * steps
-    lane = lax.broadcasted_iota(jnp.int32, (HL, STRETCH), 1)
-    by = 1
-    while by < STRETCH:
-        cums = cums + jnp.where(lane >= by, pltpu.roll(cums, by, 1), 0.0)
-        by *= 2
-    turned = jnp.concatenate([cums, steps, jnp.zeros((128 - 2 * HL, STRETCH), f32)], axis=0).T
-    group = lax.div(me, 8)
-    b_proj = grouped[pl.ds(pl.multiple_of(group * NS, NS), NS), :]
-    c_proj = grouped[pl.ds(pl.multiple_of(G * NS + group * NS, NS), NS), :]
-    pairs = lax.dot_general(b_proj.astype(bf16), c_proj.astype(bf16), TN, preferred_element_type=f32)
-    src = lax.broadcasted_iota(jnp.int32, pairs.shape, 0)
-    dst = lax.broadcasted_iota(jnp.int32, pairs.shape, 1)
-    pairs = jnp.where(src <= dst, pairs, 0.0)
-
-    for copy in moved:
-        copy.wait_recv()
-    slot = slots[seq]
-    for h in range(HL):
-        for i in range(32):
-            lines[pl.ds(h * 32 + i, 1), :] = stores[slot, h : h + 1, i * 128 : (i + 1) * 128]
-    p_row = lax.broadcasted_iota(jnp.int32, (P_SIZE, 32), 0)
-    p_col = lax.broadcasted_iota(jnp.int32, (P_SIZE, 32), 1)
-    even = (p_row == 2 * p_col).astype(f32)
-    odd = (p_row == 2 * p_col + 1).astype(f32)
-    tail = tail_all[slot]
-    t_row = lax.broadcasted_iota(jnp.int32, (8, 128), 0)
-    t_col = lax.broadcasted_iota(jnp.int32, (8, 128), 1)
-    before = []
-    for j in range(2):
-        pick = jnp.zeros((8, 128), f32)
-        for k in range(CONV - 1):
-            pick = jnp.where((t_row == 2 * k + j) & (t_col == 125 + k), 1.0, pick)
-        before.append(lax.dot_general(tail, pick, TN, precision=highest, preferred_element_type=f32))
-    taps = [flat(conv_w[k : k + 1, :], HL * P_SIZE) for k in range(CONV)]
-    mixing = flat(mix_g[...], HL * P_SIZE)
-    squares = jnp.zeros((1, STRETCH), f32)
-    for h in range(HL):
-        chan = slice(h * P_SIZE, (h + 1) * P_SIZE)
-        gate = paired[h * 128 : h * 128 + 64, :]
-        signal = paired[h * 128 + 64 : h * 128 + 128, :]
-        half = (h % 2) * P_SIZE
-        padded = jnp.concatenate([before[h // 2][half : half + P_SIZE], signal], axis=1)
-        conv = taps[CONV - 1][chan] * signal
-        for back in range(1, CONV):
-            conv = conv + taps[CONV - 1 - back][chan] * pltpu.roll(padded, back, 1)[:, 128:]
-        active = silu(conv)
-        cum = cums[h : h + 1, :]
-        step = steps[h : h + 1, :]
-        mix = jnp.exp(jnp.minimum(cum - turned[:, h : h + 1], 0.0)) * pairs * turned[:, HL + h : HL + h + 1]
-        within = jnp.dot(active.astype(bf16), mix.astype(bf16), preferred_element_type=f32)
-        rows = lines[h * 32 : (h + 1) * 32, :]
-        init = jnp.dot(even, rows[:, :NS], precision=highest, preferred_element_type=f32)
-        init = init + jnp.dot(odd, rows[:, NS:], precision=highest, preferred_element_type=f32)
-        carried = jnp.dot(init, c_proj, precision=highest, preferred_element_type=f32) * jnp.exp(cum)
-        gated = (within + carried + skip[h] * active) * silu(gate)
-        squares = squares + jnp.sum(gated * gated, axis=0, keepdims=True)
-        gained_out[chan, :] = gated * mixing[chan]
-        last = cum[:, STRETCH - 1 :]
-        to_end = jnp.exp(last - cum) * step
-        final_out[chan, :] = jnp.exp(last) * init + lax.dot_general(
-            active * to_end, b_proj, NT, precision=highest, preferred_element_type=f32
-        )
-        if h:
-            second.second_near(h)
-    squares_out[...] = jnp.broadcast_to(squares, (8, STRETCH))
-    for k in range(SIDE):
-        second.second_far(k)
-    first.finish()
-    second.finish()
-    for copy in out + moved:
-        copy.wait_send()
-    kept.wait()
-
-
-def scan_call(hidden, embed, gain_in, gain_sh, states, tails, slots, w_in, w_gr, w_st, bias, decay, skip,
-              conv_w, mix_g):
-    anywhere = pl.BlockSpec(memory_space=pl.ANY)
-    vmem = pl.BlockSpec(memory_space=pltpu.VMEM)
-    smem = pl.BlockSpec(memory_space=pltpu.SMEM)
-    dma = pltpu.SemaphoreType.DMA
-    return pl.pallas_call(
-        scan_kernel,
-        out_shape=(
-            jax.ShapeDtypeStruct((HL * P_SIZE, STRETCH), f32),
-            jax.ShapeDtypeStruct((8, STRETCH), f32),
-            jax.ShapeDtypeStruct((HL * P_SIZE, NS), f32),
-            jax.ShapeDtypeStruct((D, STRETCH), bf16),
-            jax.ShapeDtypeStruct((8, STRETCH), f32),
-        ),
-        in_specs=[vmem] * 4 + [anywhere] * 2 + [smem] + [anywhere] * 2 + [vmem] + [smem] * 3 + [vmem] * 2,
-        out_specs=(vmem, vmem, vmem, anywhere, vmem),
-        scratch_shapes=[
-            pltpu.VMEM((D, STRETCH), bf16),
-            pltpu.VMEM((SHARD, STRETCH), bf16),
-            pltpu.VMEM((SHARD, STRETCH), bf16),
-            pltpu.VMEM((D, HL * 128), bf16),
-            pltpu.VMEM((D, 2 * G * NS), bf16),
-            pltpu.VMEM((HL * 128, STRETCH), f32),
-            pltpu.VMEM((2 * G * NS, STRETCH), f32),
-            pltpu.VMEM((8, STRETCH), f32),
-            pltpu.VMEM((HEADS - 1, 8, STRETCH), f32),
-            pltpu.VMEM((2 * SEQ, HL, P_SIZE * NS), f32),
-            pltpu.VMEM((2 * SEQ, 8, 128), f32),
-            pltpu.VMEM((128, 128), f32),
-        ] + GATHER_SEMS + GATHER_SEMS + [
-            dma((HEADS - 1,)), dma((HEADS - 1,)), dma((SEQ - 1,)), dma((SEQ - 1,)),
-            dma((SEQ - 1,)), dma((SEQ - 1,)), dma((5,)),
-        ],
-        compiler_params=pltpu.CompilerParams(
-            collective_id=0, has_side_effects=True, vmem_limit_bytes=48 * 2**20
-        ),
-        name="scan_rows",
-    )(hidden, embed, gain_in, gain_sh, states, tails, slots, w_in, w_gr, w_st, bias, decay, skip, conv_w, mix_g)
 
 
 def products(weight, rows, part):
@@ -651,6 +453,381 @@
     )(gated, squares, weight, hidden, gain_sh, w_att, embed_all, embed_sq)
 
 
+CHUNKS = 4
+BLOCKS = 20
+
+
+class Pool:
+    def __init__(self, own, out, send_sems, recv_sems):
+        self.own, self.out, self.ss, self.rs = own, out, send_sems, recv_sems
+        seq = lax.axis_index("seq")
+        self.x, self.core = lax.div(seq, 2), lax.rem(seq, 2)
+        self.sent = []
+
+    def slab(self, by, core, ch):
+        per = BLOCKS // CHUNKS
+        return self.out.at[pl.ds((around(self.x, by) * 2 + core) * BLOCKS + ch * per, per)]
+
+    def copy(self, idx, src, dst, by, core):
+        return pltpu.make_async_remote_copy(
+            src_ref=src, dst_ref=dst, send_sem=self.ss.at[idx], recv_sem=self.rs.at[idx],
+            device_id={"seq": around(self.x, by) * 2 + core}, device_id_type=MESH,
+        )
+
+    def go(self, idx, src, dst, by, core):
+        copy = self.copy(idx, src, dst, by, core)
+        copy.start()
+        self.sent.append(copy)
+
+    def arrive(self, idx, dst):
+        self.copy(idx, dst, dst, 1, self.core).wait_recv()
+
+    def start(self):
+        per = BLOCKS // CHUNKS
+        for near, far in ((0, 2), (1, 3), (2, 0), (3, 1)):
+            for base, ch, by in ((0, near, 1), (4, far, -1)):
+                self.go(base + ch, self.own.at[pl.ds(ch * per, per)], self.slab(0, self.core, ch), by, self.core)
+        for ch in range(CHUNKS):
+            self.go(12 + ch, self.own.at[pl.ds(ch * per, per)], self.slab(0, self.core, ch), 0, 1 - self.core)
+
+    def share(self, j, by, ch):
+        where = self.slab(by, self.core, ch)
+        self.go(12 + 4 * j + ch, where, where, 0, 1 - self.core)
+
+    def relay(self, ch):
+        left = self.slab(-1, self.core, ch)
+        right = self.slab(1, self.core, ch)
+        if ch < 2:
+            self.arrive(ch, left)
+            self.go(8 + ch, left, left, 1, self.core)
+            self.share(1, -1, ch)
+        else:
+            self.arrive(4 + ch, right)
+            self.go(8 + ch, right, right, -1, self.core)
+            self.share(2, 1, ch)
+
+    def rest(self, ch):
+        if ch < 2:
+            self.arrive(4 + ch, self.slab(1, self.core, ch))
+            self.share(2, 1, ch)
+        else:
+            self.arrive(ch, self.slab(-1, self.core, ch))
+            self.share(1, -1, ch)
+
+    def far(self, ch):
+        self.arrive(8 + ch, self.slab(2, self.core, ch))
+        self.share(3, 2, ch)
+
+    def finish(self):
+        for j, by in enumerate((0, -1, 1, 2)):
+            for ch in range(CHUNKS):
+                self.arrive(12 + 4 * j + ch, self.slab(by, 1 - self.core, ch))
+        for copy in self.sent:
+            copy.wait_send()
+
+
+def front_kernel(hidden_in, embed_in, gain_in_in, gain_sh_in, states, tails, slots, w_in, w_gr, w_st, bias, decay,
+                 skip, conv_in, mix_in, w_out_in, w_att, pool_in,
+                 next_out, proj_out, final_out, pool_out,
+                 hidden, embed, gain_in, gain_sh, conv_w, mix_g, weight,
+                 wide, own_h, own_e, win, wgr, paired, grouped, sums, peers, stores, tail_all, lines, gained, watt,
+                 emb, wide2, acc, squares, peers3, sums2, peers2, rounded,
+                 part, near1, full1, mid, near2, full2, x_send, x_recv,
+                 h_send, h_recv, e_send, e_recv, g_send, g_recv, q_send, q_recv, s_send, s_recv, t_send, t_recv,
+                 u_send, u_recv, r_send, r_recv, p_send, p_recv, local, here):
+    seq = lax.axis_index("seq")
+    me = lax.axis_index("head")
+    small = [
+        pltpu.make_async_copy(src, dst, here.at[i])
+        for i, (src, dst) in enumerate((
+            (hidden_in, hidden), (gain_in_in, gain_in), (embed_in, embed), (gain_sh_in, gain_sh),
+            (conv_in, conv_w), (mix_in, mix_g), (w_out_in, weight),
+        ))
+    ]
+    for copy in small:
+        copy.start()
+    loads = [
+        pltpu.make_async_copy(w_in, win, local.at[0]),
+        pltpu.make_async_copy(w_gr, wgr, local.at[1]),
+        pltpu.make_async_copy(states, stores.at[pl.ds(seq * 2, 2)], local.at[2]),
+        pltpu.make_async_copy(tails, tail_all.at[seq], local.at[3]),
+        pltpu.make_async_copy(w_att, watt, local.at[4]),
+        pltpu.make_async_copy(pool_in, pool_out.at[pl.ds(seq * BLOCKS, BLOCKS)], local.at[5]),
+    ]
+    for copy in loads:
+        copy.start()
+    barrier = greet_heads()
+    for by in range(1, SEQ):
+        pl.semaphore_signal(
+            barrier, inc=1, device_id={"seq": lax.rem(seq + by, SEQ)}, device_id_type=MESH
+        )
+    mine = pl.ds(pl.multiple_of(me * SHARD, 16), SHARD)
+    small[0].wait()
+    small[1].wait()
+    value = hidden[...].astype(f32)
+    sq_h = jnp.sum(value * value, axis=0, keepdims=True)
+    ready = (value * column(gain_in, me * SHARD, SHARD)).astype(bf16)
+    own_h[...] = ready
+    wide[mine, :] = ready
+    pl.semaphore_wait(barrier, HEADS - 1 + SEQ - 1)
+    first = Gather(own_h, wide, h_send, h_recv)
+    second = Gather(own_e, emb, e_send, e_recv)
+    blocks = Pool(pool_in, pool_out, p_send, p_recv)
+    first.start()
+    for copy in small[2:]:
+        copy.wait()
+    value = embed[...].astype(f32)
+    sq_e = jnp.sum(value * value, axis=0, keepdims=True)
+    ready = (value * column(gain_sh, D + me * SHARD, SHARD)).astype(bf16)
+    own_e[...] = ready
+    emb[mine, :] = ready
+    line = lax.broadcasted_iota(jnp.int32, (8, STRETCH), 0)
+    sums[...] = jnp.where(line == 0, sq_h, jnp.where(line == 1, sq_e, 0.0))
+    out = send_sums(sums, peers, q_send, q_recv)
+    moved = []
+    for by in range(1, SEQ):
+        to = {"seq": lax.rem(seq + by, SEQ)}
+        for src, dst, ss, rs in (
+            (states, stores.at[pl.ds(seq * 2, 2)], s_send, s_recv), (tails, tail_all.at[seq], t_send, t_recv)
+        ):
+            copy = pltpu.make_async_remote_copy(
+                src_ref=src, dst_ref=dst, send_sem=ss.at[by - 1], recv_sem=rs.at[by - 1],
+                device_id=to, device_id_type=MESH,
+            )
+            copy.start()
+            moved.append(copy)
+    first.first_near()
+    blocks.start()
+    first.second_near(0)
+    first.first_far()
+    for k in (1, 2, 3):
+        first.second_near(k)
+    second.start()
+    for k in range(SIDE):
+        first.second_far(k)
+    total = add_sums(sums, peers, out)
+    embed_sq = total[1:2, :]
+    scale = lax.rsqrt(total[0:1, :] * (1.0 / D) + epsilon)
+    for copy in loads:
+        copy.wait()
+
+    def project(i, _):
+        span = pl.ds(pl.multiple_of(i * 256, 256), 256)
+        paired[span, :] = scale * lax.dot_general(win[:, span], wide[...], TN, preferred_element_type=f32)
+        return 0
+
+    lax.fori_loop(0, 2, project, 0)
+    blocks.relay(0)
+    blocks.relay(2)
+    second.first_near()
+    grouped[...] = scale * lax.dot_general(wgr[...], wide[...], TN, preferred_element_type=f32)
+    raw = scale * jnp.dot(w_st[...], wide[...], preferred_element_type=f32)
+    second.second_near(0)
+    second.first_far()
+    head = lax.broadcasted_iota(jnp.int32, (HL, STRETCH), 0)
+
+    def by_head(ref):
+        line = jnp.zeros((HL, STRETCH), f32)
+        for i in range(HL):
+            line = jnp.where(head == i, ref[i], line)
+        return line
+
+    raw = raw + by_head(bias)
+    steps = jnp.maximum(raw, 0.0) + jnp.log1p(jnp.exp(-jnp.abs(raw)))
+    cums = -by_head(decay) * steps
+    lane = lax.broadcasted_iota(jnp.int32, (HL, STRETCH), 1)
+    by = 1
+    while by < STRETCH:
+        cums = cums + jnp.where(lane >= by, pltpu.roll(cums, by, 1), 0.0)
+        by *= 2
+    turned = jnp.concatenate([cums, steps, jnp.zeros((128 - 2 * HL, STRETCH), f32)], axis=0).T
+    group = lax.div(me, 8)
+    b_proj = grouped[pl.ds(pl.multiple_of(group * NS, NS), NS), :]
+    c_proj = grouped[pl.ds(pl.multiple_of(G * NS + group * NS, NS), NS), :]
+    pairs = lax.dot_general(b_proj.astype(bf16), c_proj.astype(bf16), TN, preferred_element_type=f32)
+    src = lax.broadcasted_iota(jnp.int32, pairs.shape, 0)
+    dst = lax.broadcasted_iota(jnp.int32, pairs.shape, 1)
+    pairs = jnp.where(src <= dst, pairs, 0.0)
+
+    for copy in moved:
+        copy.wait_recv()
+    slot = slots[seq]
+    for h in range(HL):
+        for i in range(32):
+            lines[pl.ds(h * 32 + i, 1), :] = stores[slot, h : h + 1, i * 128 : (i + 1) * 128]
+    p_row = lax.broadcasted_iota(jnp.int32, (P_SIZE, 32), 0)
+    p_col = lax.broadcasted_iota(jnp.int32, (P_SIZE, 32), 1)
+    even = (p_row == 2 * p_col).astype(f32)
+    odd = (p_row == 2 * p_col + 1).astype(f32)
+    lane = lax.broadcasted_iota(jnp.int32, (HL * P_SIZE, 128), 1)
+    before = jnp.zeros((HL * P_SIZE, 128), f32)
+    for k in range(CONV - 1):
+        row = tail_all[lax.div(slot, 2), k, pl.ds(lax.rem(slot, 2), 1), :]
+        turn_row = jnp.broadcast_to(row, (128, HL * P_SIZE)).T
+        before = jnp.where(lane == 125 + k, turn_row, before)
+    taps = [flat(conv_w[k : k + 1, :], HL * P_SIZE) for k in range(CONV)]
+    mixing = flat(mix_g[...], HL * P_SIZE)
+    square = jnp.zeros((1, STRETCH), f32)
+    for h in range(HL):
+        chan = slice(h * P_SIZE, (h + 1) * P_SIZE)
+        gate = paired[h * 128 : h * 128 + 64, :]
+        signal = paired[h * 128 + 64 : h * 128 + 128, :]
+        padded = jnp.concatenate([before[chan], signal], axis=1)
+        conv = taps[CONV - 1][chan] * signal
+        for back in range(1, CONV):
+            conv = conv + taps[CONV - 1 - back][chan] * pltpu.roll(padded, back, 1)[:, 128:]
+        active = silu(conv)
+        cum = cums[h : h + 1, :]
+        step = steps[h : h + 1, :]
+        mix = jnp.exp(jnp.minimum(cum - turned[:, h : h + 1], 0.0)) * pairs * turned[:, HL + h : HL + h + 1]
+        within = jnp.dot(active.astype(bf16), mix.astype(bf16), preferred_element_type=f32)
+        rows = lines[h * 32 : (h + 1) * 32, :]
+        init = jnp.dot(even, rows[:, :NS], precision=highest, preferred_element_type=f32)
+        init = init + jnp.dot(odd, rows[:, NS:], precision=highest, preferred_element_type=f32)
+        carried = jnp.dot(init, c_proj, precision=highest, preferred_element_type=f32) * jnp.exp(cum)
+        gated = (within + carried + skip[h] * active) * silu(gate)
+        square = square + jnp.sum(gated * gated, axis=0, keepdims=True)
+        gained[chan, :] = gated * mixing[chan]
+        last = cum[:, STRETCH - 1 :]
+        to_end = jnp.exp(last - cum) * step
+        final_out[chan, :] = jnp.exp(last) * init + lax.dot_general(
+            active * to_end, b_proj, NT, precision=highest, preferred_element_type=f32
+        )
+        if h:
+            second.second_near(h)
+    squares[...] = jnp.broadcast_to(square, (8, STRETCH))
+    group = lax.div(me, 8)
+    spot = lax.rem(me, 8)
+    met = []
+    for by in range(1, 8):
+        copy = remote(
+            squares, peers3.at[by - 1], u_send.at[by - 1], u_recv.at[by - 1],
+            group * 8 + lax.rem(spot + by, 8),
+        )
+        copy.start()
+        met.append(copy)
+    for k in range(SIDE):
+        second.second_far(k)
+    blocks.relay(1)
+    blocks.relay(3)
+    total = square
+    for by in range(1, 8):
+        met[by - 1].wait_recv()
+        total = total + peers3[by - 1, 0:1, :]
+    scale = lax.rsqrt(total * (1.0 / (MH // G * P_SIZE)) + epsilon)
+    products(weight, (gained[...] * scale).astype(bf16), part)
+    scatter = Scatter(part, near1, full1, mid, near2, full2, x_send, x_recv)
+    for k in (3, 2, 1, 0):
+        scatter.one(k)
+    for k in (3, 2, 1, 0):
+        scatter.two(k)
+    acc[...] = jnp.dot(watt[:, D:], emb[...], preferred_element_type=f32)
+    scatter.three(3)
+    scatter.three(2)
+    for ch in range(CHUNKS):
+        blocks.rest(ch)
+    scatter.four(2)
+    scatter.three(1)
+    scatter.four(1)
+    scatter.three(0)
+    gain = column(gain_sh, me * SHARD, SHARD)
+    mine = pl.ds(pl.multiple_of(me * SHARD, 16), SHARD)
+    sq = jnp.zeros((1, STRETCH), f32)
+    for half in (0, 1):
+        rows = pl.ds(half * HALF, HALF)
+        value = hidden[rows, :].astype(f32) + scatter.result(half)
+        next_out[rows, :] = value
+        value = value.astype(bf16).astype(f32)
+        sq = sq + jnp.sum(value * value, axis=0, keepdims=True)
+        rounded[rows, :] = (value * gain[half * HALF : (half + 1) * HALF]).astype(bf16)
+    sums2[...] = jnp.broadcast_to(sq, (8, STRETCH))
+    gather = Gather(rounded, wide2, g_send, g_recv)
+    gather.start()
+    sent = send_sums(sums2, peers2, r_send, r_recv)
+    wide2[mine, :] = rounded[...]
+    gather.first_near()
+    gather.second_near(0)
+    gather.first_far()
+    for k in (1, 2, 3):
+        gather.second_near(k)
+    for ch in range(CHUNKS):
+        blocks.far(ch)
+    for k in range(SIDE):
+        gather.second_far(k)
+    total = add_sums(sums2, peers2, sent)[0:1, :] + embed_sq
+    scale = lax.rsqrt(total * (0.5 / D) + epsilon)
+    value = acc[...] + jnp.dot(watt[:, :D], wide2[...], preferred_element_type=f32)
+    proj_out[...] = (value * scale).astype(bf16)
+    gather.finish()
+    scatter.finish()
+    blocks.finish()
+    first.finish()
+    second.finish()
+    for copy in out + moved + met + sent:
+        copy.wait_send()
+
+
+def front_call(*args):
+    anywhere = pl.BlockSpec(memory_space=pl.ANY)
+    vmem = pl.BlockSpec(memory_space=pltpu.VMEM)
+    smem = pl.BlockSpec(memory_space=pltpu.SMEM)
+    dma = pltpu.SemaphoreType.DMA
+    return pl.pallas_call(
+        front_kernel,
+        out_shape=(
+            jax.ShapeDtypeStruct((SHARD, STRETCH), f32),
+            jax.ShapeDtypeStruct((3 * HD, STRETCH), bf16),
+            jax.ShapeDtypeStruct((HL * P_SIZE, NS), f32),
+            jax.ShapeDtypeStruct((SEQ * BLOCKS, 2, HD, BLOCK), bf16),
+        ),
+        in_specs=[anywhere] * 6 + [smem] + [anywhere] * 2 + [vmem] + [smem] * 3 + [anywhere] * 5,
+        out_specs=(vmem, vmem, vmem, anywhere),
+        scratch_shapes=[
+            pltpu.VMEM((SHARD, STRETCH), bf16),
+            pltpu.VMEM((SHARD, STRETCH), bf16),
+            pltpu.VMEM((D // 128, 128), f32),
+            pltpu.VMEM((2 * D // 128, 128), f32),
+            pltpu.VMEM((CONV, HL * P_SIZE), f32),
+            pltpu.VMEM((1, HL * P_SIZE), f32),
+            pltpu.VMEM((HL * P_SIZE, D), bf16),
+            pltpu.VMEM((D, STRETCH), bf16),
+            pltpu.VMEM((SHARD, STRETCH), bf16),
+            pltpu.VMEM((SHARD, STRETCH), bf16),
+            pltpu.VMEM((D, HL * 128), bf16),
+            pltpu.VMEM((D, 2 * G * NS), bf16),
+            pltpu.VMEM((HL * 128, STRETCH), f32),
+            pltpu.VMEM((2 * G * NS, STRETCH), f32),
+            pltpu.VMEM((8, STRETCH), f32),
+            pltpu.VMEM((HEADS - 1, 8, STRETCH), f32),
+            pltpu.VMEM((2 * SEQ, HL, P_SIZE * NS), f32),
+            pltpu.VMEM((SEQ, CONV - 1, 2, HL * P_SIZE), f32),
+            pltpu.VMEM((128, 128), f32),
+            pltpu.VMEM((HL * P_SIZE, STRETCH), f32),
+            pltpu.VMEM((3 * HD, 2 * D), bf16),
+            pltpu.VMEM((D, STRETCH), bf16),
+            pltpu.VMEM((D, STRETCH), bf16),
+            pltpu.VMEM((3 * HD, STRETCH), f32),
+            pltpu.VMEM((8, STRETCH), f32),
+            pltpu.VMEM((7, 8, STRETCH), f32),
+            pltpu.VMEM((8, STRETCH), f32),
+            pltpu.VMEM((HEADS - 1, 8, STRETCH), f32),
+            pltpu.VMEM((SHARD, STRETCH), bf16),
+        ] + SCATTER_SCRATCH + GATHER_SEMS + GATHER_SEMS + GATHER_SEMS + [
+            dma((HEADS - 1,)), dma((HEADS - 1,)),
+            dma((SEQ - 1,)), dma((SEQ - 1,)),
+            dma((SEQ - 1,)), dma((SEQ - 1,)),
+            dma((7,)), dma((7,)),
+            dma((HEADS - 1,)), dma((HEADS - 1,)),
+            dma((28,)), dma((28,)),
+            dma((6,)), dma((7,)),
+        ],
+        compiler_params=pltpu.CompilerParams(
+            collective_id=0, has_side_effects=True, vmem_limit_bytes=60 * 2**20
+        ),
+        name="front_rows",
+    )(*args)
+
+
 def merge_kernel(attended, weight, before, out,
                  part, near1, full1, mid, near2, full2, s_send, s_recv):
     barrier = greet_heads()
@@ -780,17 +957,11 @@
          conv_weight, mix_gain, w_output, state_store, conv_store, state_slot, prefix_len, block_table,
          shared_gain, w_attend, cache_pool, w_merge):
     heads_local = w_step.shape[1]
-    pool = lax.all_gather(cache_pool.transpose(0, 1, 3, 2), "seq", axis=0, tiled=True)
-    rows = state_store.shape[0]
-    tails = jnp.pad(conv_store.astype(f32).reshape(rows, 6, 128), ((0, 0), (0, 2), (0, 0)))
-    hidden_t = hidden.T
-    gain_sh = shared_gain.reshape(2 * D // 128, 128)
-    gained, squares, final_state, embed_all, embed_sq = scan_call(
-        hidden_t, embedding.T, input_gain.reshape(D // 128, 128), gain_sh, state_store, tails, state_slot,
-        w_input, w_groups, w_step.T, step_bias, decay_rate, skip_gain, conv_weight, mix_gain[None, :],
-    )
-    hidden_next, projected = mix_call(
-        gained, squares, w_output, hidden_t, gain_sh, w_attend.T, embed_all, embed_sq
+    hidden_next, projected, final_state, pool = front_call(
+        hidden.T, embedding.T, input_gain.reshape(D // 128, 128), shared_gain.reshape(2 * D // 128, 128),
+        state_store, conv_store.transpose(1, 0, 2).astype(f32), state_slot, w_input, w_groups, w_step.T,
+        step_bias, decay_rate, skip_gain, conv_weight, mix_gain[None, :], w_output, w_attend.T,
+        cache_pool.transpose(0, 1, 3, 2),
     )
     attended = attend_call(block_table, prefix_len, projected, pool)
     layer_output = merge_call(attended, w_merge, hidden_next)

time: 180 us -> 193 us (1.072)
  Pallas kernels: 148 us -> 188 us
  between operations: 14.1 us -> 0.71 us
  local copies, waits for them, and re-layouts: 15.8 us -> 2.61 us
    pallas_call x2 -> x1, Pallas kernels: 115 us -> 152 us  [front_call(): pl.pallas_call(front_kernel, out_shape=(jax.ShapeDtypeStruct((SHARD, STRE...]
    unnamed x44 -> x13, local copies, waits for them, and re-layouts: 15 us -> 1.88 us
    pallas_call x1, Pallas kernels: 3.8 us -> 13 us  [attend_call(): pl.pallas_call(attend_kernel, out_shape=jax.ShapeDtypeStruct((HD, STRETCH...]
    pallas_call x1, Pallas kernels: 28.6 us -> 22.5 us  [merge_call(): pl.pallas_call(merge_kernel, out_shape=jax.ShapeDtypeStruct((SHARD, STRET...]
  transfers between devices with their start and end apart: 1 -> 0, of which waited for: 0 -> 0; matrix products, arithmetic and copies ran while one was open for 1% -> 0% of each run, Pallas kernels for 65% -> 0%
where the time goes in v3:
time: 193 us; the launch traced here: 192 us
  Pallas kernels  188 us (97%)
  local copies, waits for them, and re-layouts  2.61 us (1%)
    pallas_call x1, Pallas kernels, front_call(): pl.pallas_call(front_kernel, out_shape=(jax.ShapeDtypeStruct((SHARD, STRE...  152 us
    pallas_call x1, Pallas kernels, merge_call(): pl.pallas_call(merge_kernel, out_shape=jax.ShapeDtypeStruct((SHARD, STRET...  22.5 us
    pallas_call x1, Pallas kernels, attend_call(): pl.pallas_call(attend_kernel, out_shape=jax.ShapeDtypeStruct((HD, STRETCH...  13 us

profile of v3, /device:TPU:0, one launch (start us, length us, event | category | flops | bytes accessed | tf_op | source)
XLA Modules:
  0.0 192.4 jit_solution(10163506386207866437)
XLA Ops:
  0.6 1.3 convert_bitcast_fusion.tails
  1.9 0.0 copy-start.3
  1.9 0.0 copy-start.4
  1.9 152.3 %front_rows.1 = (f32[224,512]{1,0:T(8,128)}, bf16[672,512]{1,0:T(8,128)(2,1)}, f32[256,64]{1,0:T(8,128)}, bf16[160,2,224,128]{3,2,1,0:T(8,128)(2,1)}) custom-call(bf16[224,512]{1,0:T(8,128)(2,1)} %bitcast.14, bf16[224,512]{1,0:T(8,128)(2,1)} %bitcast.15, f32[28,128]{1,0:T(8,128)} %bitcast.18, f32[56,128]{1,0:T(8,128)} %bitcast.16, f32[2,4,4096]{2,1,0:T(4,128)} %states.1, ...), custom_call_target="tpu_custom_call" | custom-call | tf_op jit(solution)/shard_map/front_rows/pallas_call | solution.py:775
  154.2 0.0 copy-done.3
  154.2 0.0 copy-done.4
  154.2 0.0 copy-start.1
  154.2 1.1 copy-done.1
  155.3 0.0 copy-start
  155.3 0.0 copy-start.2
  155.3 13.0 %attend_rows.1.attended = bf16[224,512]{1,0:T(8,128)(2,1)S(1)} custom-call(s32[8,64]{1,0:T(8,128)S(1)} %copy-done.3, s32[8]{0:T(128)S(1)} %copy-done.4, bf16[672,512]{1,0:T(8,128)(2,1)S(1)} %copy-done.1, bf16[160,2,224,128]{3,2,1,0:T(8,128)(2,1)} %get-tuple-element.7.pool), custom_call_target="tpu_custom_call" | custom-call | tf_op jit(solution)/shard_map/attend_rows/pallas_call | solution.py:939
  168.3 0.0 copy-done
  168.3 0.0 copy-done.2
  168.3 0.0 copy-start.5
  168.3 22.5 %merge_rows.1 = f32[224,512]{1,0:T(8,128)S(1)} custom-call(bf16[224,512]{1,0:T(8,128)(2,1)S(1)} %attend_rows.1.attended, bf16[224,3584]{1,0:T(8,128)(2,1)S(1)} %copy-done, f32[224,512]{1,0:T(8,128)S(1)} %copy-done.2), custom_call_target="tpu_custom_call" | custom-call | tf_op jit(solution)/shard_map/merge_rows/pallas_call | solution.py:846
  190.9 0.0 copy-done.5
  190.9 0.7 reshape.15
  191.6 0.8 copy.24
Async XLA Ops:
  1.9 152.3 %copy-start.3 = (s32[8,64]{1,0:T(8,128)S(1)}, s32[8,64]{1,0:T(8,128)}, u32[]{:S(2)}) copy-start(s32[8,64]{1,0:T(8,128)} %table.1) | copy-start | bytes 6148
  1.9 152.3 %copy-start.4 = (s32[8]{0:T(128)S(1)}, s32[8]{0:T(128)}, u32[]{:S(2)}) copy-start(s32[8]{0:T(128)} %lengths.1) | copy-start | bytes 100
  154.2 1.1 copy-start.1
  155.3 13.0 %copy-start = (bf16[224,3584]{1,0:T(8,128)(2,1)S(1)}, bf16[224,3584]{1,0:T(8,128)(2,1)}, u32[]{:S(2)}) copy-start(bf16[224,3584]{1,0:T(8,128)(2,1)} %weight.1) | copy-start | bytes 4816900
  155.3 13.0 %copy-start.2 = (f32[224,512]{1,0:T(8,128)S(1)}, f32[224,512]{1,0:T(8,128)}, u32[]{:S(2)}) copy-start(f32[224,512]{1,0:T(8,128)} %get-tuple-element.8.before) | copy-start | bytes 1376260
  168.3 22.5 %copy-start.5 = (f32[256,64]{1,0:T(8,128)S(1)}, f32[256,64]{1,0:T(8,128)}, u32[]{:S(2)}) copy-start(f32[256,64]{1,0:T(8,128)} %get-tuple-element.9) | copy-start | bytes 196612

commit v4 on v3

--- a/solution.py
+++ b/solution.py
@@ -608,7 +608,7 @@
     total = add_sums(sums, peers, out)
     embed_sq = total[1:2, :]
     scale = lax.rsqrt(total[0:1, :] * (1.0 / D) + epsilon)
-    for copy in loads:
+    for copy in loads[:4]:
         copy.wait()
 
     def project(i, _):
@@ -721,6 +721,7 @@
         scatter.one(k)
     for k in (3, 2, 1, 0):
         scatter.two(k)
+    loads[4].wait()
     acc[...] = jnp.dot(watt[:, D:], emb[...], preferred_element_type=f32)
     scatter.three(3)
     scatter.three(2)
@@ -760,6 +761,7 @@
     proj_out[...] = (value * scale).astype(bf16)
     gather.finish()
     scatter.finish()
+    loads[5].wait()
     blocks.finish()
     first.finish()
     second.finish()

time: 193 us -> 149 us (0.77)
  Pallas kernels: 188 us -> 142 us
    pallas_call x1, Pallas kernels: 152 us -> 110 us  [front_call(): pl.pallas_call(front_kernel, out_shape=(jax.ShapeDtypeStruct((SHARD, STRE...]
    pallas_call x1, Pallas kernels: 13 us -> 5.12 us  [attend_call(): pl.pallas_call(attend_kernel, out_shape=jax.ShapeDtypeStruct((HD, STRETCH...]
    pallas_call x1, Pallas kernels: 22.5 us -> 26.7 us  [merge_call(): pl.pallas_call(merge_kernel, out_shape=jax.ShapeDtypeStruct((SHARD, STRET...]
where the time goes in v4:
time: 149 us; the launch traced here: 147 us
  Pallas kernels  142 us (95%)
  local copies, waits for them, and re-layouts  2.61 us (2%)
    pallas_call x1, Pallas kernels, front_call(): pl.pallas_call(front_kernel, out_shape=(jax.ShapeDtypeStruct((SHARD, STRE...  110 us
    pallas_call x1, Pallas kernels, merge_call(): pl.pallas_call(merge_kernel, out_shape=jax.ShapeDtypeStruct((SHARD, STRET...  26.7 us
    pallas_call x1, Pallas kernels, attend_call(): pl.pallas_call(attend_kernel, out_shape=jax.ShapeDtypeStruct((HD, STRETCH...  5.12 us

profile of v4, /device:TPU:0, one launch (start us, length us, event | category | flops | bytes accessed | tf_op | source)
XLA Modules:
  0.0 146.6 jit_solution(1487356336745777008)
XLA Ops:
  0.6 1.3 convert_bitcast_fusion.tails
  1.9 0.0 copy-start.3
  1.9 0.0 copy-start.4
  1.9 110.2 %front_rows.1 = (f32[224,512]{1,0:T(8,128)}, bf16[672,512]{1,0:T(8,128)(2,1)}, f32[256,64]{1,0:T(8,128)}, bf16[160,2,224,128]{3,2,1,0:T(8,128)(2,1)}) custom-call(bf16[224,512]{1,0:T(8,128)(2,1)} %bitcast.14, bf16[224,512]{1,0:T(8,128)(2,1)} %bitcast.15, f32[28,128]{1,0:T(8,128)} %bitcast.18, f32[56,128]{1,0:T(8,128)} %bitcast.16, f32[2,4,4096]{2,1,0:T(4,128)} %states.1, ...), custom_call_target="tpu_custom_call" | custom-call | tf_op jit(solution)/shard_map/front_rows/pallas_call | solution.py:777
  112.1 0.0 copy-done.3
  112.1 0.0 copy-done.4
  112.1 0.0 copy-start.1
  112.2 1.1 copy-done.1
  113.2 0.0 copy-start
  113.2 0.0 copy-start.2
  113.2 5.1 %attend_rows.1.attended = bf16[224,512]{1,0:T(8,128)(2,1)S(1)} custom-call(s32[8,64]{1,0:T(8,128)S(1)} %copy-done.3, s32[8]{0:T(128)S(1)} %copy-done.4, bf16[672,512]{1,0:T(8,128)(2,1)S(1)} %copy-done.1, bf16[160,2,224,128]{3,2,1,0:T(8,128)(2,1)} %get-tuple-element.7.pool), custom_call_target="tpu_custom_call" | custom-call | tf_op jit(solution)/shard_map/attend_rows/pallas_call | solution.py:941
  118.4 0.0 copy-done
  118.4 0.0 copy-done.2
  118.4 0.0 copy-start.5
  118.4 26.7 %merge_rows.1 = f32[224,512]{1,0:T(8,128)S(1)} custom-call(bf16[224,512]{1,0:T(8,128)(2,1)S(1)} %attend_rows.1.attended, bf16[224,3584]{1,0:T(8,128)(2,1)S(1)} %copy-done, f32[224,512]{1,0:T(8,128)S(1)} %copy-done.2), custom_call_target="tpu_custom_call" | custom-call | tf_op jit(solution)/shard_map/merge_rows/pallas_call | solution.py:848
  145.1 0.0 copy-done.5
  145.1 0.7 reshape.15
  145.9 0.8 copy.24
Async XLA Ops:
  1.9 110.2 %copy-start.3 = (s32[8,64]{1,0:T(8,128)S(1)}, s32[8,64]{1,0:T(8,128)}, u32[]{:S(2)}) copy-start(s32[8,64]{1,0:T(8,128)} %table.1) | copy-start | bytes 6148
  1.9 110.2 %copy-start.4 = (s32[8]{0:T(128)S(1)}, s32[8]{0:T(128)}, u32[]{:S(2)}) copy-start(s32[8]{0:T(128)} %lengths.1) | copy-start | bytes 100
  112.1 1.1 copy-start.1
  113.2 5.1 %copy-start = (bf16[224,3584]{1,0:T(8,128)(2,1)S(1)}, bf16[224,3584]{1,0:T(8,128)(2,1)}, u32[]{:S(2)}) copy-start(bf16[224,3584]{1,0:T(8,128)(2,1)} %weight.1) | copy-start | bytes 4816900
  113.2 5.1 %copy-start.2 = (f32[224,512]{1,0:T(8,128)S(1)}, f32[224,512]{1,0:T(8,128)}, u32[]{:S(2)}) copy-start(f32[224,512]{1,0:T(8,128)} %get-tuple-element.8.before) | copy-start | bytes 1376260
  118.4 26.7 %copy-start.5 = (f32[256,64]{1,0:T(8,128)S(1)}, f32[256,64]{1,0:T(8,128)}, u32[]{:S(2)}) copy-start(f32[256,64]{1,0:T(8,128)} %get-tuple-element.9) | copy-start | bytes 196612

commit v5 on v4

--- a/solution.py
+++ b/solution.py
@@ -125,8 +125,8 @@
             self.arrive(half, 3, far, c2, RIGHT)
             self.second(half, 3)
 
-    def second_near(self, k):
-        for half in (0, 1):
+    def second_near(self, k, halves=(0, 1)):
+        for half in halves:
             c1, c2 = coords(half)
             o1 = around(c1, OFFSETS[k])
             for way in (0, 1):
@@ -136,23 +136,32 @@
                 self.arrive(half, 4 + 4 * k + way, o1, nb, FULL)
                 self.go(half, 6 + 4 * k + way, self.out.at[piece(half, o1, nb), lanes], o1, nb, lanes, c1, to)
 
-    def second_far(self, k):
-        for half in (0, 1):
+    def second_far(self, k, halves=(0, 1)):
+        for half in halves:
             c1, c2 = coords(half)
             o1 = around(c1, OFFSETS[k])
             far = around(c2, 2)
             self.arrive(half, 6 + 4 * k, o1, far, LEFT)
             self.arrive(half, 7 + 4 * k, o1, far, RIGHT)
 
-    def run(self):
-        self.start()
+    def run(self, use, between):
         self.first_near()
         self.second_near(0)
         self.first_far()
-        for k in (1, 2, 3):
-            self.second_near(k)
+        self.second_near(1)
+        self.second_far(0, (1,))
+        use(0)
+        self.second_near(2)
+        self.second_near(3)
+        between()
+        self.second_far(1, (1,))
+        use(-1)
+        self.second_far(2, (1,))
+        use(1)
+        self.second_far(3, (1,))
         for k in range(SIDE):
-            self.second_far(k)
+            self.second_far(k, (0,))
+        use(2)
 
     def finish(self):
         for copy in self.sent:
@@ -188,8 +197,8 @@
         me1, me2 = coords(half)
         remote(where, where, self.ss.at[half, idx], self.rs.at[half, idx], device(half, around(me1, 1), me2)).wait_recv()
 
-    def one(self, k):
-        for half in (0, 1):
+    def one(self, k, halves):
+        for half in halves:
             c1, c2 = coords(half)
             o1 = around(c1, OFFSETS[k])
             rows = piece(half, o1, around(c2, 2))
@@ -240,12 +249,20 @@
             self.mid[half, k, :, lanes] = (mine + self.near2[half, way].astype(f32)).astype(bf16)
             self.go(half, 18 + way, self.mid.at[half, k], self.full2.at[half, way], around(c1, OFFSETS[k]), c2)
 
-    def run(self):
+    def run(self, weight, rows, early=(), late=()):
+        for by in (2, -1, 1, 0):
+            products(weight, rows, self.part, by)
         for k in (3, 2, 1, 0):
-            self.one(k)
-        for k in (3, 2, 1, 0):
-            self.two(k)
+            self.one(k, (0, 1))
+        for step in early:
+            step()
+        self.two(3)
+        self.two(2)
+        self.two(1)
         self.three(3)
+        self.two(0)
+        for step in late:
+            step()
         self.three(2)
         self.four(2)
         self.three(1)
@@ -321,136 +338,18 @@
 HL = 4
 
 
-def products(weight, rows, part):
-    width = 512
-
-    def chunk(i, _):
-        span = pl.ds(pl.multiple_of(i * width, width), width)
-        part[span, :] = lax.dot_general(
-            weight[:, span], rows, (((0,), (0,)), ((), ())), preferred_element_type=f32
-        ).astype(bf16)
-        return 0
-
-    lax.fori_loop(0, D // width, chunk, 0)
-
-
-def mix_kernel(gated, squares, weight, hidden, gain_sh, w_att, embed_all, embed_sq, next_out, proj_out,
-               part, near1, full1, mid, near2, full2, s_send, s_recv,
-               g_send, g_recv, peers, q_send, q_recv, sums, peers2, r_send, r_recv, rounded, watt, emb, wide,
-               acc, local):
-    loads = [
-        pltpu.make_async_copy(embed_all, emb, local.at[0]),
-        pltpu.make_async_copy(w_att, watt, local.at[1]),
-    ]
-    for copy in loads:
-        copy.start()
-    barrier = greet_heads()
-    pl.semaphore_wait(barrier, HEADS - 1)
-    me = lax.axis_index("head")
-    group = lax.div(me, 8)
-    spot = lax.rem(me, 8)
-    out = []
-    for by in range(1, 8):
-        copy = remote(
-            squares, peers.at[by - 1], q_send.at[by - 1], q_recv.at[by - 1],
-            group * 8 + lax.rem(spot + by, 8),
-        )
-        copy.start()
-        out.append(copy)
-    total = squares[0:1, :]
-    for by in range(1, 8):
-        out[by - 1].wait_recv()
-        total = total + peers[by - 1, 0:1, :]
-    scale = lax.rsqrt(total * (1.0 / (MH // G * P_SIZE)) + epsilon)
-    products(weight, (gated[...] * scale).astype(bf16), part)
-    scatter = Scatter(part, near1, full1, mid, near2, full2, s_send, s_recv)
-    for k in (3, 2, 1, 0):
-        scatter.one(k)
-    for copy in loads:
-        copy.wait()
-
-    def from_embed(i):
-        acc[i * SHARD : (i + 1) * SHARD, :] = jnp.dot(
-            watt[i * SHARD : (i + 1) * SHARD, D:], emb[...], preferred_element_type=f32
-        )
-
-    for k in (3, 2, 1, 0):
-        scatter.two(k)
-    from_embed(0)
-    scatter.three(3)
-    scatter.three(2)
-    from_embed(1)
-    scatter.four(2)
-    scatter.three(1)
-    scatter.four(1)
-    scatter.three(0)
-    from_embed(2)
-    gain = column(gain_sh, me * SHARD, SHARD)
-    mine = pl.ds(pl.multiple_of(me * SHARD, 16), SHARD)
-    sq = jnp.zeros((1, STRETCH), f32)
-    for half in (0, 1):
-        rows = pl.ds(half * HALF, HALF)
-        value = hidden[rows, :].astype(f32) + scatter.result(half)
-        next_out[rows, :] = value
-        value = value.astype(bf16).astype(f32)
-        sq = sq + jnp.sum(value * value, axis=0, keepdims=True)
-        rounded[rows, :] = (value * gain[half * HALF : (half + 1) * HALF]).astype(bf16)
-    sums[...] = jnp.broadcast_to(sq, (8, STRETCH))
-    gather = Gather(rounded, wide, g_send, g_recv)
-    gather.start()
-    sent = send_sums(sums, peers2, r_send, r_recv)
-    wide[mine, :] = rounded[...]
-    gather.first_near()
-    gather.second_near(0)
-    gather.first_far()
-    for k in (1, 2, 3):
-        gather.second_near(k)
-    for k in range(SIDE):
-        gather.second_far(k)
-    total = add_sums(sums, peers2, sent)[0:1, :] + embed_sq[1:2, :]
-    scale = lax.rsqrt(total * (0.5 / D) + epsilon)
-    for i in range(3):
-        rows = slice(i * SHARD, (i + 1) * SHARD)
-        value = acc[rows, :] + jnp.dot(watt[rows, :D], wide[...], preferred_element_type=f32)
-        proj_out[rows, :] = (value * scale).astype(bf16)
-    gather.finish()
-    scatter.finish()
-    for copy in out + sent:
-        copy.wait_send()
-
-
-def mix_call(gated, squares, weight, hidden, gain_sh, w_att, embed_all, embed_sq):
-    vmem = pl.BlockSpec(memory_space=pltpu.VMEM)
-    anywhere = pl.BlockSpec(memory_space=pl.ANY)
-    dma = pltpu.SemaphoreType.DMA
-    return pl.pallas_call(
-        mix_kernel,
-        out_shape=(
-            jax.ShapeDtypeStruct((SHARD, STRETCH), f32),
-            jax.ShapeDtypeStruct((3 * HD, STRETCH), bf16),
-        ),
-        in_specs=[vmem] * 5 + [anywhere] * 2 + [vmem],
-        out_specs=(vmem, vmem),
-        scratch_shapes=SCATTER_SCRATCH + GATHER_SEMS + [
-            pltpu.VMEM((7, 8, STRETCH), f32),
-            dma((7,)),
-            dma((7,)),
-            pltpu.VMEM((8, STRETCH), f32),
-            pltpu.VMEM((HEADS - 1, 8, STRETCH), f32),
-            dma((HEADS - 1,)),
-            dma((HEADS - 1,)),
-            pltpu.VMEM((SHARD, STRETCH), bf16),
-            pltpu.VMEM((3 * HD, 2 * D), bf16),
-            pltpu.VMEM((D, STRETCH), bf16),
-            pltpu.VMEM((D, STRETCH), bf16),
-            pltpu.VMEM((3 * HD, STRETCH), f32),
-            dma((2,)),
-        ],
-        compiler_params=pltpu.CompilerParams(
-            collective_id=1, has_side_effects=True, vmem_limit_bytes=56 * 2**20
-        ),
-        name="mix_rows",
-    )(gated, squares, weight, hidden, gain_sh, w_att, embed_all, embed_sq)
+ROW = SIDE * SHARD
+
+
+def row_of(by):
+    return pl.ds(pl.multiple_of(around(place()[0], by) * ROW, 128), ROW)
+
+
+def products(weight, rows, part, by):
+    span = row_of(by)
+    part[span, :] = lax.dot_general(
+        weight[:, span], rows, TN, preferred_element_type=f32
+    ).astype(bf16)
 
 
 CHUNKS = 4
@@ -464,77 +363,55 @@
         self.x, self.core = lax.div(seq, 2), lax.rem(seq, 2)
         self.sent = []
 
-    def slab(self, by, core, ch):
+    def slab(self, by, ch):
         per = BLOCKS // CHUNKS
-        return self.out.at[pl.ds((around(self.x, by) * 2 + core) * BLOCKS + ch * per, per)]
-
-    def copy(self, idx, src, dst, by, core):
+        return self.out.at[pl.ds(around(self.x, by) * BLOCKS + ch * per, per)]
+
+    def copy(self, idx, src, dst, by):
         return pltpu.make_async_remote_copy(
             src_ref=src, dst_ref=dst, send_sem=self.ss.at[idx], recv_sem=self.rs.at[idx],
-            device_id={"seq": around(self.x, by) * 2 + core}, device_id_type=MESH,
+            device_id={"seq": around(self.x, by) * 2 + self.core}, device_id_type=MESH,
         )
 
-    def go(self, idx, src, dst, by, core):
-        copy = self.copy(idx, src, dst, by, core)
+    def go(self, idx, src, dst, by):
+        copy = self.copy(idx, src, dst, by)
         copy.start()
         self.sent.append(copy)
 
     def arrive(self, idx, dst):
-        self.copy(idx, dst, dst, 1, self.core).wait_recv()
-
-    def start(self):
+        self.copy(idx, dst, dst, 1).wait_recv()
+
+    def spread(self, right, left):
         per = BLOCKS // CHUNKS
-        for near, far in ((0, 2), (1, 3), (2, 0), (3, 1)):
-            for base, ch, by in ((0, near, 1), (4, far, -1)):
-                self.go(base + ch, self.own.at[pl.ds(ch * per, per)], self.slab(0, self.core, ch), by, self.core)
+        for base, ch, by in ((0, right, 1), (4, left, -1)):
+            self.go(base + ch, self.own.at[pl.ds(ch * per, per)], self.slab(0, ch), by)
+
+    def relay(self, ch):
+        way = -1 if ch < 2 else 1
+        where = self.slab(way, ch)
+        self.arrive(ch if ch < 2 else 4 + ch, where)
+        self.go(8 + ch, where, where, -way)
+
+    def finish(self):
         for ch in range(CHUNKS):
-            self.go(12 + ch, self.own.at[pl.ds(ch * per, per)], self.slab(0, self.core, ch), 0, 1 - self.core)
-
-    def share(self, j, by, ch):
-        where = self.slab(by, self.core, ch)
-        self.go(12 + 4 * j + ch, where, where, 0, 1 - self.core)
-
-    def relay(self, ch):
-        left = self.slab(-1, self.core, ch)
-        right = self.slab(1, self.core, ch)
-        if ch < 2:
-            self.arrive(ch, left)
-            self.go(8 + ch, left, left, 1, self.core)
-            self.share(1, -1, ch)
-        else:
-            self.arrive(4 + ch, right)
-            self.go(8 + ch, right, right, -1, self.core)
-            self.share(2, 1, ch)
-
-    def rest(self, ch):
-        if ch < 2:
-            self.arrive(4 + ch, self.slab(1, self.core, ch))
-            self.share(2, 1, ch)
-        else:
-            self.arrive(ch, self.slab(-1, self.core, ch))
-            self.share(1, -1, ch)
-
-    def far(self, ch):
-        self.arrive(8 + ch, self.slab(2, self.core, ch))
-        self.share(3, 2, ch)
-
-    def finish(self):
-        for j, by in enumerate((0, -1, 1, 2)):
-            for ch in range(CHUNKS):
-                self.arrive(12 + 4 * j + ch, self.slab(by, 1 - self.core, ch))
+            if ch < 2:
+                self.arrive(4 + ch, self.slab(1, ch))
+            else:
+                self.arrive(ch, self.slab(-1, ch))
+            self.arrive(8 + ch, self.slab(2, ch))
         for copy in self.sent:
             copy.wait_send()
 
 
 def front_kernel(hidden_in, embed_in, gain_in_in, gain_sh_in, states, tails, slots, w_in, w_gr, w_st, bias, decay,
                  skip, conv_in, mix_in, w_out_in, w_att, pool_in,
-                 next_out, proj_out, final_out, pool_out,
+                 next_out, proj_out, final_out, pool_out, other_out,
                  hidden, embed, gain_in, gain_sh, conv_w, mix_g, weight,
                  wide, own_h, own_e, win, wgr, paired, grouped, sums, peers, stores, tail_all, lines, gained, watt,
                  emb, wide2, acc, squares, peers3, sums2, peers2, rounded,
                  part, near1, full1, mid, near2, full2, x_send, x_recv,
                  h_send, h_recv, e_send, e_recv, g_send, g_recv, q_send, q_recv, s_send, s_recv, t_send, t_recv,
-                 u_send, u_recv, r_send, r_recv, p_send, p_recv, local, here):
+                 u_send, u_recv, r_send, r_recv, p_send, p_recv, local, here, raws, mine_q, v_send, v_recv):
     seq = lax.axis_index("seq")
     me = lax.axis_index("head")
     small = [
@@ -552,7 +429,7 @@
         pltpu.make_async_copy(states, stores.at[pl.ds(seq * 2, 2)], local.at[2]),
         pltpu.make_async_copy(tails, tail_all.at[seq], local.at[3]),
         pltpu.make_async_copy(w_att, watt, local.at[4]),
-        pltpu.make_async_copy(pool_in, pool_out.at[pl.ds(seq * BLOCKS, BLOCKS)], local.at[5]),
+        pltpu.make_async_copy(pool_in, pool_out.at[pl.ds(lax.div(seq, 2) * BLOCKS, BLOCKS)], local.at[5]),
     ]
     for copy in loads:
         copy.start()
@@ -584,46 +461,72 @@
     line = lax.broadcasted_iota(jnp.int32, (8, STRETCH), 0)
     sums[...] = jnp.where(line == 0, sq_h, jnp.where(line == 1, sq_e, 0.0))
     out = send_sums(sums, peers, q_send, q_recv)
+    x, core = lax.div(seq, 2), lax.rem(seq, 2)
+    held = (
+        (states, stores, lambda at: stores.at[pl.ds(at * 2, 2)], s_send, s_recv),
+        (tails, tail_all, lambda at: tail_all.at[at], t_send, t_recv),
+    )
     moved = []
-    for by in range(1, SEQ):
-        to = {"seq": lax.rem(seq + by, SEQ)}
-        for src, dst, ss, rs in (
-            (states, stores.at[pl.ds(seq * 2, 2)], s_send, s_recv), (tails, tail_all.at[seq], t_send, t_recv)
-        ):
-            copy = pltpu.make_async_remote_copy(
-                src_ref=src, dst_ref=dst, send_sem=ss.at[by - 1], recv_sem=rs.at[by - 1],
-                device_id=to, device_id_type=MESH,
-            )
-            copy.start()
-            moved.append(copy)
-    first.first_near()
-    blocks.start()
-    first.second_near(0)
-    first.first_far()
-    for k in (1, 2, 3):
-        first.second_near(k)
-    second.start()
-    for k in range(SIDE):
-        first.second_far(k)
+
+    def send_state(idx, src, dst, ss, rs, to):
+        copy = pltpu.make_async_remote_copy(
+            src_ref=src, dst_ref=dst, send_sem=ss.at[idx], recv_sem=rs.at[idx],
+            device_id={"seq": to}, device_id_type=MESH,
+        )
+        copy.start()
+        moved.append(copy)
+
+    for src, _, at, ss, rs in held:
+        for by in range(1, SIDE):
+            send_state(by - 1, src, at(seq), ss, rs, around(x, by) * 2 + core)
+        send_state(3, src, at(seq), ss, rs, x * 2 + 1 - core)
+
+    def pass_states():
+        for _, _, at, ss, rs in held:
+            for by in range(1, SIDE):
+                where = at(around(x, -by) * 2 + core)
+                pltpu.make_async_remote_copy(
+                    src_ref=where, dst_ref=where, send_sem=ss.at[by - 1], recv_sem=rs.at[by - 1],
+                    device_id={"seq": x * 2 + 1 - core}, device_id_type=MESH,
+                ).wait_recv()
+                send_state(3 + by, where, where, ss, rs, x * 2 + 1 - core)
+
+    def wait_states():
+        for _, _, at, ss, rs in held:
+            for by in range(SIDE):
+                where = at(around(x, -by) * 2 + 1 - core)
+                pltpu.make_async_remote_copy(
+                    src_ref=where, dst_ref=where, send_sem=ss.at[3 + by], recv_sem=rs.at[3 + by],
+                    device_id={"seq": x * 2 + 1 - core}, device_id_type=MESH,
+                ).wait_recv()
+
+    blocks.spread(0, 2)
+    paired[...] = jnp.zeros_like(paired)
+    grouped[...] = jnp.zeros_like(grouped)
+    raws[...] = jnp.zeros_like(raws)
+    for copy in loads[:2]:
+        copy.wait()
+
+    def project(by):
+        span = row_of(by)
+        rows = wide[span, :]
+        paired[...] += lax.dot_general(win[span, :], rows, TN, preferred_element_type=f32)
+        grouped[...] += lax.dot_general(wgr[span, :], rows, TN, preferred_element_type=f32)
+        raws[...] += jnp.dot(w_st[:, span], rows, preferred_element_type=f32)
+
+    def between():
+        second.start()
+        pass_states()
+        blocks.spread(1, 3)
+        blocks.relay(0)
+        blocks.relay(2)
+        blocks.spread(2, 0)
+
+    first.run(project, between)
     total = add_sums(sums, peers, out)
     embed_sq = total[1:2, :]
     scale = lax.rsqrt(total[0:1, :] * (1.0 / D) + epsilon)
-    for copy in loads[:4]:
-        copy.wait()
-
-    def project(i, _):
-        span = pl.ds(pl.multiple_of(i * 256, 256), 256)
-        paired[span, :] = scale * lax.dot_general(win[:, span], wide[...], TN, preferred_element_type=f32)
-        return 0
-
-    lax.fori_loop(0, 2, project, 0)
-    blocks.relay(0)
-    blocks.relay(2)
-    second.first_near()
-    grouped[...] = scale * lax.dot_general(wgr[...], wide[...], TN, preferred_element_type=f32)
-    raw = scale * jnp.dot(w_st[...], wide[...], preferred_element_type=f32)
-    second.second_near(0)
-    second.first_far()
+    raw = raws[...] * scale
     head = lax.broadcasted_iota(jnp.int32, (HL, STRETCH), 0)
 
     def by_head(ref):
@@ -642,15 +545,16 @@
         by *= 2
     turned = jnp.concatenate([cums, steps, jnp.zeros((128 - 2 * HL, STRETCH), f32)], axis=0).T
     group = lax.div(me, 8)
-    b_proj = grouped[pl.ds(pl.multiple_of(group * NS, NS), NS), :]
-    c_proj = grouped[pl.ds(pl.multiple_of(G * NS + group * NS, NS), NS), :]
+    b_proj = scale * grouped[pl.ds(pl.multiple_of(group * NS, NS), NS), :]
+    c_proj = scale * grouped[pl.ds(pl.multiple_of(G * NS + group * NS, NS), NS), :]
     pairs = lax.dot_general(b_proj.astype(bf16), c_proj.astype(bf16), TN, preferred_element_type=f32)
     src = lax.broadcasted_iota(jnp.int32, pairs.shape, 0)
     dst = lax.broadcasted_iota(jnp.int32, pairs.shape, 1)
     pairs = jnp.where(src <= dst, pairs, 0.0)
 
-    for copy in moved:
-        copy.wait_recv()
+    for copy in loads[2:4]:
+        copy.wait()
+    wait_states()
     slot = slots[seq]
     for h in range(HL):
         for i in range(32):
@@ -667,11 +571,12 @@
         before = jnp.where(lane == 125 + k, turn_row, before)
     taps = [flat(conv_w[k : k + 1, :], HL * P_SIZE) for k in range(CONV)]
     mixing = flat(mix_g[...], HL * P_SIZE)
+    second.first_near()
     square = jnp.zeros((1, STRETCH), f32)
     for h in range(HL):
         chan = slice(h * P_SIZE, (h + 1) * P_SIZE)
-        gate = paired[h * 128 : h * 128 + 64, :]
-        signal = paired[h * 128 + 64 : h * 128 + 128, :]
+        gate = scale * paired[h * 128 : h * 128 + 64, :]
+        signal = scale * paired[h * 128 + 64 : h * 128 + 128, :]
         padded = jnp.concatenate([before[chan], signal], axis=1)
         conv = taps[CONV - 1][chan] * signal
         for back in range(1, CONV):
@@ -693,8 +598,8 @@
         final_out[chan, :] = jnp.exp(last) * init + lax.dot_general(
             active * to_end, b_proj, NT, precision=highest, preferred_element_type=f32
         )
-        if h:
-            second.second_near(h)
+        if h == 1:
+            second.second_near(0)
     squares[...] = jnp.broadcast_to(square, (8, STRETCH))
     group = lax.div(me, 8)
     spot = lax.rem(me, 8)
@@ -706,31 +611,19 @@
         )
         copy.start()
         met.append(copy)
-    for k in range(SIDE):
-        second.second_far(k)
-    blocks.relay(1)
-    blocks.relay(3)
+    second.first_far()
     total = square
     for by in range(1, 8):
         met[by - 1].wait_recv()
         total = total + peers3[by - 1, 0:1, :]
     scale = lax.rsqrt(total * (1.0 / (MH // G * P_SIZE)) + epsilon)
-    products(weight, (gained[...] * scale).astype(bf16), part)
     scatter = Scatter(part, near1, full1, mid, near2, full2, x_send, x_recv)
-    for k in (3, 2, 1, 0):
-        scatter.one(k)
-    for k in (3, 2, 1, 0):
-        scatter.two(k)
-    loads[4].wait()
-    acc[...] = jnp.dot(watt[:, D:], emb[...], preferred_element_type=f32)
-    scatter.three(3)
-    scatter.three(2)
-    for ch in range(CHUNKS):
-        blocks.rest(ch)
-    scatter.four(2)
-    scatter.three(1)
-    scatter.four(1)
-    scatter.three(0)
+    scatter.run(
+        weight, (gained[...] * scale).astype(bf16),
+        [lambda: second.second_near(1)],
+        [lambda: second.second_near(2), lambda: blocks.relay(1), lambda: blocks.relay(3),
+         lambda: blocks.spread(3, 1), lambda: second.second_near(3)],
+    )
     gain = column(gain_sh, me * SHARD, SHARD)
     mine = pl.ds(pl.multiple_of(me * SHARD, 16), SHARD)
     sq = jnp.zeros((1, STRETCH), f32)
@@ -746,23 +639,31 @@
     gather.start()
     sent = send_sums(sums2, peers2, r_send, r_recv)
     wide2[mine, :] = rounded[...]
-    gather.first_near()
-    gather.second_near(0)
-    gather.first_far()
-    for k in (1, 2, 3):
-        gather.second_near(k)
-    for ch in range(CHUNKS):
-        blocks.far(ch)
+    loads[4].wait()
     for k in range(SIDE):
-        gather.second_far(k)
+        second.second_far(k)
+    acc[...] = jnp.dot(watt[:, D:], emb[...], preferred_element_type=f32)
+
+    def attend_rows(by):
+        span = row_of(by)
+        acc[...] += jnp.dot(watt[:, span], wide2[span, :], preferred_element_type=f32)
+
+    gather.run(attend_rows, lambda: None)
     total = add_sums(sums2, peers2, sent)[0:1, :] + embed_sq
     scale = lax.rsqrt(total * (0.5 / D) + epsilon)
-    value = acc[...] + jnp.dot(watt[:, :D], wide2[...], preferred_element_type=f32)
+    value = acc[...]
+    mine_q[...] = (value[:HD] * scale).astype(bf16)
+    swap = pltpu.make_async_remote_copy(
+        src_ref=mine_q, dst_ref=other_out, send_sem=v_send, recv_sem=v_recv,
+        device_id={"seq": x * 2 + 1 - core}, device_id_type=MESH,
+    )
+    swap.start()
     proj_out[...] = (value * scale).astype(bf16)
     gather.finish()
     scatter.finish()
     loads[5].wait()
     blocks.finish()
+    swap.wait()
     first.finish()
     second.finish()
     for copy in out + moved + met + sent:
@@ -780,10 +681,11 @@
             jax.ShapeDtypeStruct((SHARD, STRETCH), f32),
             jax.ShapeDtypeStruct((3 * HD, STRETCH), bf16),
             jax.ShapeDtypeStruct((HL * P_SIZE, NS), f32),
-            jax.ShapeDtypeStruct((SEQ * BLOCKS, 2, HD, BLOCK), bf16),
+            jax.ShapeDtypeStruct((SIDE * BLOCKS, 2, HD, BLOCK), bf16),
+            jax.ShapeDtypeStruct((HD, STRETCH), bf16),
         ),
         in_specs=[anywhere] * 6 + [smem] + [anywhere] * 2 + [vmem] + [smem] * 3 + [anywhere] * 5,
-        out_specs=(vmem, vmem, vmem, anywhere),
+        out_specs=(vmem, vmem, vmem, anywhere, anywhere),
         scratch_shapes=[
             pltpu.VMEM((SHARD, STRETCH), bf16),
             pltpu.VMEM((SHARD, STRETCH), bf16),
@@ -820,8 +722,12 @@
             dma((SEQ - 1,)), dma((SEQ - 1,)),
             dma((7,)), dma((7,)),
             dma((HEADS - 1,)), dma((HEADS - 1,)),
-            dma((28,)), dma((28,)),
+            dma((12,)), dma((12,)),
             dma((6,)), dma((7,)),
+            pltpu.VMEM((HL, STRETCH), f32),
+            pltpu.VMEM((HD, STRETCH), bf16),
+            dma,
+            dma,
         ],
         compiler_params=pltpu.CompilerParams(
             collective_id=0, has_side_effects=True, vmem_limit_bytes=60 * 2**20
@@ -830,58 +736,143 @@
     )(*args)
 
 
-def merge_kernel(attended, weight, before, out,
-                 part, near1, full1, mid, near2, full2, s_send, s_recv):
+def merge_kernel(own_part, other_part, weight, before, out,
+                 part, near1, full1, mid, near2, full2, s_send, s_recv, got, v_send, v_recv):
     barrier = greet_heads()
-    products(weight, attended[...], part)
-    pl.semaphore_wait(barrier, HEADS - 1)
+    seq = lax.axis_index("seq")
+    to = {"seq": seq + 1 - 2 * lax.rem(seq, 2)}
+    pl.semaphore_signal(barrier, inc=1, device_id=to, device_id_type=MESH)
+    pl.semaphore_wait(barrier, HEADS)
+    swap = pltpu.make_async_remote_copy(
+        src_ref=other_part, dst_ref=got, send_sem=v_send, recv_sem=v_recv, device_id=to, device_id_type=MESH
+    )
+    swap.start()
+    swap.wait()
+    scale = HD ** -0.5 * 1.4426950408889634
+    high = jnp.maximum(own_part[HD : HD + 1, :], got[HD : HD + 1, :])
+    one = jnp.exp2((own_part[HD : HD + 1, :] - high) * scale)
+    two = jnp.exp2((got[HD : HD + 1, :] - high) * scale)
+    total = own_part[HD + 1 : HD + 2, :] * one + got[HD + 1 : HD + 2, :] * two
+    attended = ((own_part[:HD, :] * one + got[:HD, :] * two) / total).astype(bf16)
     scatter = Scatter(part, near1, full1, mid, near2, full2, s_send, s_recv)
-    scatter.run()
+    scatter.run(weight, attended)
     for half in (0, 1):
         rows = pl.ds(half * HALF, HALF)
         out[rows, :] = before[rows, :] + scatter.result(half)
     scatter.finish()
 
 
-def merge_call(attended, weight, before):
+def merge_call(own_part, other_part, weight, before):
     vmem = pl.BlockSpec(memory_space=pltpu.VMEM)
     return pl.pallas_call(
         merge_kernel,
         out_shape=jax.ShapeDtypeStruct((SHARD, STRETCH), f32),
-        in_specs=[vmem] * 3,
+        in_specs=[vmem] * 4,
         out_specs=vmem,
-        scratch_shapes=SCATTER_SCRATCH,
+        scratch_shapes=SCATTER_SCRATCH + [
+            pltpu.VMEM((PARTS, STRETCH), f32), pltpu.SemaphoreType.DMA, pltpu.SemaphoreType.DMA
+        ],
         compiler_params=pltpu.CompilerParams(
             collective_id=2, has_side_effects=True, vmem_limit_bytes=40 * 2**20
         ),
         name="merge_rows",
-    )(attended, weight, before)
+    )(own_part, other_part, weight, before)
 
 
 def turn(value):
     return jnp.concatenate([value, jnp.zeros((256 - HD, STRETCH), f32)], axis=0).T[:, :HD]
 
 
-def attend_kernel(table, lengths, projected, pool, out, held, sems, acc, top, total):
+PARTS = 256
+
+
+def attend_kernel(table, lengths, projected, other, pool, own_out, other_out, held, sems, acc, top, total, ids):
     seq = lax.axis_index("seq")
+    core = lax.rem(seq, 2)
     scale = HD ** -0.5 * 1.4426950408889634
     span = STEPB * BLOCK
-    limit = lengths[seq]
-    blocks = lax.div(limit + BLOCK - 1, BLOCK)
-    steps = lax.div(blocks + STEPB - 1, STEPB)
-
-    def fetch(step, slot):
+
+    def listing(which, request):
+        limit = lengths[request]
+        count = lax.div(limit + BLOCK - 1, BLOCK)
+
+        def look(j, found):
+            block = table[request, j]
+            holder = lax.div(block, BLOCKS)
+            ids[which, found] = lax.div(holder, 2) * BLOCKS + lax.rem(block, BLOCKS)
+            return found + (lax.rem(holder, 2) == core).astype(jnp.int32)
+
+        found = lax.fori_loop(0, count, look, 0)
+        for i in range(STEPB):
+            ids[which, found + i] = 0
+        last = lax.rem(lax.div(table[request, count - 1], BLOCKS), 2) == core
+        return found * BLOCK - jnp.where(last, count * BLOCK - limit, 0)
+
+    def fetch(which, step, slot):
         return [
             pltpu.make_async_copy(
-                pool.at[table[seq, step * STEPB + i]],
-                held.at[slot, :, :, pl.ds(i * BLOCK, BLOCK)],
-                sems.at[slot, i],
+                pool.at[ids[which, step * STEPB + i]],
+                held.at[which, slot, :, :, pl.ds(i * BLOCK, BLOCK)],
+                sems.at[which, slot, i],
             )
             for i in range(STEPB)
         ]
 
-    for copy in fetch(0, 0):
-        copy.start()
+    def begin(which, request):
+        keys = listing(which, request)
+
+        @pl.when(keys > 0)
+        def _():
+            for copy in fetch(which, 0, 0):
+                copy.start()
+
+        return keys
+
+    def prefix(which, keys, q):
+        steps = lax.div(keys + span - 1, span)
+
+        def step_body(step, _):
+            slot = lax.rem(step, 2)
+
+            @pl.when(step + 1 < steps)
+            def _():
+                for copy in fetch(which, step + 1, 1 - slot):
+                    copy.start()
+
+            for copy in fetch(which, step, slot):
+                copy.wait()
+            scores = jnp.dot(q, held[which, slot, 0], preferred_element_type=f32)
+
+            def rest(scores):
+                old = top[...]
+                high = jnp.maximum(old, jnp.max(scores, axis=1, keepdims=True))
+                weights = jnp.exp2((scores - high) * scale)
+                factor = jnp.exp2((old - high) * scale)
+                top[...] = high
+                total[...] = total[...] * factor + jnp.sum(weights, axis=1, keepdims=True)
+                acc[...] = acc[...] * factor + lax.dot_general(
+                    weights.astype(bf16), held[which, slot, 1], NT, preferred_element_type=f32
+                )
+
+            @pl.when((step + 1) * span <= keys)
+            def _():
+                rest(scores)
+
+            @pl.when((step + 1) * span > keys)
+            def _():
+                where = step * span + lax.broadcasted_iota(jnp.int32, scores.shape, 1)
+                rest(jnp.where(where < keys, scores, masked))
+
+            return 0
+
+        lax.fori_loop(0, steps, step_body, 0)
+
+    def result():
+        fill = jnp.zeros((STRETCH, PARTS - HD - 2), f32)
+        return jnp.concatenate([acc[...], top[...], total[...], fill], axis=1).T
+
+    own_keys = begin(0, seq)
+    other_keys = begin(1, seq + 1 - 2 * core)
     q = turn(projected[:HD, :].astype(f32)).astype(bf16)
     scores = jnp.dot(q, projected[HD : 2 * HD, :], preferred_element_type=f32)
     row = lax.broadcasted_iota(jnp.int32, scores.shape, 0)
@@ -894,79 +885,48 @@
     acc[...] = lax.dot_general(
         weights.astype(bf16), projected[2 * HD :, :], NT, preferred_element_type=f32
     )
-
-    def step_body(step, _):
-        slot = lax.rem(step, 2)
-
-        @pl.when(step + 1 < steps)
-        def _():
-            for copy in fetch(step + 1, 1 - slot):
-                copy.start()
-
-        for copy in fetch(step, slot):
-            copy.wait()
-        scores = jnp.dot(q, held[slot, 0], preferred_element_type=f32)
-
-        def rest(scores):
-            old = top[...]
-            high = jnp.maximum(old, jnp.max(scores, axis=1, keepdims=True))
-            weights = jnp.exp2((scores - high) * scale)
-            factor = jnp.exp2((old - high) * scale)
-            top[...] = high
-            total[...] = total[...] * factor + jnp.sum(weights, axis=1, keepdims=True)
-            acc[...] = acc[...] * factor + lax.dot_general(
-                weights.astype(bf16), held[slot, 1], NT, preferred_element_type=f32
-            )
-
-        @pl.when((step + 1) * span <= limit)
-        def _():
-            rest(scores)
-
-        @pl.when((step + 1) * span > limit)
-        def _():
-            where = step * span + lax.broadcasted_iota(jnp.int32, scores.shape, 1)
-            rest(jnp.where(where < limit, scores, masked))
-
-        return 0
-
-    lax.fori_loop(0, steps, step_body, 0)
-    value = acc[...] / total[...]
-    value = jnp.concatenate([value, jnp.zeros((STRETCH, 256 - HD), f32)], axis=1).T
-    out[...] = value[:HD].astype(bf16)
-
-
-def attend_call(table, lengths, projected, pool):
+    prefix(0, own_keys, q)
+    own_out[...] = result()
+    top[...] = jnp.full_like(top, masked)
+    total[...] = jnp.zeros_like(total)
+    acc[...] = jnp.zeros_like(acc)
+    prefix(1, other_keys, turn(other[...].astype(f32)).astype(bf16))
+    other_out[...] = result()
+
+
+def attend_call(table, lengths, projected, other, pool):
     vmem = pl.BlockSpec(memory_space=pltpu.VMEM)
     smem = pl.BlockSpec(memory_space=pltpu.SMEM)
     return pl.pallas_call(
         attend_kernel,
-        out_shape=jax.ShapeDtypeStruct((HD, STRETCH), bf16),
-        in_specs=[smem, smem, vmem, pl.BlockSpec(memory_space=pl.ANY)],
-        out_specs=vmem,
+        out_shape=(jax.ShapeDtypeStruct((PARTS, STRETCH), f32),) * 2,
+        in_specs=[smem, smem, vmem, vmem, pl.BlockSpec(memory_space=pl.ANY)],
+        out_specs=(vmem, vmem),
         scratch_shapes=[
-            pltpu.VMEM((2, 2, HD, STEPB * BLOCK), bf16),
-            pltpu.SemaphoreType.DMA((2, STEPB)),
+            pltpu.VMEM((2, 2, 2, HD, STEPB * BLOCK), bf16),
+            pltpu.SemaphoreType.DMA((2, 2, STEPB)),
             pltpu.VMEM((STRETCH, HD), f32),
             pltpu.VMEM((STRETCH, 1), f32),
             pltpu.VMEM((STRETCH, 1), f32),
+            pltpu.SMEM((2, MAXB + STEPB), jnp.int32),
         ],
         compiler_params=pltpu.CompilerParams(vmem_limit_bytes=48 * 2**20),
         name="attend_rows",
-    )(table, lengths, projected, pool)
+    )(table, lengths, projected, other, pool)
 
 
 def body(hidden, embedding, input_gain, w_input, w_groups, w_step, step_bias, decay_rate, skip_gain,
          conv_weight, mix_gain, w_output, state_store, conv_store, state_slot, prefix_len, block_table,
          shared_gain, w_attend, cache_pool, w_merge):
     heads_local = w_step.shape[1]
-    hidden_next, projected, final_state, pool = front_call(
+    hidden_next, projected, final_state, pool, other = front_call(
         hidden.T, embedding.T, input_gain.reshape(D // 128, 128), shared_gain.reshape(2 * D // 128, 128),
         state_store, conv_store.transpose(1, 0, 2).astype(f32), state_slot, w_input, w_groups, w_step.T,
         step_bias, decay_rate, skip_gain, conv_weight, mix_gain[None, :], w_output, w_attend.T,
         cache_pool.transpose(0, 1, 3, 2),
     )
-    attended = attend_call(block_table, prefix_len, projected, pool)
-    layer_output = merge_call(attended, w_merge, hidden_next)
+    own_part, other_part = attend_call(block_table, prefix_len, projected, other, pool)
+    layer_output = merge_call(own_part, other_part, w_merge, hidden_next)
     return (layer_output.T, final_state.reshape(1, heads_local, P_SIZE * NS))
 
 

time: 149 us -> 149 us (level)
  the two profiles are of different devices: /device:TPU:0 before, /device:TPU:6 now
where the time goes in v5:
time: 149 us
  Pallas kernels  143 us (96%)
  local copies, waits for them, and re-layouts  3.55 us (2%)
    pallas_call x1, Pallas kernels, front_call(): pl.pallas_call(front_kernel, out_shape=(jax.ShapeDtypeStruct((SHARD, STRE...  101 us
    pallas_call x1, Pallas kernels, merge_call(): pl.pallas_call(merge_kernel, out_shape=jax.ShapeDtypeStruct((SHARD, STRET...  30.3 us
    pallas_call x1, Pallas kernels, attend_call(): pl.pallas_call(attend_kernel, out_shape=(jax.ShapeDtypeStruct((PARTS, STR...  12 us

profile of v5, /device:TPU:6, one launch (start us, length us, event | category | flops | bytes accessed | tf_op | source)
XLA Modules:
  0.0 148.9 jit_solution(7220593647180808895)
XLA Ops:
  0.6 1.3 convert_bitcast_fusion.tails
  1.9 0.0 copy-start.4
  1.9 0.0 copy-start.5
  1.9 101.1 %front_rows.1 = (f32[224,512]{1,0:T(8,128)}, bf16[672,512]{1,0:T(8,128)(2,1)}, f32[256,64]{1,0:T(8,128)}, bf16[80,2,224,128]{3,2,1,0:T(8,128)(2,1)}, bf16[224,512]{1,0:T(8,128)(2,1)}) custom-call(bf16[224,512]{1,0:T(8,128)(2,1)} %bitcast.14, bf16[224,512]{1,0:T(8,128)(2,1)} %bitcast.15, f32[28,128]{1,0:T(8,128)} %bitcast.18, f32[56,128]{1,0:T(8,128)} %bitcast.16, ...), custom_call_target="tpu_custom_call" | custom-call | tf_op jit(solution)/shard_map/front_rows/pallas_call | solution.py:678
  103.0 0.0 copy-done.4
  103.0 0.0 copy-done.5
  103.0 0.0 copy-start.1
  103.0 1.1 copy-done.1
  104.1 0.0 copy-start.3
  104.1 0.9 copy-done.3
  105.0 0.0 copy-start
  105.0 0.0 copy-start.2
  105.0 12.0 %attend_rows.1 = (f32[256,512]{1,0:T(8,128)S(1)}, f32[256,512]{1,0:T(8,128)S(1)}) custom-call(s32[8,64]{1,0:T(8,128)S(1)} %copy-done.4, s32[8]{0:T(128)S(1)} %copy-done.5, bf16[672,512]{1,0:T(8,128)(2,1)S(1)} %copy-done.1, bf16[224,512]{1,0:T(8,128)(2,1)S(1)} %copy-done.3, bf16[80,2,224,128]{3,2,1,0:T(8,128)(2,1)} %get-tuple-element.11.pool), custom_call_target="tpu_custom_call" | custom-call | tf_op jit(solution)/shard_map/attend_rows/pallas_call | solution.py:900
  117.0 0.0 copy-start.6
  117.0 0.0 copy-done
  117.0 0.0 copy-done.2
  117.0 30.3 %merge_rows.1 = f32[224,512]{1,0:T(8,128)S(1)} custom-call(f32[256,512]{1,0:T(8,128)S(1)} %get-tuple-element.12.own_part, f32[256,512]{1,0:T(8,128)S(1)} %get-tuple-element.13.other_part, bf16[224,3584]{1,0:T(8,128)(2,1)S(1)} %copy-done, f32[224,512]{1,0:T(8,128)S(1)} %copy-done.2), custom_call_target="tpu_custom_call" | custom-call | tf_op jit(solution)/shard_map/merge_rows/pallas_call | solution.py:767
  147.4 0.0 copy-done.6
  147.4 0.7 reshape.15
  148.1 0.8 copy.24
Async XLA Ops:
  1.9 101.1 %copy-start.4 = (s32[8,64]{1,0:T(8,128)S(1)}, s32[8,64]{1,0:T(8,128)}, u32[]{:S(2)}) copy-start(s32[8,64]{1,0:T(8,128)} %table.1) | copy-start | bytes 6148
  1.9 101.1 %copy-start.5 = (s32[8]{0:T(128)S(1)}, s32[8]{0:T(128)}, u32[]{:S(2)}) copy-start(s32[8]{0:T(128)} %lengths.1) | copy-start | bytes 100
  103.0 1.1 copy-start.1
  104.1 0.9 copy-start.3
  105.0 12.0 %copy-start = (bf16[224,3584]{1,0:T(8,128)(2,1)S(1)}, bf16[224,3584]{1,0:T(8,128)(2,1)}, u32[]{:S(2)}) copy-start(bf16[224,3584]{1,0:T(8,128)(2,1)} %weight.1) | copy-start | bytes 4816900
  105.0 12.0 %copy-start.2 = (f32[224,512]{1,0:T(8,128)S(1)}, f32[224,512]{1,0:T(8,128)}, u32[]{:S(2)}) copy-start(f32[224,512]{1,0:T(8,128)} %get-tuple-element.14.before) | copy-start | bytes 1376260
  117.0 30.4 %copy-start.6 = (f32[256,64]{1,0:T(8,128)S(1)}, f32[256,64]{1,0:T(8,128)}, u32[]{:S(2)}) copy-start(f32[256,64]{1,0:T(8,128)} %get-tuple-element.15) | copy-start | bytes 196612

commit v6 on v5

--- a/solution.py
+++ b/solution.py
@@ -363,62 +363,87 @@
         self.x, self.core = lax.div(seq, 2), lax.rem(seq, 2)
         self.sent = []
 
-    def slab(self, by, ch):
+    def slab(self, by, core, ch):
         per = BLOCKS // CHUNKS
-        return self.out.at[pl.ds(around(self.x, by) * BLOCKS + ch * per, per)]
-
-    def copy(self, idx, src, dst, by):
+        return self.out.at[pl.ds((around(self.x, by) * 2 + core) * BLOCKS + ch * per, per)]
+
+    def copy(self, idx, src, dst, by, core):
         return pltpu.make_async_remote_copy(
             src_ref=src, dst_ref=dst, send_sem=self.ss.at[idx], recv_sem=self.rs.at[idx],
-            device_id={"seq": around(self.x, by) * 2 + self.core}, device_id_type=MESH,
+            device_id={"seq": around(self.x, by) * 2 + core}, device_id_type=MESH,
         )
 
-    def go(self, idx, src, dst, by):
-        copy = self.copy(idx, src, dst, by)
+    def go(self, idx, src, dst, by, core):
+        copy = self.copy(idx, src, dst, by, core)
         copy.start()
         self.sent.append(copy)
 
     def arrive(self, idx, dst):
-        self.copy(idx, dst, dst, 1).wait_recv()
+        self.copy(idx, dst, dst, 1, self.core).wait_recv()
 
     def spread(self, right, left):
         per = BLOCKS // CHUNKS
         for base, ch, by in ((0, right, 1), (4, left, -1)):
-            self.go(base + ch, self.own.at[pl.ds(ch * per, per)], self.slab(0, ch), by)
+            self.go(base + ch, self.own.at[pl.ds(ch * per, per)], self.slab(0, self.core, ch), by, self.core)
+
+    def start(self):
+        per = BLOCKS // CHUNKS
+        self.spread(0, 2)
+        for ch in range(CHUNKS):
+            self.go(12 + ch, self.own.at[pl.ds(ch * per, per)], self.slab(0, self.core, ch), 0, 1 - self.core)
+
+    def share(self, j, by, ch):
+        where = self.slab(by, self.core, ch)
+        self.go(12 + 4 * j + ch, where, where, 0, 1 - self.core)
 
     def relay(self, ch):
-        way = -1 if ch < 2 else 1
-        where = self.slab(way, ch)
-        self.arrive(ch if ch < 2 else 4 + ch, where)
-        self.go(8 + ch, where, where, -way)
+        left = self.slab(-1, self.core, ch)
+        right = self.slab(1, self.core, ch)
+        if ch < 2:
+            self.arrive(ch, left)
+            self.go(8 + ch, left, left, 1, self.core)
+            self.share(1, -1, ch)
+        else:
+            self.arrive(4 + ch, right)
+            self.go(8 + ch, right, right, -1, self.core)
+            self.share(2, 1, ch)
+
+    def rest(self, ch):
+        if ch < 2:
+            self.arrive(4 + ch, self.slab(1, self.core, ch))
+            self.share(2, 1, ch)
+        else:
+            self.arrive(ch, self.slab(-1, self.core, ch))
+            self.share(1, -1, ch)
+
+    def far(self, ch):
+        self.arrive(8 + ch, self.slab(2, self.core, ch))
+        self.share(3, 2, ch)
 
     def finish(self):
-        for ch in range(CHUNKS):
-            if ch < 2:
-                self.arrive(4 + ch, self.slab(1, ch))
-            else:
-                self.arrive(ch, self.slab(-1, ch))
-            self.arrive(8 + ch, self.slab(2, ch))
+        for j, by in enumerate((0, -1, 1, 2)):
+            for ch in range(CHUNKS):
+                self.arrive(12 + 4 * j + ch, self.slab(by, 1 - self.core, ch))
         for copy in self.sent:
             copy.wait_send()
 
 
-def front_kernel(hidden_in, embed_in, gain_in_in, gain_sh_in, states, tails, slots, w_in, w_gr, w_st, bias, decay,
+def front_kernel(hidden_in, embed_in, gain_in_in, gain_sh_in, states, tails_in, slots, w_in, w_gr, w_st, bias, decay,
                  skip, conv_in, mix_in, w_out_in, w_att, pool_in,
-                 next_out, proj_out, final_out, pool_out, other_out,
+                 next_out, proj_out, final_out, pool_out,
                  hidden, embed, gain_in, gain_sh, conv_w, mix_g, weight,
                  wide, own_h, own_e, win, wgr, paired, grouped, sums, peers, stores, tail_all, lines, gained, watt,
                  emb, wide2, acc, squares, peers3, sums2, peers2, rounded,
                  part, near1, full1, mid, near2, full2, x_send, x_recv,
                  h_send, h_recv, e_send, e_recv, g_send, g_recv, q_send, q_recv, s_send, s_recv, t_send, t_recv,
-                 u_send, u_recv, r_send, r_recv, p_send, p_recv, local, here, raws, mine_q, v_send, v_recv):
+                 u_send, u_recv, r_send, r_recv, p_send, p_recv, local, here, raws, tails_raw, tails):
     seq = lax.axis_index("seq")
     me = lax.axis_index("head")
     small = [
         pltpu.make_async_copy(src, dst, here.at[i])
         for i, (src, dst) in enumerate((
             (hidden_in, hidden), (gain_in_in, gain_in), (embed_in, embed), (gain_sh_in, gain_sh),
-            (conv_in, conv_w), (mix_in, mix_g), (w_out_in, weight),
+            (conv_in, conv_w), (mix_in, mix_g), (w_out_in, weight), (tails_in, tails_raw),
         ))
     ]
     for copy in small:
@@ -427,9 +452,8 @@
         pltpu.make_async_copy(w_in, win, local.at[0]),
         pltpu.make_async_copy(w_gr, wgr, local.at[1]),
         pltpu.make_async_copy(states, stores.at[pl.ds(seq * 2, 2)], local.at[2]),
-        pltpu.make_async_copy(tails, tail_all.at[seq], local.at[3]),
-        pltpu.make_async_copy(w_att, watt, local.at[4]),
-        pltpu.make_async_copy(pool_in, pool_out.at[pl.ds(lax.div(seq, 2) * BLOCKS, BLOCKS)], local.at[5]),
+        pltpu.make_async_copy(w_att, watt, local.at[3]),
+        pltpu.make_async_copy(pool_in, pool_out.at[pl.ds(seq * BLOCKS, BLOCKS)], local.at[4]),
     ]
     for copy in loads:
         copy.start()
@@ -453,13 +477,15 @@
     first.start()
     for copy in small[2:]:
         copy.wait()
+    tails[...] = tails_raw[...].astype(f32)
+    tail_all[seq] = tails[...]
     value = embed[...].astype(f32)
     sq_e = jnp.sum(value * value, axis=0, keepdims=True)
     ready = (value * column(gain_sh, D + me * SHARD, SHARD)).astype(bf16)
     own_e[...] = ready
     emb[mine, :] = ready
-    line = lax.broadcasted_iota(jnp.int32, (8, STRETCH), 0)
-    sums[...] = jnp.where(line == 0, sq_h, jnp.where(line == 1, sq_e, 0.0))
+    sums[0:1, :] = sq_h
+    sums[1:2, :] = sq_e
     out = send_sums(sums, peers, q_send, q_recv)
     x, core = lax.div(seq, 2), lax.rem(seq, 2)
     held = (
@@ -500,7 +526,7 @@
                     device_id={"seq": x * 2 + 1 - core}, device_id_type=MESH,
                 ).wait_recv()
 
-    blocks.spread(0, 2)
+    blocks.start()
     paired[...] = jnp.zeros_like(paired)
     grouped[...] = jnp.zeros_like(grouped)
     raws[...] = jnp.zeros_like(raws)
@@ -552,8 +578,7 @@
     dst = lax.broadcasted_iota(jnp.int32, pairs.shape, 1)
     pairs = jnp.where(src <= dst, pairs, 0.0)
 
-    for copy in loads[2:4]:
-        copy.wait()
+    loads[2].wait()
     wait_states()
     slot = slots[seq]
     for h in range(HL):
@@ -600,7 +625,7 @@
         )
         if h == 1:
             second.second_near(0)
-    squares[...] = jnp.broadcast_to(square, (8, STRETCH))
+    squares[...] = square
     group = lax.div(me, 8)
     spot = lax.rem(me, 8)
     met = []
@@ -634,12 +659,12 @@
         value = value.astype(bf16).astype(f32)
         sq = sq + jnp.sum(value * value, axis=0, keepdims=True)
         rounded[rows, :] = (value * gain[half * HALF : (half + 1) * HALF]).astype(bf16)
-    sums2[...] = jnp.broadcast_to(sq, (8, STRETCH))
+    sums2[...] = sq
     gather = Gather(rounded, wide2, g_send, g_recv)
     gather.start()
     sent = send_sums(sums2, peers2, r_send, r_recv)
     wide2[mine, :] = rounded[...]
-    loads[4].wait()
+    loads[3].wait()
     for k in range(SIDE):
         second.second_far(k)
     acc[...] = jnp.dot(watt[:, D:], emb[...], preferred_element_type=f32)
@@ -648,22 +673,21 @@
         span = row_of(by)
         acc[...] += jnp.dot(watt[:, span], wide2[span, :], preferred_element_type=f32)
 
-    gather.run(attend_rows, lambda: None)
-    total = add_sums(sums2, peers2, sent)[0:1, :] + embed_sq
+    def rest():
+        for ch in range(CHUNKS):
+            blocks.rest(ch)
+
+    gather.run(attend_rows, rest)
+    for ch in range(CHUNKS):
+        blocks.far(ch)
+    total = add_sums(sums2, peers2, sent) + embed_sq
     scale = lax.rsqrt(total * (0.5 / D) + epsilon)
     value = acc[...]
-    mine_q[...] = (value[:HD] * scale).astype(bf16)
-    swap = pltpu.make_async_remote_copy(
-        src_ref=mine_q, dst_ref=other_out, send_sem=v_send, recv_sem=v_recv,
-        device_id={"seq": x * 2 + 1 - core}, device_id_type=MESH,
-    )
-    swap.start()
     proj_out[...] = (value * scale).astype(bf16)
     gather.finish()
     scatter.finish()
-    loads[5].wait()
+    loads[4].wait()
     blocks.finish()
-    swap.wait()
     first.finish()
     second.finish()
     for copy in out + moved + met + sent:
@@ -681,11 +705,10 @@
             jax.ShapeDtypeStruct((SHARD, STRETCH), f32),
             jax.ShapeDtypeStruct((3 * HD, STRETCH), bf16),
             jax.ShapeDtypeStruct((HL * P_SIZE, NS), f32),
-            jax.ShapeDtypeStruct((SIDE * BLOCKS, 2, HD, BLOCK), bf16),
-            jax.ShapeDtypeStruct((HD, STRETCH), bf16),
+            jax.ShapeDtypeStruct((SEQ * BLOCKS, 2, HD, BLOCK), bf16),
         ),
         in_specs=[anywhere] * 6 + [smem] + [anywhere] * 2 + [vmem] + [smem] * 3 + [anywhere] * 5,
-        out_specs=(vmem, vmem, vmem, anywhere, anywhere),
+        out_specs=(vmem, vmem, vmem, anywhere),
         scratch_shapes=[
             pltpu.VMEM((SHARD, STRETCH), bf16),
             pltpu.VMEM((SHARD, STRETCH), bf16),
@@ -701,8 +724,8 @@
             pltpu.VMEM((D, 2 * G * NS), bf16),
             pltpu.VMEM((HL * 128, STRETCH), f32),
             pltpu.VMEM((2 * G * NS, STRETCH), f32),
-            pltpu.VMEM((8, STRETCH), f32),
-            pltpu.VMEM((HEADS - 1, 8, STRETCH), f32),
+            pltpu.VMEM((2, STRETCH), f32),
+            pltpu.VMEM((HEADS - 1, 2, STRETCH), f32),
             pltpu.VMEM((2 * SEQ, HL, P_SIZE * NS), f32),
             pltpu.VMEM((SEQ, CONV - 1, 2, HL * P_SIZE), f32),
             pltpu.VMEM((128, 128), f32),
@@ -711,10 +734,10 @@
             pltpu.VMEM((D, STRETCH), bf16),
             pltpu.VMEM((D, STRETCH), bf16),
             pltpu.VMEM((3 * HD, STRETCH), f32),
-            pltpu.VMEM((8, STRETCH), f32),
-            pltpu.VMEM((7, 8, STRETCH), f32),
-            pltpu.VMEM((8, STRETCH), f32),
-            pltpu.VMEM((HEADS - 1, 8, STRETCH), f32),
+            pltpu.VMEM((1, STRETCH), f32),
+            pltpu.VMEM((7, 1, STRETCH), f32),
+            pltpu.VMEM((1, STRETCH), f32),
+            pltpu.VMEM((HEADS - 1, 1, STRETCH), f32),
             pltpu.VMEM((SHARD, STRETCH), bf16),
         ] + SCATTER_SCRATCH + GATHER_SEMS + GATHER_SEMS + GATHER_SEMS + [
             dma((HEADS - 1,)), dma((HEADS - 1,)),
@@ -722,12 +745,11 @@
             dma((SEQ - 1,)), dma((SEQ - 1,)),
             dma((7,)), dma((7,)),
             dma((HEADS - 1,)), dma((HEADS - 1,)),
-            dma((12,)), dma((12,)),
-            dma((6,)), dma((7,)),
+            dma((28,)), dma((28,)),
+            dma((5,)), dma((8,)),
             pltpu.VMEM((HL, STRETCH), f32),
-            pltpu.VMEM((HD, STRETCH), bf16),
-            dma,
-            dma,
+            pltpu.VMEM((CONV - 1, 2, HL * P_SIZE), bf16),
+            pltpu.VMEM((CONV - 1, 2, HL * P_SIZE), f32),
         ],
         compiler_params=pltpu.CompilerParams(
             collective_id=0, has_side_effects=True, vmem_limit_bytes=60 * 2**20
@@ -736,143 +758,57 @@
     )(*args)
 
 
-def merge_kernel(own_part, other_part, weight, before, out,
-                 part, near1, full1, mid, near2, full2, s_send, s_recv, got, v_send, v_recv):
+def merge_kernel(attended, weight, before, out,
+                 part, near1, full1, mid, near2, full2, s_send, s_recv):
     barrier = greet_heads()
-    seq = lax.axis_index("seq")
-    to = {"seq": seq + 1 - 2 * lax.rem(seq, 2)}
-    pl.semaphore_signal(barrier, inc=1, device_id=to, device_id_type=MESH)
-    pl.semaphore_wait(barrier, HEADS)
-    swap = pltpu.make_async_remote_copy(
-        src_ref=other_part, dst_ref=got, send_sem=v_send, recv_sem=v_recv, device_id=to, device_id_type=MESH
-    )
-    swap.start()
-    swap.wait()
-    scale = HD ** -0.5 * 1.4426950408889634
-    high = jnp.maximum(own_part[HD : HD + 1, :], got[HD : HD + 1, :])
-    one = jnp.exp2((own_part[HD : HD + 1, :] - high) * scale)
-    two = jnp.exp2((got[HD : HD + 1, :] - high) * scale)
-    total = own_part[HD + 1 : HD + 2, :] * one + got[HD + 1 : HD + 2, :] * two
-    attended = ((own_part[:HD, :] * one + got[:HD, :] * two) / total).astype(bf16)
+    pl.semaphore_wait(barrier, HEADS - 1)
     scatter = Scatter(part, near1, full1, mid, near2, full2, s_send, s_recv)
-    scatter.run(weight, attended)
+    scatter.run(weight, attended[...])
     for half in (0, 1):
         rows = pl.ds(half * HALF, HALF)
         out[rows, :] = before[rows, :] + scatter.result(half)
     scatter.finish()
 
 
-def merge_call(own_part, other_part, weight, before):
+def merge_call(attended, weight, before):
     vmem = pl.BlockSpec(memory_space=pltpu.VMEM)
     return pl.pallas_call(
         merge_kernel,
         out_shape=jax.ShapeDtypeStruct((SHARD, STRETCH), f32),
-        in_specs=[vmem] * 4,
+        in_specs=[vmem] * 3,
         out_specs=vmem,
-        scratch_shapes=SCATTER_SCRATCH + [
-            pltpu.VMEM((PARTS, STRETCH), f32), pltpu.SemaphoreType.DMA, pltpu.SemaphoreType.DMA
-        ],
+        scratch_shapes=SCATTER_SCRATCH,
         compiler_params=pltpu.CompilerParams(
             collective_id=2, has_side_effects=True, vmem_limit_bytes=40 * 2**20
         ),
         name="merge_rows",
-    )(own_part, other_part, weight, before)
+    )(attended, weight, before)
 
 
 def turn(value):
     return jnp.concatenate([value, jnp.zeros((256 - HD, STRETCH), f32)], axis=0).T[:, :HD]
 
 
-PARTS = 256
-
-
-def attend_kernel(table, lengths, projected, other, pool, own_out, other_out, held, sems, acc, top, total, ids):
+def attend_kernel(table, lengths, projected, pool, out, held, sems, acc, top, total):
     seq = lax.axis_index("seq")
-    core = lax.rem(seq, 2)
     scale = HD ** -0.5 * 1.4426950408889634
     span = STEPB * BLOCK
-
-    def listing(which, request):
-        limit = lengths[request]
-        count = lax.div(limit + BLOCK - 1, BLOCK)
-
-        def look(j, found):
-            block = table[request, j]
-            holder = lax.div(block, BLOCKS)
-            ids[which, found] = lax.div(holder, 2) * BLOCKS + lax.rem(block, BLOCKS)
-            return found + (lax.rem(holder, 2) == core).astype(jnp.int32)
-
-        found = lax.fori_loop(0, count, look, 0)
-        for i in range(STEPB):
-            ids[which, found + i] = 0
-        last = lax.rem(lax.div(table[request, count - 1], BLOCKS), 2) == core
-        return found * BLOCK - jnp.where(last, count * BLOCK - limit, 0)
-
-    def fetch(which, step, slot):
+    limit = lengths[seq]
+    blocks = lax.div(limit + BLOCK - 1, BLOCK)
+    steps = lax.div(blocks + STEPB - 1, STEPB)
+
+    def fetch(step, slot):
         return [
             pltpu.make_async_copy(
-                pool.at[ids[which, step * STEPB + i]],
-                held.at[which, slot, :, :, pl.ds(i * BLOCK, BLOCK)],
-                sems.at[which, slot, i],
+                pool.at[table[seq, step * STEPB + i]],
+                held.at[slot, :, :, pl.ds(i * BLOCK, BLOCK)],
+                sems.at[slot, i],
             )
             for i in range(STEPB)
         ]
 
-    def begin(which, request):
-        keys = listing(which, request)
-
-        @pl.when(keys > 0)
-        def _():
-            for copy in fetch(which, 0, 0):
-                copy.start()
-
-        return keys
-
-    def prefix(which, keys, q):
-        steps = lax.div(keys + span - 1, span)
-
-        def step_body(step, _):
-            slot = lax.rem(step, 2)
-
-            @pl.when(step + 1 < steps)
-            def _():
-                for copy in fetch(which, step + 1, 1 - slot):
-                    copy.start()
-
-            for copy in fetch(which, step, slot):
-                copy.wait()
-            scores = jnp.dot(q, held[which, slot, 0], preferred_element_type=f32)
-
-            def rest(scores):
-                old = top[...]
-                high = jnp.maximum(old, jnp.max(scores, axis=1, keepdims=True))
-                weights = jnp.exp2((scores - high) * scale)
-                factor = jnp.exp2((old - high) * scale)
-                top[...] = high
-                total[...] = total[...] * factor + jnp.sum(weights, axis=1, keepdims=True)
-                acc[...] = acc[...] * factor + lax.dot_general(
-                    weights.astype(bf16), held[which, slot, 1], NT, preferred_element_type=f32
-                )
-
-            @pl.when((step + 1) * span <= keys)
-            def _():
-                rest(scores)
-
-            @pl.when((step + 1) * span > keys)
-            def _():
-                where = step * span + lax.broadcasted_iota(jnp.int32, scores.shape, 1)
-                rest(jnp.where(where < keys, scores, masked))
-
-            return 0
-
-        lax.fori_loop(0, steps, step_body, 0)
-
-    def result():
-        fill = jnp.zeros((STRETCH, PARTS - HD - 2), f32)
-        return jnp.concatenate([acc[...], top[...], total[...], fill], axis=1).T
-
-    own_keys = begin(0, seq)
-    other_keys = begin(1, seq + 1 - 2 * core)
+    for copy in fetch(0, 0):
+        copy.start()
     q = turn(projected[:HD, :].astype(f32)).astype(bf16)
     scores = jnp.dot(q, projected[HD : 2 * HD, :], preferred_element_type=f32)
     row = lax.broadcasted_iota(jnp.int32, scores.shape, 0)
@@ -885,48 +821,79 @@
     acc[...] = lax.dot_general(
         weights.astype(bf16), projected[2 * HD :, :], NT, preferred_element_type=f32
     )
-    prefix(0, own_keys, q)
-    own_out[...] = result()
-    top[...] = jnp.full_like(top, masked)
-    total[...] = jnp.zeros_like(total)
-    acc[...] = jnp.zeros_like(acc)
-    prefix(1, other_keys, turn(other[...].astype(f32)).astype(bf16))
-    other_out[...] = result()
-
-
-def attend_call(table, lengths, projected, other, pool):
+
+    def step_body(step, _):
+        slot = lax.rem(step, 2)
+
+        @pl.when(step + 1 < steps)
+        def _():
+            for copy in fetch(step + 1, 1 - slot):
+                copy.start()
+
+        for copy in fetch(step, slot):
+            copy.wait()
+        scores = jnp.dot(q, held[slot, 0], preferred_element_type=f32)
+
+        def rest(scores):
+            old = top[...]
+            high = jnp.maximum(old, jnp.max(scores, axis=1, keepdims=True))
+            weights = jnp.exp2((scores - high) * scale)
+            factor = jnp.exp2((old - high) * scale)
+            top[...] = high
+            total[...] = total[...] * factor + jnp.sum(weights, axis=1, keepdims=True)
+            acc[...] = acc[...] * factor + lax.dot_general(
+                weights.astype(bf16), held[slot, 1], NT, preferred_element_type=f32
+            )
+
+        @pl.when((step + 1) * span <= limit)
+        def _():
+            rest(scores)
+
+        @pl.when((step + 1) * span > limit)
+        def _():
+            where = step * span + lax.broadcasted_iota(jnp.int32, scores.shape, 1)
+            rest(jnp.where(where < limit, scores, masked))
+
+        return 0
+
+    lax.fori_loop(0, steps, step_body, 0)
+    value = acc[...] / total[...]
+    value = jnp.concatenate([value, jnp.zeros((STRETCH, 256 - HD), f32)], axis=1).T
+    out[...] = value[:HD].astype(bf16)
+
+
+def attend_call(table, lengths, projected, pool):
     vmem = pl.BlockSpec(memory_space=pltpu.VMEM)
     smem = pl.BlockSpec(memory_space=pltpu.SMEM)
     return pl.pallas_call(
         attend_kernel,
-        out_shape=(jax.ShapeDtypeStruct((PARTS, STRETCH), f32),) * 2,
-        in_specs=[smem, smem, vmem, vmem, pl.BlockSpec(memory_space=pl.ANY)],
-        out_specs=(vmem, vmem),
+        out_shape=jax.ShapeDtypeStruct((HD, STRETCH), bf16),
+        in_specs=[smem, smem, vmem, pl.BlockSpec(memory_space=pl.ANY)],
+        out_specs=vmem,
         scratch_shapes=[
-            pltpu.VMEM((2, 2, 2, HD, STEPB * BLOCK), bf16),
-            pltpu.SemaphoreType.DMA((2, 2, STEPB)),
+            pltpu.VMEM((2, 2, HD, STEPB * BLOCK), bf16),
+            pltpu.SemaphoreType.DMA((2, STEPB)),
             pltpu.VMEM((STRETCH, HD), f32),
             pltpu.VMEM((STRETCH, 1), f32),
             pltpu.VMEM((STRETCH, 1), f32),
-            pltpu.SMEM((2, MAXB + STEPB), jnp.int32),
         ],
         compiler_params=pltpu.CompilerParams(vmem_limit_bytes=48 * 2**20),
         name="attend_rows",
-    )(table, lengths, projected, other, pool)
+    )(table, lengths, projected, pool)
 
 
 def body(hidden, embedding, input_gain, w_input, w_groups, w_step, step_bias, decay_rate, skip_gain,
          conv_weight, mix_gain, w_output, state_store, conv_store, state_slot, prefix_len, block_table,
          shared_gain, w_attend, cache_pool, w_merge):
     heads_local = w_step.shape[1]
-    hidden_next, projected, final_state, pool, other = front_call(
+    hidden_next, projected, final_state, pool = front_call(
         hidden.T, embedding.T, input_gain.reshape(D // 128, 128), shared_gain.reshape(2 * D // 128, 128),
-        state_store, conv_store.transpose(1, 0, 2).astype(f32), state_slot, w_input, w_groups, w_step.T,
+        state_store, conv_store.transpose(1, 0, 2), state_slot, w_input, w_groups, w_step.T,
         step_bias, decay_rate, skip_gain, conv_weight, mix_gain[None, :], w_output, w_attend.T,
         cache_pool.transpose(0, 1, 3, 2),
     )
-    own_part, other_part = attend_call(block_table, prefix_len, projected, other, pool)
-    layer_output = merge_call(own_part, other_part, w_merge, hidden_next)
+    attended = attend_call(block_table, prefix_len, projected, pool)
+    layer_output = merge_call(attended, w_merge, hidden_next)
     return (layer_output.T, final_state.reshape(1, heads_local, P_SIZE * NS))
 
 

time: 149 us -> 140 us (0.940)
  the two profiles are of different devices: /device:TPU:6 before, /device:TPU:0 now
where the time goes in v6:
time: 140 us; the launch traced here: 137 us
  Pallas kernels  134 us (96%)
  local copies, waits for them, and re-layouts  2.62 us (2%)
    pallas_call x1, Pallas kernels, front_call(): pl.pallas_call(front_kernel, out_shape=(jax.ShapeDtypeStruct((SHARD, STRE...  104 us
    pallas_call x1, Pallas kernels, merge_call(): pl.pallas_call(merge_kernel, out_shape=jax.ShapeDtypeStruct((SHARD, STRET...  26.3 us
    pallas_call x1, Pallas kernels, attend_call(): pl.pallas_call(attend_kernel, out_shape=jax.ShapeDtypeStruct((HD, STRETCH...  3.8 us

profile of v6, /device:TPU:0, one launch (start us, length us, event | category | flops | bytes accessed | tf_op | source)
XLA Modules:
  0.0 137.3 jit_solution(2414208557852131395)
XLA Ops:
  0.6 0.0 copy-start.3
  0.6 0.0 copy-start.4
  0.7 103.9 %front_rows.1 = (f32[224,512]{1,0:T(8,128)}, bf16[672,512]{1,0:T(8,128)(2,1)}, f32[256,64]{1,0:T(8,128)}, bf16[160,2,224,128]{3,2,1,0:T(8,128)(2,1)}) custom-call(bf16[224,512]{1,0:T(8,128)(2,1)} %bitcast.13, bf16[224,512]{1,0:T(8,128)(2,1)} %bitcast.14, f32[28,128]{1,0:T(8,128)} %bitcast.17, f32[56,128]{1,0:T(8,128)} %bitcast.15, f32[2,4,4096]{2,1,0:T(4,128)} %states.1, ...), custom_call_target="tpu_custom_call" | custom-call | tf_op jit(solution)/shard_map/front_rows/pallas_call | solution.py:702
  104.6 0.0 copy-done.3
  104.6 0.0 copy-done.4
  104.6 0.0 copy-start.1
  104.6 1.1 copy-done.1
  105.7 0.0 copy-start
  105.7 0.0 copy-start.2
  105.7 3.8 %attend_rows.1.attended = bf16[224,512]{1,0:T(8,128)(2,1)S(1)} custom-call(s32[8,64]{1,0:T(8,128)S(1)} %copy-done.3, s32[8]{0:T(128)S(1)} %copy-done.4, bf16[672,512]{1,0:T(8,128)(2,1)S(1)} %copy-done.1, bf16[160,2,224,128]{3,2,1,0:T(8,128)(2,1)} %get-tuple-element.7.pool), custom_call_target="tpu_custom_call" | custom-call | tf_op jit(solution)/shard_map/attend_rows/pallas_call | solution.py:868
  109.5 0.0 copy-done
  109.5 0.0 copy-done.2
  109.6 0.0 copy-start.5
  109.6 26.3 %merge_rows.1 = f32[224,512]{1,0:T(8,128)S(1)} custom-call(bf16[224,512]{1,0:T(8,128)(2,1)S(1)} %attend_rows.1.attended, bf16[224,3584]{1,0:T(8,128)(2,1)S(1)} %copy-done, f32[224,512]{1,0:T(8,128)S(1)} %copy-done.2), custom_call_target="tpu_custom_call" | custom-call | tf_op jit(solution)/shard_map/merge_rows/pallas_call | solution.py:775
  135.8 0.0 copy-done.5
  135.8 0.7 reshape.15
  136.6 0.8 copy.24
Async XLA Ops:
  0.6 104.0 %copy-start.3 = (s32[8,64]{1,0:T(8,128)S(1)}, s32[8,64]{1,0:T(8,128)}, u32[]{:S(2)}) copy-start(s32[8,64]{1,0:T(8,128)} %table.1) | copy-start | bytes 6148
  0.6 104.0 %copy-start.4 = (s32[8]{0:T(128)S(1)}, s32[8]{0:T(128)}, u32[]{:S(2)}) copy-start(s32[8]{0:T(128)} %lengths.1) | copy-start | bytes 100
  104.6 1.1 copy-start.1
  105.7 3.8 %copy-start = (bf16[224,3584]{1,0:T(8,128)(2,1)S(1)}, bf16[224,3584]{1,0:T(8,128)(2,1)}, u32[]{:S(2)}) copy-start(bf16[224,3584]{1,0:T(8,128)(2,1)} %weight.1) | copy-start | bytes 4816900
  105.7 3.8 %copy-start.2 = (f32[224,512]{1,0:T(8,128)S(1)}, f32[224,512]{1,0:T(8,128)}, u32[]{:S(2)}) copy-start(f32[224,512]{1,0:T(8,128)} %get-tuple-element.8.before) | copy-start | bytes 1376260
  109.6 26.3 %copy-start.5 = (f32[256,64]{1,0:T(8,128)S(1)}, f32[256,64]{1,0:T(8,128)}, u32[]{:S(2)}) copy-start(f32[256,64]{1,0:T(8,128)} %get-tuple-element.9) | copy-start | bytes 196612

commit v7 on v6

--- a/solution.py
+++ b/solution.py
@@ -250,10 +250,14 @@
             self.go(half, 18 + way, self.mid.at[half, k], self.full2.at[half, way], around(c1, OFFSETS[k]), c2)
 
     def run(self, weight, rows, early=(), late=()):
-        for by in (2, -1, 1, 0):
-            products(weight, rows, self.part, by)
-        for k in (3, 2, 1, 0):
-            self.one(k, (0, 1))
+        products(weight, rows, self.part, 2)
+        self.one(3, (0, 1))
+        products(weight, rows, self.part, 1)
+        self.one(2, (0, 1))
+        products(weight, rows, self.part, -1)
+        self.one(1, (0, 1))
+        products(weight, rows, self.part, 0)
+        self.one(0, (0, 1))
         for step in early:
             step()
         self.two(3)

time: 140 us -> 140 us (level)
  the two profiles are of different devices: /device:TPU:0 before, /device:TPU:5 now
where the time goes in v7:
time: 140 us; the launch traced here: 139 us
  Pallas kernels  136 us (97%)
  local copies, waits for them, and re-layouts  2.62 us (2%)
    pallas_call x1, Pallas kernels, front_call(): pl.pallas_call(front_kernel, out_shape=(jax.ShapeDtypeStruct((SHARD, STRE...  103 us
    pallas_call x1, Pallas kernels, merge_call(): pl.pallas_call(merge_kernel, out_shape=jax.ShapeDtypeStruct((SHARD, STRET...  20.1 us
    pallas_call x1, Pallas kernels, attend_call(): pl.pallas_call(attend_kernel, out_shape=jax.ShapeDtypeStruct((HD, STRETCH...  13 us

profile of v7, /device:TPU:5, one launch (start us, length us, event | category | flops | bytes accessed | tf_op | source)
XLA Modules:
  0.0 139.3 jit_solution(11968089768484828637)
XLA Ops:
  0.6 0.0 copy-start.3
  0.6 0.0 copy-start.4
  0.7 102.8 %front_rows.1 = (f32[224,512]{1,0:T(8,128)}, bf16[672,512]{1,0:T(8,128)(2,1)}, f32[256,64]{1,0:T(8,128)}, bf16[160,2,224,128]{3,2,1,0:T(8,128)(2,1)}) custom-call(bf16[224,512]{1,0:T(8,128)(2,1)} %bitcast.13, bf16[224,512]{1,0:T(8,128)(2,1)} %bitcast.14, f32[28,128]{1,0:T(8,128)} %bitcast.17, f32[56,128]{1,0:T(8,128)} %bitcast.15, f32[2,4,4096]{2,1,0:T(4,128)} %states.1, ...), custom_call_target="tpu_custom_call" | custom-call | tf_op jit(solution)/shard_map/front_rows/pallas_call | solution.py:706
  103.5 0.0 copy-done.3
  103.5 0.0 copy-done.4
  103.5 0.0 copy-start.1
  103.5 1.1 copy-done.1
  104.6 0.0 copy-start
  104.6 0.0 copy-start.2
  104.6 13.0 %attend_rows.1.attended = bf16[224,512]{1,0:T(8,128)(2,1)S(1)} custom-call(s32[8,64]{1,0:T(8,128)S(1)} %copy-done.3, s32[8]{0:T(128)S(1)} %copy-done.4, bf16[672,512]{1,0:T(8,128)(2,1)S(1)} %copy-done.1, bf16[160,2,224,128]{3,2,1,0:T(8,128)(2,1)} %get-tuple-element.7.pool), custom_call_target="tpu_custom_call" | custom-call | tf_op jit(solution)/shard_map/attend_rows/pallas_call | solution.py:872
  117.6 0.0 copy-done
  117.6 0.0 copy-done.2
  117.6 0.0 copy-start.5
  117.6 20.1 %merge_rows.1 = f32[224,512]{1,0:T(8,128)S(1)} custom-call(bf16[224,512]{1,0:T(8,128)(2,1)S(1)} %attend_rows.1.attended, bf16[224,3584]{1,0:T(8,128)(2,1)S(1)} %copy-done, f32[224,512]{1,0:T(8,128)S(1)} %copy-done.2), custom_call_target="tpu_custom_call" | custom-call | tf_op jit(solution)/shard_map/merge_rows/pallas_call | solution.py:779
  137.8 0.0 copy-done.5
  137.8 0.7 reshape.15
  138.5 0.8 copy.24
Async XLA Ops:
  0.6 102.9 %copy-start.3 = (s32[8,64]{1,0:T(8,128)S(1)}, s32[8,64]{1,0:T(8,128)}, u32[]{:S(2)}) copy-start(s32[8,64]{1,0:T(8,128)} %table.1) | copy-start | bytes 6148
  0.6 102.9 %copy-start.4 = (s32[8]{0:T(128)S(1)}, s32[8]{0:T(128)}, u32[]{:S(2)}) copy-start(s32[8]{0:T(128)} %lengths.1) | copy-start | bytes 100
  103.5 1.1 copy-start.1
  104.6 13.0 %copy-start = (bf16[224,3584]{1,0:T(8,128)(2,1)S(1)}, bf16[224,3584]{1,0:T(8,128)(2,1)}, u32[]{:S(2)}) copy-start(bf16[224,3584]{1,0:T(8,128)(2,1)} %weight.1) | copy-start | bytes 4816900
  104.6 13.0 %copy-start.2 = (f32[224,512]{1,0:T(8,128)S(1)}, f32[224,512]{1,0:T(8,128)}, u32[]{:S(2)}) copy-start(f32[224,512]{1,0:T(8,128)} %get-tuple-element.8.before) | copy-start | bytes 1376260
  117.6 20.1 %copy-start.5 = (f32[256,64]{1,0:T(8,128)S(1)}, f32[256,64]{1,0:T(8,128)}, u32[]{:S(2)}) copy-start(f32[256,64]{1,0:T(8,128)} %get-tuple-element.9) | copy-start | bytes 196612
